TPU v7x, 512 devices: a whole 4x8x8 slice. The times are simulated.
512 devices in a mesh: gx: 16 (over x_lo, y), gy: 4 (over x_hi, core), sa: 8 (over z).
Axes of the slice: x: 4 (x_hi: 2, x_lo: 2; x = x_hi * 2 + x_lo), y: 8, z: 8, core: 2. Of those that a mesh axis runs over, the one named last changes fastest.
Arguments:
- trajectory: float32 [2, 32, 36, 256, 512], P(None, 'sa', None, 'gx', 'gy'), may hold values from 0.2 to 2
- adjoint_seed: float32 [32, 36, 256, 512], P('sa', None, 'gx', 'gy'), may hold values from -6 to 6
- wind: float32 [256, 512], P('gx', 'gy'), may hold values from 0.05 to 1
- growth_shape: float32 [32, 36], P('sa'), may hold values from -1 to 1
- group_speeds: float32 [2, 32, 36], P(None, 'sa'), may hold values from 0.05 to 0.45
- upwind_codes: int32 [32, 36], P('sa'), may hold values from 0 to 3
- sea_mask: int32 [256, 512], P('gx', 'gy'), may hold values 0 or 1
- boundary_flags: int32 [256, 512], P('gx', 'gy'), may hold values from 0 to 1, as said below
Outputs:
- state_gradient: float32 [32, 36, 256, 512], P('sa', None, 'gx', 'gy')
- wind_gradient: float32 [256, 512], P('gx', 'gy')
Inputs may be any that keep to these rules, and one draw needn't show every extreme that they name: `upwind_codes`: code % 2 == 1: the upwind neighbour along the first grid dimension is the next cell, else the previous; code // 2 likewise along the second. `sea_mask`: 1 for sea, 0 for land. `boundary_flags`: 1 only on cells of the grid's outermost rows and columns.
All inputs are finite; a program needn't handle non-finite values. No bound on the sum of `sea_mask` on one device may be relied on, other than what follows from the above.
Results may differ from a plain program's by a relative error of at most 0.0001.
Values sent between devices are 32-bit elements; how exact they have to be, the bound alone decides.
No kernel may reach another device: no remote copies, remote signals or barrier semaphores. Data moves between devices by JAX's collectives and lax.ppermute only.
A program may use at most 64 MiB of HBM per device.

v0:
```python
import jax
import jax.numpy as jnp
from jax import lax
from jax.sharding import PartitionSpec as P

FREQS = 32
DIRS = 36
STEPS = 2


steep_scale = 0.05
freq_growth = 1.1


def extended(cells, sides, width):
    for axis, dim in sides:
        count = lax.axis_size(axis)
        ends = count - 1
        head = lax.slice_in_dim(cells, 0, width, axis=dim)
        tail = lax.slice_in_dim(cells, cells.shape[dim] - width, cells.shape[dim], axis=dim)
        cells = jnp.concatenate(
            [
                lax.ppermute(tail, axis, [(i, (i + 1) % count) for i in range(ends)]),
                cells,
                lax.ppermute(head, axis, [((i + 1) % count, i) for i in range(ends)]),
            ],
            axis=dim,
        )
    return cells


def spectral_tables(local_freqs, offset):
    levels = jnp.arange(FREQS).astype(jnp.float32) - FREQS // 2
    frequency = jnp.power(jnp.float32(freq_growth), levels)
    weights = frequency / jnp.sum(frequency) / DIRS
    return (
        lax.dynamic_slice_in_dim(frequency, offset, local_freqs),
        lax.dynamic_slice_in_dim(weights, offset, local_freqs),
    )


def upwind_tables(codes, speeds):
    bit_x = (codes % 2)[:, :, None, None] == 1
    bit_y = (codes // 2)[:, :, None, None] == 1
    return (bit_x, bit_y, speeds[0][:, :, None, None], speeds[1][:, :, None, None])


def propagate(padded, density, tables, sea, held):
    bit_x, bit_y, speed_x, speed_y = tables
    inflow_x = jnp.where(bit_x, padded[:, :, 2:, 1:-1], padded[:, :, :-2, 1:-1])
    inflow_y = jnp.where(bit_y, padded[:, :, 1:-1, 2:], padded[:, :, 1:-1, :-2])
    moved = density - speed_x * (density - inflow_x) - speed_y * (density - inflow_y)
    return sea * ((1.0 - held) * moved + held * density)


def moments(moved, weights, frequency):
    energy_part = jnp.sum(moved * weights[:, None, None, None], axis=(0, 1))
    first_part = jnp.sum(moved * (weights * frequency)[:, None, None, None], axis=(0, 1))
    return (energy_part, first_part)


def source(moved, energy, first_moment, wind, growth, frequency):
    mean_freq = first_moment / energy
    steep = steep_scale * energy * mean_freq**4
    damping = (steep / (1.0 + steep)) ** 2
    rate = (
        0.5 * wind * growth[:, :, None, None]
        - 0.5 * damping * frequency[:, None, None, None] / mean_freq
    )
    return moved * jnp.exp(rate)


def adjoint_step(cotangent, forward, wind, growth, frequency, weights, tables, sea, held):
    moved, energy, first_moment = forward

    def local_source(moved_in, energy_in, first_in, wind_in):
        return source(moved_in, energy_in, first_in, wind_in, growth, frequency)

    _, pullback = jax.vjp(local_source, moved, energy, first_moment, wind)
    lam_moved, lam_energy, lam_first, lam_wind = pullback(cotangent)
    lam_energy, lam_first, lam_wind = lax.psum((lam_energy, lam_first, lam_wind), "sa")
    lam_moved = (
        lam_moved
        + weights[:, None, None, None] * lam_energy
        + (weights * frequency)[:, None, None, None] * lam_first
    )
    lam_flow = sea * (1.0 - held) * lam_moved
    padded = extended(lam_flow, (("gx", 2), ("gy", 3)), 1)
    bit_x, bit_y, speed_x, speed_y = tables
    back_x = jnp.where(bit_x, padded[:, :, :-2, 1:-1], padded[:, :, 2:, 1:-1])
    back_y = jnp.where(bit_y, padded[:, :, 1:-1, :-2], padded[:, :, 1:-1, 2:])
    lam_density = (
        sea * held * lam_moved
        + (1.0 - speed_x - speed_y) * lam_flow
        + speed_x * back_x
        + speed_y * back_y
    )
    return (lam_density, lam_wind)


def shards(
    trajectory,
    adjoint_seed,
    wind,
    growth_shape,
    group_speeds,
    upwind_codes,
    sea_mask,
    boundary_flags,
):
    local_freqs = adjoint_seed.shape[0]
    offset = lax.axis_index("sa") * local_freqs
    frequency, weights = spectral_tables(local_freqs, offset)
    tables = upwind_tables(upwind_codes, group_speeds)
    sea = sea_mask.astype(jnp.float32)
    held = boundary_flags.astype(jnp.float32)
    forward_list = []
    for position in range(STEPS):
        padded = extended(trajectory[position], (("gx", 2), ("gy", 3)), 1)
        moved = propagate(padded, trajectory[position], tables, sea, held)
        energy_part, first_part = moments(moved, weights, frequency)
        energy_sum, first_sum = lax.psum((energy_part, first_part), "sa")
        forward_list.append((moved, 1.0 + energy_sum, 1.0 + first_sum))
    cotangent = adjoint_seed
    wind_total = jnp.zeros_like(wind)
    for position in reversed(range(STEPS)):
        cotangent, wind_part = adjoint_step(
            cotangent,
            forward_list[position],
            wind,
            growth_shape,
            frequency,
            weights,
            tables,
            sea,
            held,
        )
        wind_total = wind_total + wind_part
    return (cotangent, wind_total)


def solution(mesh):
    return jax.shard_map(
        shards,
        mesh=mesh,
        in_specs=(
            P(None, "sa", None, "gx", "gy"),
            P("sa", None, "gx", "gy"),
            P("gx", "gy"),
            P("sa", None),
            P(None, "sa", None),
            P("sa", None),
            P("gx", "gy"),
            P("gx", "gy"),
        ),
        out_specs=(P("sa", None, "gx", "gy"), P("gx", "gy")),
        check_vma=False,
    )
```

profile of v0, /device:TPU:57, one launch (start us, length us, event | category | flops | bytes accessed | tf_op | source)
XLA Modules:
  0.0 219.8 jit_solution(10740809346740063617)
XLA Ops:
  0.6 1.8 fusion.74
  2.4 0.4 copy.47
  2.8 3.0 %collective-permute-start = (f32[4,36,1,128]{3,1,2,0:T(8,128)S(1)}, f32[4,36,1,128]{3,1,2,0:T(8,128)S(1)}, u32[]{:S(2)}, u32[]{:S(2)}) collective-permute-start(f32[4,36,1,128]{3,1,2,0:T(8,128)S(1)} %get-tuple-element.48), channel_id=1, source_target_pairs={{32,0},{64,32},{96,64},{128,96},{160,128},{192,160},{224,192},{256... | collective-permute-start | bytes 221192 | tf_op jit(solution)/shard_map/ppermute | solution.py:25
  5.8 4.4 %collective-permute-start.1 = (f32[4,36,1,128]{3,1,2,0:T(8,128)S(1)}, f32[4,36,1,128]{3,1,2,0:T(8,128)S(1)}, u32[]{:S(2)}, u32[]{:S(2)}) collective-permute-start(f32[4,36,1,128]{3,1,2,0:T(8,128)S(1)} %get-tuple-element.47), channel_id=1, source_target_pairs={{0,32},{32,64},{64,96},{96,128},{128,160},{160,192},{192,224},{224... | collective-permute-start | bytes 221192 | tf_op jit(solution)/shard_map/ppermute | solution.py:23
  10.3 0.4 copy.46
  10.7 1.9 collective-permute-start.8
  12.6 5.5 %collective-permute-start.9 = (f32[4,36,1,128]{3,1,2,0:T(8,128)S(1)}, f32[4,36,1,128]{3,1,2,0:T(8,128)S(1)}, u32[]{:S(2)}, u32[]{:S(2)}) collective-permute-start(f32[4,36,1,128]{3,1,2,0:T(8,128)S(1)} %get-tuple-element.49), channel_id=1, source_target_pairs={{0,32},{32,64},{64,96},{96,128},{128,160},{160,192},{192,224},{224... | collective-permute-start | bytes 221192 | tf_op jit(solution)/shard_map/ppermute | solution.py:23
  18.1 0.6 fusion.69
  18.8 0.7 divide_multiply_fusion
  19.5 0.1 pad_maximum_fusion
  19.6 2.1 fusion.77
  21.7 2.1 copy.11
  23.8 3.7 %collective-permute-start.2 = (f32[4,36,18,1]{1,2,3,0:T(8,128)S(1)}, f32[4,36,18,1]{1,2,3,0:T(8,128)S(1)}, u32[]{:S(2)}, u32[]{:S(2)}) collective-permute-start(f32[4,36,18,1]{1,2,3,0:T(8,128)S(1)} %copy.11), channel_id=1, source_target_pairs={{8,0},{16,8},{24,16},{9,1},{17,9},{25,17},{10,2},{18,10},{26,18},{... | collective-permute-start | bytes 31112 | tf_op jit(solution)/shard_map/ppermute | solution.py:25
  27.5 2.1 copy.13
  29.6 4.6 %collective-permute-start.3 = (f32[4,36,18,1]{1,2,3,0:T(8,128)S(1)}, f32[4,36,18,1]{1,2,3,0:T(8,128)S(1)}, u32[]{:S(2)}, u32[]{:S(2)}) collective-permute-start(f32[4,36,18,1]{1,2,3,0:T(8,128)S(1)} %copy.13), channel_id=1, source_target_pairs={{0,8},{8,16},{16,24},{1,9},{9,17},{17,25},{2,10},{10,18},{18,26},{... | collective-permute-start | bytes 31112 | tf_op jit(solution)/shard_map/ppermute | solution.py:23
  34.2 0.1 pad_maximum_fusion.2
  34.3 2.1 fusion.78
  36.4 2.1 copy.22
  38.5 1.9 collective-permute-start.10
  40.4 2.1 copy.24
  42.6 5.2 %collective-permute-start.11 = (f32[4,36,18,1]{1,2,3,0:T(8,128)S(1)}, f32[4,36,18,1]{1,2,3,0:T(8,128)S(1)}, u32[]{:S(2)}, u32[]{:S(2)}) collective-permute-start(f32[4,36,18,1]{1,2,3,0:T(8,128)S(1)} %copy.24), channel_id=1, source_target_pairs={{0,8},{8,16},{16,24},{1,9},{9,17},{17,25},{2,10},{10,18},{18,26},{... | collective-permute-start | bytes 31112 | tf_op jit(solution)/shard_map/ppermute | solution.py:23
  47.7 0.1 fusion.73
  47.8 1.8 copy.12
  49.6 1.8 copy.14
  51.4 1.7 copy.23
  53.1 1.8 copy.25
  54.9 6.1 %multiply_reduce_fusion.4 = (f32[16,128]{1,0:T(8,128)S(1)}, f32[16,128]{1,0:T(8,128)S(1)}, f32[16,128]{1,0:T(8,128)S(1)}, f32[16,128]{1,0:T(8,128)S(1)}, f32[4,3...) fusion(f32[4]{0:T(128)S(1)} %get-tuple-element.30, f32[4]{0:T(128)S(1)} %get-tuple-element.32, ...), kind=kLoop, calls=%fused_computation.88 | loop fusion | flops 14147584 | bytes 5113792 | tf_op jit(solution)/shard_map/reduce_sum | solution.py:58
  61.0 28.9 %all-reduce.2 = (f32[16,128]{1,0:T(8,128)S(1)}, f32[16,128]{1,0:T(8,128)S(1)}) all-reduce(f32[16,128]{1,0:T(8,128)S(1)} %get-tuple-element.11, f32[16,128]{1,0:T(8,128)S(1)} %get-tuple-element.10), channel_id=1, replica_groups=mesh['gx'=16,'gy'=4,'sa'=8] {'sa'}, use_global_device_ids=true, to_apply=%region_2.3 | all-reduce | flops 4096 | bytes 32768 | tf_op jit(solution)/shard_map/psum | solution.py:122
  89.9 0.1 multiply_divide_fusion.1
  89.9 2.6 %multiply_reduce_fusion.1 = (f32[16,128]{1,0:T(8,128)S(1)}, f32[4,16,128]{2,1,0:T(8,128)S(1)}) fusion(f32[4,36]{1,0:T(4,128)S(1)} %copy-done.1, f32[4,16,128]{2,1,0:T(8,128)S(1)} %multiply_divide_fusion.1, f32[16,128]{1,0:T(8,128)S(1)} %broadcast_multiply_fusion.4, f32[4,36,16,128]{3,1,2,0:T(8,128)} %get-tuple-element.29, f32[4,36,16,128]{3,2,1,0:T(8,128)} %param.9), kind=kLoop, calls=%fused_computation.85 | loop fusion | flops 2054144 | bytes 2441792 | tf_op jit(solution)/shard_map/transpose(jvp())/reduce_sum | solution.py:67
  92.5 0.1 multiply_reduce_fusion.7
  92.6 20.3 %all-reduce.1 = (f32[16,128]{1,0:T(8,128)S(1)}, f32[16,128]{1,0:T(8,128)S(1)}, f32[16,128]{1,0:T(8,128)S(1)}, f32[16,128]{1,0:T(8,128)S(1)}) all-reduce(f32[16,128]{1,0:T(8,128)S(1)} %get-tuple-element.54, f32[16,128]{1,0:T(8,128)S(1)} %get-tuple-element.53, ...), channel_id=1, replica_groups=mesh['gx'=16,'gy'=4,'sa'=8] {'sa'}, use_global_device_ids=true, to_apply=%region_9.10 | all-reduce | flops 8192 | bytes 65536 | tf_op jit(solution)/shard_map/psum | solution.py:81
  113.1 0.7 fusion.45
  113.8 1.9 collective-permute-start.4
  115.7 3.4 %collective-permute-start.5 = (f32[4,36,1,128]{3,1,2,0:T(8,128)S(1)}, f32[4,36,1,128]{3,1,2,0:T(8,128)S(1)}, u32[]{:S(2)}, u32[]{:S(2)}) collective-permute-start(f32[4,36,1,128]{3,1,2,0:T(8,128)S(1)} %get-tuple-element.46), channel_id=1, source_target_pairs={{32,0},{64,32},{96,64},{128,96},{160,128},{192,160},{224,192},{256... | collective-permute-start | bytes 221192 | tf_op jit(solution)/shard_map/ppermute | solution.py:25
  119.2 3.9 %collective-permute-done.5 = f32[4,36,1,128]{3,1,2,0:T(8,128)S(1)} collective-permute-done((f32[4,36,1,128]{3,1,2,0:T(8,128)S(1)}, f32[4,36,1,128]{3,1,2,0:T(8,128)S(1)}, u32[]{:S(2)}, u32[]{:S(2)}) %collective-permute-start.5) | collective-permute-done | bytes 73760 | tf_op jit(solution)/shard_map/ppermute | solution.py:25
  123.0 0.1 pad_maximum_fusion.1
  123.1 2.1 fusion.76
  125.2 2.1 copy.17
  127.4 17.0 %collective-permute-start.6 = (f32[4,36,18,1]{1,2,3,0:T(8,128)S(1)}, f32[4,36,18,1]{1,2,3,0:T(8,128)S(1)}, u32[]{:S(2)}, u32[]{:S(2)}) collective-permute-start(f32[4,36,18,1]{1,2,3,0:T(8,128)S(1)} %copy.17), channel_id=1, source_target_pairs={{0,8},{8,16},{16,24},{1,9},{9,17},{17,25},{2,10},{10,18},{18,26},{... | collective-permute-start | bytes 31112 | tf_op jit(solution)/shard_map/ppermute | solution.py:23
  144.3 2.1 copy.19
  146.5 2.1 collective-permute-start.7
  148.6 1.7 copy.18
  150.4 3.0 %collective-permute-done.7 = f32[4,36,18,1]{1,2,3,0:T(8,128)S(1)} collective-permute-done((f32[4,36,18,1]{1,2,3,0:T(8,128)S(1)}, f32[4,36,18,1]{1,2,3,0:T(8,128)S(1)}, u32[]{:S(2)}, u32[]{:S(2)}) %collective-permute-start.7) | collective-permute-done | bytes 10400 | tf_op jit(solution)/shard_map/ppermute | solution.py:25
  153.4 1.8 copy.20
  155.1 3.9 %multiply_reduce_fusion = (f32[16,128]{1,0:T(8,128)S(1)}, f32[4,16,128]{2,1,0:T(8,128)S(1)}, f32[4,36,16,128]{3,1,2,0:T(8,128)S(1)}) fusion(f32[4,36]{1,0:T(4,128)S(1)} %copy-done.1, f32[4,16,128]{2,1,0:T(8,128)S(1)} %multiply_divide_fusion, f32[16,128]{1,0:T(8,128)S(1)} %broadcast_multiply_fusion.4, f32[4,36,16,128]{3,1,2,0:T(8,128)} %get-tuple-element.28, ...), kind=kLoop, calls=%fused_computation.84 | loop fusion | flops 8247296 | bytes 5077792 | tf_op jit(solution)/shard_map/transpose(jvp())/reduce_sum | solution.py:67
  159.0 0.1 multiply_reduce_fusion.6
  159.2 20.8 %all-reduce = (f32[16,128]{1,0:T(8,128)S(1)}, f32[16,128]{1,0:T(8,128)S(1)}, f32[16,128]{1,0:T(8,128)}) all-reduce(f32[16,128]{1,0:T(8,128)S(1)} %get-tuple-element.52, f32[16,128]{1,0:T(8,128)S(1)} %get-tuple-element.51, f32[16,128]{1,0:T(8,128)S(1)} %add_multiply_fusion.2), channel_id=1, replica_groups=mesh['gx'=16,'gy'=4,'sa'=8] {'sa'}, use_global_device_ids=true, to_apply=%region_18.19 | all-reduce | flops 6144 | bytes 49152 | tf_op jit(solution)/shard_map/psum | solution.py:81
  180.0 0.1 broadcast_multiply_fusion
  180.1 0.4 fusion.44
  180.5 1.9 collective-permute-start.12
  182.5 3.4 %collective-permute-start.13 = (f32[4,36,1,128]{3,1,2,0:T(8,128)S(1)}, f32[4,36,1,128]{3,1,2,0:T(8,128)S(1)}, u32[]{:S(2)}, u32[]{:S(2)}) collective-permute-start(f32[4,36,1,128]{3,1,2,0:T(8,128)S(1)} %get-tuple-element.44), channel_id=1, source_target_pairs={{32,0},{64,32},{96,64},{128,96},{160,128},{192,160},{224,192},{256... | collective-permute-start | bytes 221192 | tf_op jit(solution)/shard_map/ppermute | solution.py:25
  185.8 3.9 %collective-permute-done.13 = f32[4,36,1,128]{3,1,2,0:T(8,128)S(1)} collective-permute-done((f32[4,36,1,128]{3,1,2,0:T(8,128)S(1)}, f32[4,36,1,128]{3,1,2,0:T(8,128)S(1)}, u32[]{:S(2)}, u32[]{:S(2)}) %collective-permute-start.13) | collective-permute-done | bytes 73760 | tf_op jit(solution)/shard_map/ppermute | solution.py:25
  189.7 0.1 pad_maximum_fusion.3
  189.8 2.1 fusion.75
  191.9 2.1 copy.26
  194.1 10.6 %collective-permute-start.14 = (f32[4,36,18,1]{1,2,3,0:T(8,128)S(1)}, f32[4,36,18,1]{1,2,3,0:T(8,128)S(1)}, u32[]{:S(2)}, u32[]{:S(2)}) collective-permute-start(f32[4,36,18,1]{1,2,3,0:T(8,128)S(1)} %copy.26), channel_id=1, source_target_pairs={{0,8},{8,16},{16,24},{1,9},{9,17},{17,25},{2,10},{10,18},{18,26},{... | collective-permute-start | bytes 31112 | tf_op jit(solution)/shard_map/ppermute | solution.py:23
  204.6 2.1 copy.28
  206.7 1.9 collective-permute-start.15
  208.7 1.7 copy.27
  210.4 3.2 %collective-permute-done.15 = f32[4,36,18,1]{1,2,3,0:T(8,128)S(1)} collective-permute-done((f32[4,36,18,1]{1,2,3,0:T(8,128)S(1)}, f32[4,36,18,1]{1,2,3,0:T(8,128)S(1)}, u32[]{:S(2)}, u32[]{:S(2)}) %collective-permute-start.15) | collective-permute-done | bytes 10400 | tf_op jit(solution)/shard_map/ppermute | solution.py:25
  213.7 1.8 copy.29
  215.4 3.1 %fusion.12 = f32[4,36,16,128]{3,1,2,0:T(8,128)S(1)} fusion(f32[4,36,18,1]{3,1,2,0:T(8,128)} %copy.29, f32[4,36,1,128]{3,1,2,0:T(8,128)S(1)} %collective-permute-done.13, f32[4,36,16,128]{3,1,2,0:T(8,128)S(1)} %fusion.44, f32[4,36,1,128]{3,1,2,0:T(8,128)S(1)} %collective-permute-done.12, f32[4,36,18,1]{3,1,2,0:T(8,128)} %copy.27, ...), kind=kLoop, calls=%fused_computation.19 | loop fusion | flops 6488064 | bytes 3824416 | tf_op jit(solution)/shard_map/add | solution.py:93
  218.6 1.2 copy.30
  (46 shorter events, 0.5 us)
Async XLA Ops:
  2.8 16.7 %collective-permute-start = (f32[4,36,1,128]{3,1,2,0:T(8,128)S(1)}, f32[4,36,1,128]{3,1,2,0:T(8,128)S(1)}, u32[]{:S(2)}, u32[]{:S(2)}) collective-permute-start(f32[4,36,1,128]{3,1,2,0:T(8,128)S(1)} %get-tuple-element.48), channel_id=1, source_target_pairs={{32,0},{64,32},{96,64},{128,96},{160,128},{192,160},{224,192},{256... | collective-permute-start | bytes 221192 | tf_op jit(solution)/shard_map/ppermute | solution.py:25
  5.8 13.7 %collective-permute-start.1 = (f32[4,36,1,128]{3,1,2,0:T(8,128)S(1)}, f32[4,36,1,128]{3,1,2,0:T(8,128)S(1)}, u32[]{:S(2)}, u32[]{:S(2)}) collective-permute-start(f32[4,36,1,128]{3,1,2,0:T(8,128)S(1)} %get-tuple-element.47), channel_id=1, source_target_pairs={{0,32},{32,64},{64,96},{96,128},{128,160},{160,192},{192,224},{224... | collective-permute-start | bytes 221192 | tf_op jit(solution)/shard_map/ppermute | solution.py:23
  10.2 8.5 %copy-start.4 = (f32[2,4,36]{2,1,0:T(4,128)S(1)}, f32[2,4,36]{2,1,0:T(4,128)}, u32[]{:S(2)}) copy-start(f32[2,4,36]{2,1,0:T(4,128)} %param.12) | copy-start | bytes 3460
  10.2 8.5 %copy-start.6 = (s32[4,36]{1,0:T(4,128)S(1)}, s32[4,36]{1,0:T(4,128)}, u32[]{:S(2)}) copy-start(s32[4,36]{1,0:T(4,128)} %param.13) | copy-start | bytes 1732
  10.2 8.5 %copy-start.5 = (f32[16,128]{1,0:T(8,128)S(1)}, f32[16,128]{1,0:T(8,128)}, u32[]{:S(2)}) copy-start(f32[16,128]{1,0:T(8,128)} %param.10) | copy-start | bytes 24580
  10.3 8.5 %copy-start.2 = (s32[16,128]{1,0:T(8,128)S(1)}, s32[16,128]{1,0:T(8,128)}, u32[]{:S(2)}) copy-start(s32[16,128]{1,0:T(8,128)} %param.14) | copy-start | bytes 24580
  10.3 8.5 %copy-start.3 = (s32[16,128]{1,0:T(8,128)S(1)}, s32[16,128]{1,0:T(8,128)}, u32[]{:S(2)}) copy-start(s32[16,128]{1,0:T(8,128)} %param.15) | copy-start | bytes 24580
  10.7 23.5 %collective-permute-start.8 = (f32[4,36,1,128]{3,1,2,0:T(8,128)S(1)}, f32[4,36,1,128]{3,1,2,0:T(8,128)S(1)}, u32[]{:S(2)}, u32[]{:S(2)}) collective-permute-start(f32[4,36,1,128]{3,1,2,0:T(8,128)S(1)} %get-tuple-element.50), channel_id=1, source_target_pairs={{32,0},{64,32},{96,64},{128,96},{160,128},{192,160},{224,192},{256... | collective-permute-start | bytes 221192 | tf_op jit(solution)/shard_map/ppermute | solution.py:25
  12.6 21.6 %collective-permute-start.9 = (f32[4,36,1,128]{3,1,2,0:T(8,128)S(1)}, f32[4,36,1,128]{3,1,2,0:T(8,128)S(1)}, u32[]{:S(2)}, u32[]{:S(2)}) collective-permute-start(f32[4,36,1,128]{3,1,2,0:T(8,128)S(1)} %get-tuple-element.49), channel_id=1, source_target_pairs={{0,32},{32,64},{64,96},{96,128},{128,160},{160,192},{192,224},{224... | collective-permute-start | bytes 221192 | tf_op jit(solution)/shard_map/ppermute | solution.py:23
  23.8 24.0 %collective-permute-start.2 = (f32[4,36,18,1]{1,2,3,0:T(8,128)S(1)}, f32[4,36,18,1]{1,2,3,0:T(8,128)S(1)}, u32[]{:S(2)}, u32[]{:S(2)}) collective-permute-start(f32[4,36,18,1]{1,2,3,0:T(8,128)S(1)} %copy.11), channel_id=1, source_target_pairs={{8,0},{16,8},{24,16},{9,1},{17,9},{25,17},{10,2},{18,10},{26,18},{... | collective-permute-start | bytes 31112 | tf_op jit(solution)/shard_map/ppermute | solution.py:25
  29.6 20.0 %collective-permute-start.3 = (f32[4,36,18,1]{1,2,3,0:T(8,128)S(1)}, f32[4,36,18,1]{1,2,3,0:T(8,128)S(1)}, u32[]{:S(2)}, u32[]{:S(2)}) collective-permute-start(f32[4,36,18,1]{1,2,3,0:T(8,128)S(1)} %copy.13), channel_id=1, source_target_pairs={{0,8},{8,16},{16,24},{1,9},{9,17},{17,25},{2,10},{10,18},{18,26},{... | collective-permute-start | bytes 31112 | tf_op jit(solution)/shard_map/ppermute | solution.py:23
  38.5 12.9 %collective-permute-start.10 = (f32[4,36,18,1]{1,2,3,0:T(8,128)S(1)}, f32[4,36,18,1]{1,2,3,0:T(8,128)S(1)}, u32[]{:S(2)}, u32[]{:S(2)}) collective-permute-start(f32[4,36,18,1]{1,2,3,0:T(8,128)S(1)} %copy.22), channel_id=1, source_target_pairs={{8,0},{16,8},{24,16},{9,1},{17,9},{25,17},{10,2},{18,10},{26,18},{... | collective-permute-start | bytes 31112 | tf_op jit(solution)/shard_map/ppermute | solution.py:25
  42.6 10.5 %collective-permute-start.11 = (f32[4,36,18,1]{1,2,3,0:T(8,128)S(1)}, f32[4,36,18,1]{1,2,3,0:T(8,128)S(1)}, u32[]{:S(2)}, u32[]{:S(2)}) collective-permute-start(f32[4,36,18,1]{1,2,3,0:T(8,128)S(1)} %copy.24), channel_id=1, source_target_pairs={{0,8},{8,16},{16,24},{1,9},{9,17},{17,25},{2,10},{10,18},{18,26},{... | collective-permute-start | bytes 31112 | tf_op jit(solution)/shard_map/ppermute | solution.py:23
  54.9 35.1 %copy-start.1 = (f32[4,36]{1,0:T(4,128)S(1)}, f32[4,36]{1,0:T(4,128)}, u32[]{:S(2)}) copy-start(f32[4,36]{1,0:T(4,128)} %param.11) | copy-start | bytes 1732
  89.9 23.2 %copy-start = (f32[4,36,16,128]{3,2,1,0:T(8,128)S(1)}, f32[4,36,16,128]{3,2,1,0:T(8,128)}, u32[]{:S(2)}) copy-start(f32[4,36,16,128]{3,2,1,0:T(8,128)} %param.9) | copy-start | bytes 3538948
  113.8 5.3 %collective-permute-start.4 = (f32[4,36,1,128]{3,1,2,0:T(8,128)S(1)}, f32[4,36,1,128]{3,1,2,0:T(8,128)S(1)}, u32[]{:S(2)}, u32[]{:S(2)}) collective-permute-start(f32[4,36,1,128]{3,1,2,0:T(8,128)S(1)} %get-tuple-element.45), channel_id=1, source_target_pairs={{0,32},{32,64},{64,96},{96,128},{128,160},{160,192},{192,224},{224... | collective-permute-start | bytes 221192 | tf_op jit(solution)/shard_map/ppermute | solution.py:23
  115.7 7.3 %collective-permute-start.5 = (f32[4,36,1,128]{3,1,2,0:T(8,128)S(1)}, f32[4,36,1,128]{3,1,2,0:T(8,128)S(1)}, u32[]{:S(2)}, u32[]{:S(2)}) collective-permute-start(f32[4,36,1,128]{3,1,2,0:T(8,128)S(1)} %get-tuple-element.46), channel_id=1, source_target_pairs={{32,0},{64,32},{96,64},{128,96},{160,128},{192,160},{224,192},{256... | collective-permute-start | bytes 221192 | tf_op jit(solution)/shard_map/ppermute | solution.py:25
  127.4 21.3 %collective-permute-start.6 = (f32[4,36,18,1]{1,2,3,0:T(8,128)S(1)}, f32[4,36,18,1]{1,2,3,0:T(8,128)S(1)}, u32[]{:S(2)}, u32[]{:S(2)}) collective-permute-start(f32[4,36,18,1]{1,2,3,0:T(8,128)S(1)} %copy.17), channel_id=1, source_target_pairs={{0,8},{8,16},{16,24},{1,9},{9,17},{17,25},{2,10},{10,18},{18,26},{... | collective-permute-start | bytes 31112 | tf_op jit(solution)/shard_map/ppermute | solution.py:23
  146.5 6.9 %collective-permute-start.7 = (f32[4,36,18,1]{1,2,3,0:T(8,128)S(1)}, f32[4,36,18,1]{1,2,3,0:T(8,128)S(1)}, u32[]{:S(2)}, u32[]{:S(2)}) collective-permute-start(f32[4,36,18,1]{1,2,3,0:T(8,128)S(1)} %copy.19), channel_id=1, source_target_pairs={{8,0},{16,8},{24,16},{9,1},{17,9},{25,17},{10,2},{18,10},{26,18},{... | collective-permute-start | bytes 31112 | tf_op jit(solution)/shard_map/ppermute | solution.py:25
  180.5 5.3 %collective-permute-start.12 = (f32[4,36,1,128]{3,1,2,0:T(8,128)S(1)}, f32[4,36,1,128]{3,1,2,0:T(8,128)S(1)}, u32[]{:S(2)}, u32[]{:S(2)}) collective-permute-start(f32[4,36,1,128]{3,1,2,0:T(8,128)S(1)} %get-tuple-element.43), channel_id=1, source_target_pairs={{0,32},{32,64},{64,96},{96,128},{128,160},{160,192},{192,224},{224... | collective-permute-start | bytes 221192 | tf_op jit(solution)/shard_map/ppermute | solution.py:23
  182.5 7.3 %collective-permute-start.13 = (f32[4,36,1,128]{3,1,2,0:T(8,128)S(1)}, f32[4,36,1,128]{3,1,2,0:T(8,128)S(1)}, u32[]{:S(2)}, u32[]{:S(2)}) collective-permute-start(f32[4,36,1,128]{3,1,2,0:T(8,128)S(1)} %get-tuple-element.44), channel_id=1, source_target_pairs={{32,0},{64,32},{96,64},{128,96},{160,128},{192,160},{224,192},{256... | collective-permute-start | bytes 221192 | tf_op jit(solution)/shard_map/ppermute | solution.py:25
  194.1 14.6 %collective-permute-start.14 = (f32[4,36,18,1]{1,2,3,0:T(8,128)S(1)}, f32[4,36,18,1]{1,2,3,0:T(8,128)S(1)}, u32[]{:S(2)}, u32[]{:S(2)}) collective-permute-start(f32[4,36,18,1]{1,2,3,0:T(8,128)S(1)} %copy.26), channel_id=1, source_target_pairs={{0,8},{8,16},{16,24},{1,9},{9,17},{17,25},{2,10},{10,18},{18,26},{... | collective-permute-start | bytes 31112 | tf_op jit(solution)/shard_map/ppermute | solution.py:23
  206.7 6.9 %collective-permute-start.15 = (f32[4,36,18,1]{1,2,3,0:T(8,128)S(1)}, f32[4,36,18,1]{1,2,3,0:T(8,128)S(1)}, u32[]{:S(2)}, u32[]{:S(2)}) collective-permute-start(f32[4,36,18,1]{1,2,3,0:T(8,128)S(1)} %copy.28), channel_id=1, source_target_pairs={{8,0},{16,8},{24,16},{9,1},{17,9},{25,17},{10,2},{18,10},{26,18},{... | collective-permute-start | bytes 31112 | tf_op jit(solution)/shard_map/ppermute | solution.py:25
where the time goes:
time: 221 us; the launch traced here: 220 us
  starting transfers between devices  72.3 us (33%)
  blocking collectives  70 us (32%)
  local copies, waits for them, and re-layouts  43.2 us (20%)
  other arithmetic  19.2 us (9%)
  waiting for transfers between devices  14.1 us (6%)
    ppermute x8, starting transfers between devices, extended(): lax.ppermute(tail, axis, [(i, (i + 1) % count) for i in range(ends)])  51 us
    psum x2, blocking collectives, adjoint_step(): lax.psum((lam_energy, lam_first, lam_wind), 'sa')  41.2 us
    psum x1, blocking collectives, shards(): energy_sum, first_sum = lax.psum((energy_part, first_part), 'sa')  28.9 us
    ppermute x8, starting transfers between devices, extended(): lax.ppermute(head, axis, [((i + 1) % count, i) for i in range(ends)])  21.3 us
    ppermute x8, waiting for transfers between devices, extended(): lax.ppermute(head, axis, [((i + 1) % count, i) for i in range(ends)])  14 us
    slice x10, local copies, waits for them, and re-layouts, extended(): lax.slice_in_dim(cells, cells.shape[dim] - width, cells.shape[dim], axis=...  12.7 us
    slice x6, local copies, waits for them, and re-layouts, extended(): head = lax.slice_in_dim(cells, 0, width, axis=dim)  12.6 us
    ppermute x4, local copies, waits for them, and re-layouts, extended(): lax.ppermute(head, axis, [((i + 1) % count, i) for i in range(ends)])  7.05 us
  transfers between devices with their start and end apart: 16, of which 4 were waited for; matrix products, arithmetic and copies ran while one was open for 13% of the time, Pallas kernels for 0%

commit v1 on v0

v1 whole, which is shorter than its diff:
```python
import functools

import jax
import jax.numpy as jnp
import numpy as np
from jax import lax
from jax.experimental import pallas as pl
from jax.experimental.pallas import tpu as pltpu
from jax.sharding import PartitionSpec as P

FREQS = 32
DIRS = 36
TILE = 8
PACK = 4
F32 = jnp.float32

steep_scale = 0.05
freq_growth = 1.1

frequency_table = np.power(np.float32(freq_growth), np.arange(FREQS, dtype=np.float32) - FREQS // 2)
frequency_table = frequency_table.astype(np.float32)
weight_table = (frequency_table / np.sum(frequency_table) / np.float32(DIRS)).astype(np.float32)

VMEM = pl.BlockSpec(memory_space=pltpu.VMEM)
SMEM = pl.BlockSpec(memory_space=pltpu.SMEM)
HBM = pl.BlockSpec(memory_space=pltpu.HBM)

STAY, FROM_PREV_X, FROM_NEXT_X, FROM_PREV_Y, FROM_NEXT_Y, GROWTH = range(6)


def bin_constants(table, f, local):
    i = lax.axis_index("sa") * local + f
    return table[0, i], table[1, i]


def is_even(axis):
    return lax.rem(lax.axis_index(axis), 2) == 0


def span(t):
    return slice(t * TILE, (t + 1) * TILE)


def lanes_of(shape):
    return lax.broadcasted_iota(jnp.int32, shape, len(shape) - 1)


def tile_frequency(t):
    f = t * TILE // DIRS
    return f, (t * TILE + TILE - 1) // DIRS != f


def low_half():
    return lax.broadcasted_iota(jnp.int32, (TILE, 128), 0) < TILE // 2


def pick(values, t):
    f, mixed = tile_frequency(t)
    return jnp.where(low_half(), values[f], values[f + 1]) if mixed else values[f]


def accumulate(sums, t, value):
    f, mixed = tile_frequency(t)
    if mixed:
        low = low_half()
        sums[f] = sums[f] + jnp.where(low, value, 0.0)
        sums[f + 1] = sums[f + 1] + jnp.where(low, 0.0, value)
    else:
        sums[f] = sums[f] + value


def over_rows(count, body):
    body(0, True, False)

    def inner(r, carry):
        body(r, False, False)
        return carry

    lax.fori_loop(1, count - 1, inner, 0)
    body(count - 1, False, True)


def column_lane(r, t):
    return (t % PACK) * 32 + 2 * r


def pack_columns(packed, value, r, t):
    at = column_lane(r, t)
    lane = lanes_of(value.shape)
    here = (lane == at) | (lane == lax.rem(at + 127, 128))
    g = t // PACK
    packed[g] = jnp.where(here, pltpu.roll(value, at, 1), packed[g])


def join_columns(near, far, out):
    even = is_even("gy")
    for g in range(out.shape[0]):
        before = jnp.where(even, far[g], near[g])
        after = jnp.where(even, near[g], far[g])
        lane = lanes_of(before.shape)
        out[g] = jnp.where(lane % 2 == 0, pltpu.roll(before, 1, 1), pltpu.roll(after, 127, 1))


def along_lanes(value, columns, r, t):
    lane = lanes_of(value.shape)
    at = column_lane(r, t)
    edge = pltpu.roll(columns[t // PACK], lax.rem(128 - at, 128), 1)
    before = jnp.where(lane == 0, edge, pltpu.roll(value, 1, 1))
    after = jnp.where(lane == 127, edge, pltpu.roll(value, 127, 1))
    return before, after


def put_rows(near_rows, far_rows, t, value, first, last):
    even = is_even("gx")
    if first:
        far_rows[span(t), :] = jnp.where(even, value, far_rows[span(t), :])
        near_rows[span(t), :] = value
    if last:
        near_rows[span(t), :] = jnp.where(even, value, near_rows[span(t), :])
        far_rows[span(t), :] = jnp.where(even, far_rows[span(t), :], value)


def row_halo(near_rows, far_rows, t, upper):
    even = is_even("gx")
    near, far = near_rows[span(t), :], far_rows[span(t), :]
    return jnp.where(even, far, near) if upper else jnp.where(even, near, far)


def set_masks(sea, held, masks):
    sea, held = sea[...].astype(F32), held[...].astype(F32)
    masks[0] = sea * (1.0 - held)
    masks[1] = sea * held


def row_of(ref, r):
    return ref[pl.ds(r, 1), :]


def gathered(sums, q):
    rows = sums.shape[1] // TILE
    total = sums[q, pl.ds(0, rows, TILE), :]
    for k in range(1, TILE):
        total = total + sums[q, pl.ds(k, rows, TILE), :]
    return total


def edges_kernel(state, laid, near_rows, far_rows, cols, arrived):
    steps, rows, bins, lanes = laid.shape
    copies = [
        [pltpu.make_async_copy(state.at[s, :, r, :], laid.at[s, r], arrived.at[s, r]) for r in range(rows)]
        for s in range(steps)
    ]
    for r in range(rows):
        for s in range(steps):
            copies[s][r].start()
    packed = [[jnp.zeros((TILE, lanes), F32)] * cols.shape[1] for _ in range(steps)]
    for r in range(rows):
        for s in range(steps):
            copies[s][r].wait()
            for t in range(bins // TILE):
                value = laid[s, r, span(t), :]
                pack_columns(packed[s], value, r, t)
                put_rows(near_rows.at[s], far_rows.at[s], t, value, r == 0, r == rows - 1)
    for s in range(steps):
        for g in range(cols.shape[1]):
            cols[s, g] = packed[s][g]


def seed_kernel(seed, coef, wind, grown, laid, arrived):
    rows, bins, _ = grown.shape
    copies = [pltpu.make_async_copy(seed.at[:, r, :], laid.at[r], arrived.at[r]) for r in range(rows)]
    for copy in copies:
        copy.start()
    for r in range(rows):
        copies[r].wait()
        half_wind = 0.5 * row_of(wind, r)
        for t in range(bins // TILE):
            grown[r, span(t), :] = laid[r, span(t), :] * jnp.exp(half_wind * coef[GROWTH, span(t), :])


def moved_of(laid, near_rows, far_rows, columns, coef, s1, s2, r, t, first, last):
    value = laid[r, span(t), :]
    prev_x = row_halo(near_rows, far_rows, t, True) if first else laid[r - 1, span(t), :]
    next_x = row_halo(near_rows, far_rows, t, False) if last else laid[r + 1, span(t), :]
    prev_y, next_y = along_lanes(value, columns, r, t)
    flow = (
        coef[STAY, span(t), :] * value
        + coef[FROM_PREV_X, span(t), :] * prev_x
        + coef[FROM_NEXT_X, span(t), :] * next_x
        + coef[FROM_PREV_Y, span(t), :] * prev_y
        + coef[FROM_NEXT_Y, span(t), :] * next_y
    )
    return s1 * flow + s2 * value


def forward_kernel(
    local, table, coef, laid, grown, sea, held, near_rows, far_rows, near_cols, far_cols,
    slots, wind_parts, moved_0, masks, columns, sums,
):
    _, rows, bins, _ = laid.shape
    set_masks(sea, held, masks)
    for s in range(2):
        join_columns(near_cols.at[s], far_cols.at[s], columns.at[s])
    zero = jnp.zeros((TILE, 128), F32)

    def body(r, first, last):
        s1, s2 = row_of(masks.at[0], r), row_of(masks.at[1], r)
        parts = [[zero] * local for _ in range(4)]
        for t in range(bins // TILE):
            early, later = (
                moved_of(laid.at[s], near_rows.at[s], far_rows.at[s], columns.at[s], coef, s1, s2, r, t, first, last)
                for s in range(2)
            )
            moved_0[r, span(t), :] = early
            term = grown[r, span(t), :] * later
            values = later, early, term, coef[GROWTH, span(t), :] * term
            for part, value in zip(parts, values):
                accumulate(part, t, value)
        at = r * TILE if isinstance(r, int) else pl.multiple_of(r * TILE, TILE)
        for i, part in enumerate(parts):
            for f in range(local):
                sums[i * local + f, pl.ds(at, TILE), :] = part[f]

    over_rows(rows, body)
    totals = [jnp.zeros((rows, 128), F32)] * 4
    for f in range(local):
        freq, weight = bin_constants(table, f, local)
        later, early = gathered(sums, f), gathered(sums, local + f)
        terms = weight * later, weight * freq * later, weight * early, weight * freq * early
        totals = [total + term for total, term in zip(totals, terms)]
        wind_parts[f] = gathered(sums, 3 * local + f)
    totals = totals + [gathered(sums, 2 * local + f) for f in range(local)]
    for i, value in enumerate(totals):
        for peer in range(slots.shape[0]):
            slots[peer, i] = value


def rates(energy, first):
    mean_freq = first / energy
    steep = steep_scale * energy * mean_freq**4
    inverse = 1.0 / (1.0 + steep)
    damping = (steep * inverse) ** 2
    q = damping / mean_freq
    return q, q / energy * (1.0 - 6.0 * inverse), q / first * (8.0 * inverse - 1.0)


def set_rates(local, table, q, by_energy, by_first, decays, rests):
    for f in range(local):
        freq, weight = bin_constants(table, f, local)
        decays[f] = jnp.exp((-0.5 * freq) * q)
        rests[f] = weight * by_energy + (weight * freq) * by_first


def lam_rows(local, source, masks, decays, rests, lam, near_rows, far_rows, cols, packed):
    rows, bins, _ = lam.shape
    for g in range(packed.shape[0]):
        packed[g] = jnp.zeros((TILE, 128), F32)

    def body(r, first, last):
        s1 = row_of(masks.at[0], r)
        decay = [row_of(decays.at[f], r) for f in range(local)]
        rest = [row_of(rests.at[f], r) for f in range(local)]
        columns = [packed[g] for g in range(packed.shape[0])]
        for t in range(bins // TILE):
            value = source[r, span(t), :] * pick(decay, t) + pick(rest, t)
            lam[r, span(t), :] = value
            flow = s1 * value
            pack_columns(columns, flow, r, t)
            put_rows(near_rows, far_rows, t, flow, first, last)
        for g in range(packed.shape[0]):
            packed[g] = columns[g]

    over_rows(rows, body)
    for g in range(packed.shape[0]):
        cols[g] = packed[g]


def lam_1_kernel(
    local, table, grown, sea, held, got, wind_parts,
    lam, wind_1, cells, near_rows, far_rows, cols, masks, decays, rests, packed,
):
    peers = got.shape[0]
    set_masks(sea, held, masks)

    def total(i):
        value = got[0, i]
        for peer in range(1, peers):
            value = value + got[peer, i]
        return value

    q, by_energy, by_first = rates(1.0 + total(0), 1.0 + total(1))
    cells[0], cells[1], cells[2] = rates(1.0 + total(2), 1.0 + total(3))
    lam_q = jnp.zeros_like(q)
    for peer in range(peers):
        for f in range(local):
            freq = float(frequency_table[peer * local + f])
            lam_q = lam_q + (-0.5 * freq) * jnp.exp((-0.5 * freq) * q) * got[peer, 4 + f]
    set_rates(local, table, q, lam_q * by_energy, lam_q * by_first, decays, rests)
    wind = jnp.zeros_like(q)
    for f in range(local):
        wind = wind + 0.5 * decays[f] * wind_parts[f]
    wind_1[...] = wind
    lam_rows(local, grown, masks, decays, rests, lam, near_rows, far_rows, cols, packed)


def back_of(lam, near_rows, far_rows, columns, coef, masks, r, t, first, last):
    value = lam[r, span(t), :]
    flow = row_of(masks.at[0], r) * value
    if first:
        prev_x = row_halo(near_rows, far_rows, t, True)
    else:
        prev_x = row_of(masks.at[0], r - 1) * lam[r - 1, span(t), :]
    if last:
        next_x = row_halo(near_rows, far_rows, t, False)
    else:
        next_x = row_of(masks.at[0], r + 1) * lam[r + 1, span(t), :]
    prev_y, next_y = along_lanes(flow, columns, r, t)
    return (
        row_of(masks.at[1], r) * value
        + coef[STAY, span(t), :] * flow
        + coef[FROM_NEXT_X, span(t), :] * prev_x
        + coef[FROM_PREV_X, span(t), :] * next_x
        + coef[FROM_NEXT_Y, span(t), :] * prev_y
        + coef[FROM_PREV_Y, span(t), :] * next_y
    )


def back_1_kernel(
    local, table, coef, lam, moved_0, wind, sea, held, cells, wind_1, near_rows, far_rows, near_cols, far_cols,
    grown, slots, masks, columns, decays, sums,
):
    rows, bins, _ = lam.shape
    set_masks(sea, held, masks)
    join_columns(near_cols, far_cols, columns)
    for f in range(local):
        freq, _ = bin_constants(table, f, local)
        decay = jnp.exp((-0.5 * freq) * cells[0])
        decays[f] = (-0.5 * freq) * decay
        decays[local + f] = 0.5 * decay
    zero = jnp.zeros((TILE, 128), F32)

    def body(r, first, last):
        half_wind = 0.5 * row_of(wind, r)
        for_q = [row_of(decays.at[f], r) for f in range(local)]
        for_wind = [row_of(decays.at[local + f], r) for f in range(local)]
        lam_q, lam_wind = zero, zero
        for t in range(bins // TILE):
            density = back_of(lam, near_rows, far_rows, columns, coef, masks, r, t, first, last)
            g = coef[GROWTH, span(t), :]
            density = density * jnp.exp(half_wind * g)
            grown[r, span(t), :] = density
            term = density * moved_0[r, span(t), :]
            lam_q = lam_q + pick(for_q, t) * term
            lam_wind = lam_wind + pick(for_wind, t) * (g * term)
        at = r * TILE if isinstance(r, int) else pl.multiple_of(r * TILE, TILE)
        sums[0, pl.ds(at, TILE), :] = lam_q
        sums[1, pl.ds(at, TILE), :] = lam_wind

    over_rows(rows, body)
    lam_q, lam_wind = gathered(sums, 0), gathered(sums, 1) + wind_1[...]
    for peer in range(slots.shape[0]):
        slots[peer, 0] = lam_q
        slots[peer, 1] = lam_wind


def lam_0_kernel(
    local, table, grown, sea, held, cells, got,
    lam, wind_total, near_rows, far_rows, cols, masks, decays, rests, packed,
):
    set_masks(sea, held, masks)
    lam_q, lam_wind = got[0, 0], got[0, 1]
    for peer in range(1, got.shape[0]):
        lam_q, lam_wind = lam_q + got[peer, 0], lam_wind + got[peer, 1]
    wind_total[...] = lam_wind
    set_rates(local, table, cells[0], lam_q * cells[1], lam_q * cells[2], decays, rests)
    lam_rows(local, grown, masks, decays, rests, lam, near_rows, far_rows, cols, packed)


def back_0_kernel(
    coef, lam, sea, held, near_rows, far_rows, near_cols, far_cols, out, laid, masks, columns, sent
):
    rows, bins, _ = lam.shape
    set_masks(sea, held, masks)
    join_columns(near_cols, far_cols, columns)
    copies = [pltpu.make_async_copy(laid.at[r], out.at[:, r, :], sent.at[r]) for r in range(rows)]
    for r in range(rows):
        for t in range(bins // TILE):
            laid[r, span(t), :] = back_of(
                lam, near_rows, far_rows, columns, coef, masks, r, t, r == 0, r == rows - 1
            )
        copies[r].start()
    for copy in copies:
        copy.wait()


def swap(near, far, axis):
    count = lax.axis_size(axis)

    def pairs(first):
        return [(i + a, i + 1 - a) for i in range(first, count - 1, 2) for a in (0, 1)]

    return lax.ppermute(near, axis, pairs(0)), lax.ppermute(far, axis, pairs(1))


def exchange(near_rows, far_rows, cols):
    return *swap(near_rows, far_rows, "gx"), *swap(cols, cols, "gy")


def call(body, outs, specs, *args, out_specs=None, scratch=(), us=2, mib=40):
    return pl.pallas_call(
        body,
        out_shape=[jax.ShapeDtypeStruct(shape, F32) for shape in outs],
        in_specs=specs,
        out_specs=out_specs or [VMEM] * len(outs),
        scratch_shapes=list(scratch),
        cost_estimate=pl.CostEstimate(flops=us * 1000000, bytes_accessed=us * 1000000, transcendentals=0),
        compiler_params=pltpu.CompilerParams(vmem_limit_bytes=mib * 1024 * 1024),
    )(*args)


def scratch(*shape):
    return pltpu.VMEM(shape, F32)


def coefficients(growth, speed, code):
    x, y = speed[0], speed[1]
    next_x, next_y = code % 2 == 1, code // 2 == 1
    values = [
        1.0 - x - y,
        jnp.where(next_x, 0.0, x),
        jnp.where(next_x, x, 0.0),
        jnp.where(next_y, 0.0, y),
        jnp.where(next_y, y, 0.0),
        growth,
    ]
    values = jnp.stack(values).reshape(len(values), -1, 1)
    return jnp.broadcast_to(values, values.shape[:2] + (128,))


def shards(trajectory, adjoint_seed, wind, growth, speed, code, sea, held):
    steps, local, dirs, nx, ny = trajectory.shape
    bins = local * dirs
    peers = lax.axis_size("sa")
    groups = -(-bins // (TILE * PACK))
    table = jnp.asarray(np.stack([frequency_table, weight_table]))

    rows, cols, whole, cell = (bins, ny), (groups, TILE, ny), (nx, bins, ny), (nx, ny)
    edges = [rows, rows, cols]
    masks, columns = scratch(2, *cell), scratch(*cols)
    decays, rests, packed = scratch(local, *cell), scratch(local, *cell), scratch(*cols)

    laid, *edge = call(
        edges_kernel,
        [(steps,) + shape for shape in [whole] + edges],
        [HBM],
        trajectory.reshape(steps, bins, nx, ny),
        scratch=[pltpu.SemaphoreType.DMA((steps, nx))],
        mib=40,
    )
    coef = coefficients(growth, speed, code)
    (grown,) = call(
        seed_kernel,
        [whole],
        [HBM, VMEM, VMEM],
        adjoint_seed.reshape(bins, nx, ny), coef, wind,
        scratch=[scratch(*whole), pltpu.SemaphoreType.DMA((nx,))],
    )
    halos = exchange(*edge)
    slots, wind_parts, moved_0 = call(
        functools.partial(forward_kernel, local),
        [(peers, 4 + local) + cell, (local,) + cell, whole],
        [SMEM] + [VMEM] * 9,
        table, coef, laid, grown, sea, held, *halos,
        scratch=[masks, scratch(steps, *cols), scratch(4 * local, nx * TILE, ny)],
    )
    got = lax.all_to_all(slots, "sa", 0, 0)
    lam, wind_1, cells, *edge = call(
        functools.partial(lam_1_kernel, local),
        [whole, cell, (3,) + cell] + edges,
        [SMEM] + [VMEM] * 5,
        table, grown, sea, held, got, wind_parts,
        scratch=[masks, decays, rests, packed],
    )
    halos = exchange(*edge)
    grown, slots = call(
        functools.partial(back_1_kernel, local),
        [whole, (peers, 2) + cell],
        [SMEM] + [VMEM] * 12,
        table, coef, lam, moved_0, wind, sea, held, cells, wind_1, *halos,
        scratch=[masks, columns, scratch(2 * local, *cell), scratch(2, nx * TILE, ny)],
    )
    got = lax.all_to_all(slots, "sa", 0, 0)
    lam, wind_total, *edge = call(
        functools.partial(lam_0_kernel, local),
        [whole, cell] + edges,
        [SMEM] + [VMEM] * 5,
        table, grown, sea, held, cells, got,
        scratch=[masks, decays, rests, packed],
    )
    halos = exchange(*edge)
    (out,) = call(
        back_0_kernel,
        [(bins, nx, ny)],
        [VMEM] * 8,
        coef, lam, sea, held, *halos,
        out_specs=[HBM],
        scratch=[scratch(*whole), masks, columns, pltpu.SemaphoreType.DMA((nx,))],
    )
    return out.reshape(local, dirs, nx, ny), wind_total


def solution(mesh):
    return jax.shard_map(
        shards,
        mesh=mesh,
        in_specs=(
            P(None, "sa", None, "gx", "gy"),
            P("sa", None, "gx", "gy"),
            P("gx", "gy"),
            P("sa", None),
            P(None, "sa", None),
            P("sa", None),
            P("gx", "gy"),
            P("gx", "gy"),
        ),
        out_specs=(P("sa", None, "gx", "gy"), P("gx", "gy")),
        check_vma=False,
    )
```

time: 221 us -> 112 us (0.51)
  local copies, waits for them, and re-layouts: 43.2 us -> 9.24 us
  blocking collectives: 70 us -> 36.6 us
  starting transfers between devices: 72.3 us -> 39.8 us
  Pallas kernels: 0 us -> 20.3 us
  other arithmetic: 19.2 us -> 1.76 us
  waiting for transfers between devices: 14.1 us -> 2.32 us
    psum x3 -> x0, blocking collectives: 70 us -> none  [the longest x2 41.2 us: adjoint_step(): lax.psum((lam_energy, lam_first, lam_wind), 'sa')]
    all_to_all x0 -> x2, blocking collectives: none -> 36.6 us  [shards(): got = lax.all_to_all(slots, 'sa', 0, 0)]
    ppermute x16 -> x12, starting transfers between devices: 72.3 us -> 39.8 us  [the longest x6 25.4 us: swap(): lax.ppermute(far, axis, pairs(1))]
    slice x17 -> x0, local copies, waits for them, and re-layouts: 27.1 us -> none  [the longest x10 12.7 us: extended(): lax.slice_in_dim(cells, cells.shape[dim] - width, cells.shape[dim], axis=...]
    pallas_call x0 -> x7, Pallas kernels: none -> 20.3 us  [call(): pl.pallas_call(body, out_shape=[jax.ShapeDtypeStruct(shape, F32) for shap...]
    ppermute x8 -> x0, local copies, waits for them, and re-layouts: 14.1 us -> none  [the longest x4 7.05 us: extended(): lax.ppermute(head, axis, [((i + 1) % count, i) for i in range(ends)])]
    reduce_sum x6 -> x0, other arithmetic: 13.3 us -> none  [the longest x2 6.44 us: source(): 0.5 * wind * growth[:, :, None, None]]
    ppermute x16 -> x12, waiting for transfers between devices: 14.1 us -> 2.32 us  [the longest x6 2.3 us: swap(): lax.ppermute(near, axis, pairs(0))]
  transfers between devices with their start and end apart: 16 -> 12, of which waited for: 4 -> 2; matrix products, arithmetic and copies ran while one was open for 13% -> 8% of each run, Pallas kernels for 0% -> 1%
where the time goes in v1:
time: 112 us; the launch traced here: 111 us
  starting transfers between devices  39.8 us (36%)
  blocking collectives  36.6 us (33%)
  Pallas kernels  20.3 us (18%)
  local copies, waits for them, and re-layouts  9.24 us (8%)
  waiting for transfers between devices  2.32 us (2%)
  other arithmetic  1.76 us (2%)
    all_to_all x2, blocking collectives, shards(): got = lax.all_to_all(slots, 'sa', 0, 0)  36.6 us
    ppermute x6, starting transfers between devices, swap(): lax.ppermute(far, axis, pairs(1))  25.4 us
    pallas_call x7, Pallas kernels, call(): pl.pallas_call(body, out_shape=[jax.ShapeDtypeStruct(shape, F32) for shap...  20.3 us
    ppermute x6, starting transfers between devices, swap(): lax.ppermute(near, axis, pairs(0))  14.4 us
    another operation x7, local copies, waits for them, and re-layouts, coefficients(): values = jnp.stack(values).reshape(len(values), -1, 1)  7.38 us
    ppermute x6, waiting for transfers between devices, swap(): lax.ppermute(near, axis, pairs(0))  2.3 us
  transfers between devices with their start and end apart: 12, of which 2 were waited for; matrix products, arithmetic and copies ran while one was open for 8% of the time, Pallas kernels for 1%

profile of v1, /device:TPU:57, one launch (start us, length us, event | category | flops | bytes accessed | tf_op | source)
XLA Modules:
  0.0 111.0 jit_solution(1528856702331160245)
XLA Ops:
  0.6 0.0 copy-start
  0.6 1.7 %copy-done = f32[2,4,36,16,128]{4,3,2,1,0:T(8,128)S(1)} copy-done((f32[2,4,36,16,128]{4,3,2,1,0:T(8,128)S(1)}, f32[2,4,36,16,128]{4,3,2,1,0:T(8,128)}, u32[]{:S(2)}) %copy-start) | copy-done | bytes 2359320
  2.3 0.0 copy-start.6
  2.3 0.0 copy-start.7
  2.3 0.0 copy-start.1
  2.3 0.0 copy-start.4
  2.3 5.3 %shard_map.105 = (f32[2,16,144,128]{3,2,1,0:T(8,128)S(1)}, f32[2,144,128]{2,1,0:T(8,128)}, f32[2,144,128]{2,1,0:T(8,128)}, f32[2,5,8,128]{3,2,1,0:T(8,128)}) custom-call(f32[2,144,16,128]{3,2,1,0:T(8,128)S(1)} %bitcast.16), custom_call_target="tpu_custom_call" | custom-call | flops 2000000 | bytes 2000000 | tf_op jit(solution)/shard_map/pallas_call | solution.py:410
  7.7 5.2 %collective-permute-start.3 = (f32[2,5,8,128]{3,2,1,0:T(8,128)}, f32[2,5,8,128]{3,2,1,0:T(8,128)}, u32[]{:S(2)}, u32[]{:S(2)}) collective-permute-start(f32[2,5,8,128]{3,2,1,0:T(8,128)} %get-tuple-element.25), channel_id=1, source_target_pairs={{8,16},{16,8},{9,17},{17,9},{10,18},{18,10},{11,19},{19,11},{12,20... | collective-permute-start | bytes 122888 | tf_op jit(solution)/shard_map/ppermute | solution.py:402
  12.9 1.9 %collective-permute-start.2 = (f32[2,5,8,128]{3,2,1,0:T(8,128)}, f32[2,5,8,128]{3,2,1,0:T(8,128)}, u32[]{:S(2)}, u32[]{:S(2)}) collective-permute-start(f32[2,5,8,128]{3,2,1,0:T(8,128)} %get-tuple-element.25), channel_id=1, source_target_pairs={{0,8},{8,0},{16,24},{24,16},{1,9},{9,1},{17,25},{25,17},{2,10},{10... | collective-permute-start | bytes 122888 | tf_op jit(solution)/shard_map/ppermute | solution.py:402
  14.8 3.0 %collective-permute-start = (f32[2,144,128]{2,1,0:T(8,128)}, f32[2,144,128]{2,1,0:T(8,128)}, u32[]{:S(2)}, u32[]{:S(2)}) collective-permute-start(f32[2,144,128]{2,1,0:T(8,128)} %get-tuple-element.23), channel_id=1, source_target_pairs={{0,32},{32,0},{64,96},{96,64},{128,160},{160,128},{192,224},{224,1... | collective-permute-start | bytes 442376 | tf_op jit(solution)/shard_map/ppermute | solution.py:402
  17.8 1.9 %collective-permute-start.1 = (f32[2,144,128]{2,1,0:T(8,128)}, f32[2,144,128]{2,1,0:T(8,128)}, u32[]{:S(2)}, u32[]{:S(2)}) collective-permute-start(f32[2,144,128]{2,1,0:T(8,128)} %get-tuple-element.24), channel_id=1, source_target_pairs={{32,64},{64,32},{96,128},{128,96},{160,192},{192,160},{224,256},{2... | collective-permute-start | bytes 442376 | tf_op jit(solution)/shard_map/ppermute | solution.py:402
  19.7 0.0 copy-done.6
  19.7 0.0 copy-done.7
  19.7 0.6 bitcast_select_fusion
  20.3 0.6 bitcast_select_fusion.1
  20.9 0.6 subtract_subtract_fusion
  21.5 1.3 %stack.26 = f32[1,144,1]{1,2,0:T(1,128)} reshape(f32[4,36]{1,0:T(4,128)} %param.12) | data formatting | bytes 1152 | tf_op jit(solution)/shard_map/stack | solution.py:436
  22.8 1.4 %stack.21 = f32[1,144,1]{1,2,0:T(1,128)} reshape(f32[1,4,36]{2,1,0:T(4,128)} %subtract_subtract_fusion) | data formatting | bytes 1152 | tf_op jit(solution)/shard_map/stack | solution.py:436
  24.2 1.3 %stack.25 = f32[1,144,1]{1,2,0:T(1,128)} reshape(f32[4,36]{1,0:T(4,128)} %get-tuple-element.42) | data formatting | bytes 1152 | tf_op jit(solution)/shard_map/stack | solution.py:436
  25.5 0.7 stack.23
  26.2 0.6 stack.22
  26.8 1.3 %stack.24 = f32[1,144,1]{1,2,0:T(1,128)} reshape(f32[4,36]{1,0:T(4,128)} %bitcast_select_fusion.1) | data formatting | bytes 1152 | tf_op jit(solution)/shard_map/stack | solution.py:436
  28.2 0.7 stack.27
  28.9 0.2 broadcast_in_dim.17.coef
  29.1 0.0 copy-done.1
  29.1 0.0 copy-done.4
  29.1 0.0 copy-start.2
  29.1 0.0 copy-start.3
  29.1 0.0 copy-start.5
  29.1 1.3 %shard_map.104.grown = f32[16,144,128]{2,1,0:T(8,128)S(1)} custom-call(f32[144,16,128]{2,1,0:T(8,128)S(1)} %bitcast.17, f32[6,144,128]{2,1,0:T(8,128)S(1)} %broadcast_in_dim.17.coef, f32[16,128]{1,0:T(8,128)S(1)} %copy-done.4), custom_call_target="tpu_custom_call" | custom-call | flops 2000000 | bytes 2000000 | tf_op jit(solution)/shard_map/pallas_call | solution.py:410
  30.5 0.0 collective-permute-done.3.far_cols
  30.5 0.0 collective-permute-done.2.near_cols
  30.5 0.0 collective-permute-done.near_rows
  30.5 0.0 collective-permute-done.1.far_rows
  30.5 0.0 copy-done.2
  30.5 0.0 copy-done.3
  30.5 0.0 copy-done.5
  30.5 4.3 %shard_map.106 = (f32[8,8,16,128]{3,2,1,0:T(8,128)S(1)}, f32[4,16,128]{2,1,0:T(8,128)S(1)}, f32[16,144,128]{2,1,0:T(8,128)S(1)}) custom-call(f32[2,32]{1,0:T(2,128)S(1)} %copy-done.5, f32[6,144,128]{2,1,0:T(8,128)S(1)} %broadcast_in_dim.17.coef, f32[2,16,144,128]{3,2,1,0:T(8,128)S(1)} %get-tuple-element.22.laid, f32[16,144,128]{2,1,0:T(8,128)S(1)} %shard_map.104.grown, ...), custom_call_target="tpu_custom_call" | custom-call | flops 2000000 | bytes 2000000 | tf_op jit(solution)/shard_map/pallas_call | solution.py:410
  34.9 25.6 %all_to_all.10.got = f32[8,8,16,128]{3,2,1,0:T(8,128)S(1)} all-to-all(f32[8,8,16,128]{3,2,1,0:T(8,128)S(1)} %get-tuple-element.26), channel_id=1, replica_groups=mesh['gx'=16,'gy'=4,'sa'=8] {'sa'}, dimensions={0} | all-to-all | bytes 1048576 | tf_op jit(solution)/shard_map/all_to_all | solution.py:476
  60.5 2.1 %shard_map.107 = (f32[16,144,128]{2,1,0:T(8,128)S(1)}, f32[16,128]{1,0:T(8,128)S(1)}, f32[3,16,128]{2,1,0:T(8,128)S(1)}, f32[144,128]{1,0:T(8,128)S(1)}, f32[144...) custom-call(f32[2,32]{1,0:T(2,128)S(1)} %copy-done.5, f32[16,144,128]{2,1,0:T(8,128)S(1)} %shard_map.104.grown, ...), custom_call_target="tpu_custom_call" | custom-call | flops 2000000 | bytes 2000000 | tf_op jit(solution)/shard_map/pallas_call | solution.py:410
  62.6 3.7 %collective-permute-start.4 = (f32[144,128]{1,0:T(8,128)S(1)}, f32[144,128]{1,0:T(8,128)S(1)}, u32[]{:S(2)}, u32[]{:S(2)}) collective-permute-start(f32[144,128]{1,0:T(8,128)S(1)} %get-tuple-element.32), channel_id=1, source_target_pairs={{0,32},{32,0},{64,96},{96,64},{128,160},{160,128},{192,224},{224,1... | collective-permute-start | bytes 221192 | tf_op jit(solution)/shard_map/ppermute | solution.py:402
  66.4 3.4 %collective-permute-start.5 = (f32[144,128]{1,0:T(8,128)S(1)}, f32[144,128]{1,0:T(8,128)S(1)}, u32[]{:S(2)}, u32[]{:S(2)}) collective-permute-start(f32[144,128]{1,0:T(8,128)S(1)} %get-tuple-element.33), channel_id=1, source_target_pairs={{32,64},{64,32},{96,128},{128,96},{160,192},{192,160},{224,256},{2... | collective-permute-start | bytes 221192 | tf_op jit(solution)/shard_map/ppermute | solution.py:402
  69.7 5.6 %collective-permute-start.7 = (f32[5,8,128]{2,1,0:T(8,128)S(1)}, f32[5,8,128]{2,1,0:T(8,128)S(1)}, u32[]{:S(2)}, u32[]{:S(2)}) collective-permute-start(f32[5,8,128]{2,1,0:T(8,128)S(1)} %get-tuple-element.34), channel_id=1, source_target_pairs={{8,16},{16,8},{9,17},{17,9},{10,18},{18,10},{11,19},{19,11},{12,20... | collective-permute-start | bytes 61448 | tf_op jit(solution)/shard_map/ppermute | solution.py:402
  75.3 1.9 %collective-permute-start.6 = (f32[5,8,128]{2,1,0:T(8,128)S(1)}, f32[5,8,128]{2,1,0:T(8,128)S(1)}, u32[]{:S(2)}, u32[]{:S(2)}) collective-permute-start(f32[5,8,128]{2,1,0:T(8,128)S(1)} %get-tuple-element.34), channel_id=1, source_target_pairs={{0,8},{8,0},{16,24},{24,16},{1,9},{9,1},{17,25},{25,17},{2,10},{10... | collective-permute-start | bytes 61448 | tf_op jit(solution)/shard_map/ppermute | solution.py:402
  77.3 0.0 collective-permute-done.7.far_cols
  77.3 1.1 %collective-permute-done.6.near_cols = f32[5,8,128]{2,1,0:T(8,128)S(1)} collective-permute-done((f32[5,8,128]{2,1,0:T(8,128)S(1)}, f32[5,8,128]{2,1,0:T(8,128)S(1)}, u32[]{:S(2)}, u32[]{:S(2)}) %collective-permute-start.6) | collective-permute-done | bytes 20512 | tf_op jit(solution)/shard_map/ppermute | solution.py:402
  78.4 0.0 collective-permute-done.4.near_rows
  78.4 0.0 collective-permute-done.5.far_rows
  78.4 2.8 %shard_map.108 = (f32[16,144,128]{2,1,0:T(8,128)S(1)}, f32[8,2,16,128]{3,2,1,0:T(8,128)S(1)}) custom-call(f32[2,32]{1,0:T(2,128)S(1)} %copy-done.5, f32[6,144,128]{2,1,0:T(8,128)S(1)} %broadcast_in_dim.17.coef, f32[16,144,128]{2,1,0:T(8,128)S(1)} %get-tuple-element.28.lam, f32[16,144,128]{2,1,0:T(8,128)S(1)} %get-tuple-element.29.moved_0, ...), custom_call_target="tpu_custom_call" | custom-call | flops 2000000 | bytes 2000000 | tf_op jit(solution)/shard_map/pallas_call | solution.py:410
  81.3 11.0 %all_to_all.11.got = f32[8,2,16,128]{3,2,1,0:T(8,128)S(1)} all-to-all(f32[8,2,16,128]{3,2,1,0:T(8,128)S(1)} %get-tuple-element.36), channel_id=1, replica_groups=mesh['gx'=16,'gy'=4,'sa'=8] {'sa'}, dimensions={0} | all-to-all | bytes 262144 | tf_op jit(solution)/shard_map/all_to_all | solution.py:492
  92.3 2.5 %shard_map.109 = (f32[16,144,128]{2,1,0:T(8,128)S(1)}, f32[16,128]{1,0:T(8,128)}, f32[144,128]{1,0:T(8,128)S(1)}, f32[144,128]{1,0:T(8,128)S(1)}, f32[5,8,128]{2,1,0:T(8,128)S(1)}) custom-call(f32[2,32]{1,0:T(2,128)S(1)} %copy-done.5, f32[16,144,128]{2,1,0:T(8,128)S(1)} %get-tuple-element.35.grown, s32[16,128]{1,0:T(8,128)S(1)} %copy-done.2, ...), custom_call_target="tpu_custom_call" | custom-call | flops 2000000 | bytes 2000000 | tf_op jit(solution)/shard_map/pallas_call | solution.py:410
  94.8 1.9 %collective-permute-start.8 = (f32[144,128]{1,0:T(8,128)S(1)}, f32[144,128]{1,0:T(8,128)S(1)}, u32[]{:S(2)}, u32[]{:S(2)}) collective-permute-start(f32[144,128]{1,0:T(8,128)S(1)} %get-tuple-element.38), channel_id=1, source_target_pairs={{0,32},{32,0},{64,96},{96,64},{128,160},{160,128},{192,224},{224,1... | collective-permute-start | bytes 221192 | tf_op jit(solution)/shard_map/ppermute | solution.py:402
  96.7 4.2 %collective-permute-start.9 = (f32[144,128]{1,0:T(8,128)S(1)}, f32[144,128]{1,0:T(8,128)S(1)}, u32[]{:S(2)}, u32[]{:S(2)}) collective-permute-start(f32[144,128]{1,0:T(8,128)S(1)} %get-tuple-element.39), channel_id=1, source_target_pairs={{32,64},{64,32},{96,128},{128,96},{160,192},{192,160},{224,256},{2... | collective-permute-start | bytes 221192 | tf_op jit(solution)/shard_map/ppermute | solution.py:402
  100.9 5.2 %collective-permute-start.11 = (f32[5,8,128]{2,1,0:T(8,128)S(1)}, f32[5,8,128]{2,1,0:T(8,128)S(1)}, u32[]{:S(2)}, u32[]{:S(2)}) collective-permute-start(f32[5,8,128]{2,1,0:T(8,128)S(1)} %get-tuple-element.40), channel_id=1, source_target_pairs={{8,16},{16,8},{9,17},{17,9},{10,18},{18,10},{11,19},{19,11},{12,20... | collective-permute-start | bytes 61448 | tf_op jit(solution)/shard_map/ppermute | solution.py:402
  106.1 1.9 %collective-permute-start.10 = (f32[5,8,128]{2,1,0:T(8,128)S(1)}, f32[5,8,128]{2,1,0:T(8,128)S(1)}, u32[]{:S(2)}, u32[]{:S(2)}) collective-permute-start(f32[5,8,128]{2,1,0:T(8,128)S(1)} %get-tuple-element.40), channel_id=1, source_target_pairs={{0,8},{8,0},{16,24},{24,16},{1,9},{9,1},{17,25},{25,17},{2,10},{10... | collective-permute-start | bytes 61448 | tf_op jit(solution)/shard_map/ppermute | solution.py:402
  108.0 0.0 collective-permute-done.11.far_cols
  108.0 1.1 %collective-permute-done.10.near_cols = f32[5,8,128]{2,1,0:T(8,128)S(1)} collective-permute-done((f32[5,8,128]{2,1,0:T(8,128)S(1)}, f32[5,8,128]{2,1,0:T(8,128)S(1)}, u32[]{:S(2)}, u32[]{:S(2)}) %collective-permute-start.10) | collective-permute-done | bytes 20512 | tf_op jit(solution)/shard_map/ppermute | solution.py:402
  109.1 0.0 collective-permute-done.8.near_rows
  109.1 0.0 collective-permute-done.9.far_rows
  109.1 1.8 %shard_map.110 = f32[144,16,128]{2,1,0:T(8,128)} custom-call(f32[6,144,128]{2,1,0:T(8,128)S(1)} %broadcast_in_dim.17.coef, f32[16,144,128]{2,1,0:T(8,128)S(1)} %get-tuple-element.37.lam, s32[16,128]{1,0:T(8,128)S(1)} %copy-done.2, s32[16,128]{1,0:T(8,128)S(1)} %copy-done.3, f32[144,128]{1,0:T(8,128)S(1)} %collective-permute-done.8.near_rows, ...), custom_call_target="tpu_custom_call" | custom-call | flops 2000000 | bytes 2000000 | tf_op jit(solution)/shard_map/pallas_call | solution.py:410
Async XLA Ops:
  0.6 1.7 %copy-start = (f32[2,4,36,16,128]{4,3,2,1,0:T(8,128)S(1)}, f32[2,4,36,16,128]{4,3,2,1,0:T(8,128)}, u32[]{:S(2)}) copy-start(f32[2,4,36,16,128]{4,3,2,1,0:T(8,128)} %param.9) | copy-start | bytes 7077892
  2.3 17.4 %copy-start.6 = (f32[2,4,36]{2,1,0:T(4,128)S(1)}, f32[2,4,36]{2,1,0:T(4,128)}, u32[]{:S(2)}) copy-start(f32[2,4,36]{2,1,0:T(4,128)} %param.13) | copy-start | bytes 3460
  2.3 17.4 %copy-start.7 = (s32[4,36]{1,0:T(4,128)S(1)}, s32[4,36]{1,0:T(4,128)}, u32[]{:S(2)}) copy-start(s32[4,36]{1,0:T(4,128)} %param.14) | copy-start | bytes 1732
  2.3 26.8 %copy-start.1 = (f32[4,36,16,128]{3,2,1,0:T(8,128)S(1)}, f32[4,36,16,128]{3,2,1,0:T(8,128)}, u32[]{:S(2)}) copy-start(f32[4,36,16,128]{3,2,1,0:T(8,128)} %param.10) | copy-start | bytes 3538948
  2.3 26.8 %copy-start.4 = (f32[16,128]{1,0:T(8,128)S(1)}, f32[16,128]{1,0:T(8,128)}, u32[]{:S(2)}) copy-start(f32[16,128]{1,0:T(8,128)} %wind.3) | copy-start | bytes 24580
  7.7 22.8 %collective-permute-start.3 = (f32[2,5,8,128]{3,2,1,0:T(8,128)}, f32[2,5,8,128]{3,2,1,0:T(8,128)}, u32[]{:S(2)}, u32[]{:S(2)}) collective-permute-start(f32[2,5,8,128]{3,2,1,0:T(8,128)} %get-tuple-element.25), channel_id=1, source_target_pairs={{8,16},{16,8},{9,17},{17,9},{10,18},{18,10},{11,19},{19,11},{12,20... | collective-permute-start | bytes 122888 | tf_op jit(solution)/shard_map/ppermute | solution.py:402
  12.9 17.6 %collective-permute-start.2 = (f32[2,5,8,128]{3,2,1,0:T(8,128)}, f32[2,5,8,128]{3,2,1,0:T(8,128)}, u32[]{:S(2)}, u32[]{:S(2)}) collective-permute-start(f32[2,5,8,128]{3,2,1,0:T(8,128)} %get-tuple-element.25), channel_id=1, source_target_pairs={{0,8},{8,0},{16,24},{24,16},{1,9},{9,1},{17,25},{25,17},{2,10},{10... | collective-permute-start | bytes 122888 | tf_op jit(solution)/shard_map/ppermute | solution.py:402
  14.8 15.7 %collective-permute-start = (f32[2,144,128]{2,1,0:T(8,128)}, f32[2,144,128]{2,1,0:T(8,128)}, u32[]{:S(2)}, u32[]{:S(2)}) collective-permute-start(f32[2,144,128]{2,1,0:T(8,128)} %get-tuple-element.23), channel_id=1, source_target_pairs={{0,32},{32,0},{64,96},{96,64},{128,160},{160,128},{192,224},{224,1... | collective-permute-start | bytes 442376 | tf_op jit(solution)/shard_map/ppermute | solution.py:402
  17.8 12.7 %collective-permute-start.1 = (f32[2,144,128]{2,1,0:T(8,128)}, f32[2,144,128]{2,1,0:T(8,128)}, u32[]{:S(2)}, u32[]{:S(2)}) collective-permute-start(f32[2,144,128]{2,1,0:T(8,128)} %get-tuple-element.24), channel_id=1, source_target_pairs={{32,64},{64,32},{96,128},{128,96},{160,192},{192,160},{224,256},{2... | collective-permute-start | bytes 442376 | tf_op jit(solution)/shard_map/ppermute | solution.py:402
  29.1 1.4 %copy-start.2 = (s32[16,128]{1,0:T(8,128)S(1)}, s32[16,128]{1,0:T(8,128)}, u32[]{:S(2)}) copy-start(s32[16,128]{1,0:T(8,128)} %sea.9) | copy-start | bytes 24580
  29.1 1.4 %copy-start.3 = (s32[16,128]{1,0:T(8,128)S(1)}, s32[16,128]{1,0:T(8,128)}, u32[]{:S(2)}) copy-start(s32[16,128]{1,0:T(8,128)} %held.9) | copy-start | bytes 24580
  29.1 1.4 %copy-start.5 = (f32[2,32]{1,0:T(2,128)S(1)}, f32[2,32]{1,0:T(2,128)}, u32[]{:S(2)}) copy-start(f32[2,32]{1,0:T(2,128)} %constant.33.clone.table) | copy-start | bytes 772
  62.6 15.8 %collective-permute-start.4 = (f32[144,128]{1,0:T(8,128)S(1)}, f32[144,128]{1,0:T(8,128)S(1)}, u32[]{:S(2)}, u32[]{:S(2)}) collective-permute-start(f32[144,128]{1,0:T(8,128)S(1)} %get-tuple-element.32), channel_id=1, source_target_pairs={{0,32},{32,0},{64,96},{96,64},{128,160},{160,128},{192,224},{224,1... | collective-permute-start | bytes 221192 | tf_op jit(solution)/shard_map/ppermute | solution.py:402
  66.4 12.1 %collective-permute-start.5 = (f32[144,128]{1,0:T(8,128)S(1)}, f32[144,128]{1,0:T(8,128)S(1)}, u32[]{:S(2)}, u32[]{:S(2)}) collective-permute-start(f32[144,128]{1,0:T(8,128)S(1)} %get-tuple-element.33), channel_id=1, source_target_pairs={{32,64},{64,32},{96,128},{128,96},{160,192},{192,160},{224,256},{2... | collective-permute-start | bytes 221192 | tf_op jit(solution)/shard_map/ppermute | solution.py:402
  69.7 7.5 %collective-permute-start.7 = (f32[5,8,128]{2,1,0:T(8,128)S(1)}, f32[5,8,128]{2,1,0:T(8,128)S(1)}, u32[]{:S(2)}, u32[]{:S(2)}) collective-permute-start(f32[5,8,128]{2,1,0:T(8,128)S(1)} %get-tuple-element.34), channel_id=1, source_target_pairs={{8,16},{16,8},{9,17},{17,9},{10,18},{18,10},{11,19},{19,11},{12,20... | collective-permute-start | bytes 61448 | tf_op jit(solution)/shard_map/ppermute | solution.py:402
  75.3 3.1 %collective-permute-start.6 = (f32[5,8,128]{2,1,0:T(8,128)S(1)}, f32[5,8,128]{2,1,0:T(8,128)S(1)}, u32[]{:S(2)}, u32[]{:S(2)}) collective-permute-start(f32[5,8,128]{2,1,0:T(8,128)S(1)} %get-tuple-element.34), channel_id=1, source_target_pairs={{0,8},{8,0},{16,24},{24,16},{1,9},{9,1},{17,25},{25,17},{2,10},{10... | collective-permute-start | bytes 61448 | tf_op jit(solution)/shard_map/ppermute | solution.py:402
  94.8 14.4 %collective-permute-start.8 = (f32[144,128]{1,0:T(8,128)S(1)}, f32[144,128]{1,0:T(8,128)S(1)}, u32[]{:S(2)}, u32[]{:S(2)}) collective-permute-start(f32[144,128]{1,0:T(8,128)S(1)} %get-tuple-element.38), channel_id=1, source_target_pairs={{0,32},{32,0},{64,96},{96,64},{128,160},{160,128},{192,224},{224,1... | collective-permute-start | bytes 221192 | tf_op jit(solution)/shard_map/ppermute | solution.py:402
  96.7 12.5 %collective-permute-start.9 = (f32[144,128]{1,0:T(8,128)S(1)}, f32[144,128]{1,0:T(8,128)S(1)}, u32[]{:S(2)}, u32[]{:S(2)}) collective-permute-start(f32[144,128]{1,0:T(8,128)S(1)} %get-tuple-element.39), channel_id=1, source_target_pairs={{32,64},{64,32},{96,128},{128,96},{160,192},{192,160},{224,256},{2... | collective-permute-start | bytes 221192 | tf_op jit(solution)/shard_map/ppermute | solution.py:402
  100.9 7.1 %collective-permute-start.11 = (f32[5,8,128]{2,1,0:T(8,128)S(1)}, f32[5,8,128]{2,1,0:T(8,128)S(1)}, u32[]{:S(2)}, u32[]{:S(2)}) collective-permute-start(f32[5,8,128]{2,1,0:T(8,128)S(1)} %get-tuple-element.40), channel_id=1, source_target_pairs={{8,16},{16,8},{9,17},{17,9},{10,18},{18,10},{11,19},{19,11},{12,20... | collective-permute-start | bytes 61448 | tf_op jit(solution)/shard_map/ppermute | solution.py:402
  106.1 3.1 %collective-permute-start.10 = (f32[5,8,128]{2,1,0:T(8,128)S(1)}, f32[5,8,128]{2,1,0:T(8,128)S(1)}, u32[]{:S(2)}, u32[]{:S(2)}) collective-permute-start(f32[5,8,128]{2,1,0:T(8,128)S(1)} %get-tuple-element.40), channel_id=1, source_target_pairs={{0,8},{8,0},{16,24},{24,16},{1,9},{9,1},{17,25},{25,17},{2,10},{10... | collective-permute-start | bytes 61448 | tf_op jit(solution)/shard_map/ppermute | solution.py:402

commit v2 on v1

--- a/solution.py
+++ b/solution.py
@@ -12,6 +12,7 @@
 DIRS = 36
 TILE = 8
 PACK = 4
+WAITS = 4
 F32 = jnp.float32
 
 steep_scale = 0.05
@@ -69,15 +70,22 @@
         sums[f] = sums[f] + value
 
 
-def over_rows(count, body):
-    body(0, True, False)
-
+def inner_rows(count, body):
     def inner(r, carry):
         body(r, False, False)
         return carry
 
     lax.fori_loop(1, count - 1, inner, 0)
+
+
+def outer_rows(count, body):
+    body(0, True, False)
     body(count - 1, False, True)
+
+
+def tile_at(r):
+    at = r * TILE if isinstance(r, int) else pl.multiple_of(r * TILE, TILE)
+    return pl.ds(at, TILE)
 
 
 def column_lane(r, t):
@@ -155,8 +163,11 @@
             copies[s][r].start()
     packed = [[jnp.zeros((TILE, lanes), F32)] * cols.shape[1] for _ in range(steps)]
     for r in range(rows):
+        if r % WAITS == 0:
+            for s in range(steps):
+                for copy in copies[s][r : r + WAITS]:
+                    copy.wait()
         for s in range(steps):
-            copies[s][r].wait()
             for t in range(bins // TILE):
                 value = laid[s, r, span(t), :]
                 pack_columns(packed[s], value, r, t)
@@ -166,13 +177,33 @@
             cols[s, g] = packed[s][g]
 
 
-def seed_kernel(seed, coef, wind, grown, laid, arrived):
-    rows, bins, _ = grown.shape
+def prepare_kernel(local, growth, speed, code, seed, wind, coef, grown, laid, arrived):
+    rows, bins, lanes = grown.shape
     copies = [pltpu.make_async_copy(seed.at[:, r, :], laid.at[r], arrived.at[r]) for r in range(rows)]
     for copy in copies:
         copy.start()
+
+    def fill(d, carry):
+        for f in range(local):
+            x, y = speed[0, f, d], speed[1, f, d]
+            next_x, next_y = lax.rem(code[f, d], 2) == 1, code[f, d] >= 2
+            values = [
+                1.0 - x - y,
+                jnp.where(next_x, 0.0, x),
+                jnp.where(next_x, x, 0.0),
+                jnp.where(next_y, 0.0, y),
+                jnp.where(next_y, y, 0.0),
+                growth[f, d],
+            ]
+            for k, value in enumerate(values):
+                coef[k, pl.ds(f * DIRS + d, 1), :] = jnp.full((1, lanes), value, F32)
+        return carry
+
+    lax.fori_loop(0, DIRS, fill, 0)
     for r in range(rows):
-        copies[r].wait()
+        if r % WAITS == 0:
+            for copy in copies[r : r + WAITS]:
+                copy.wait()
         half_wind = 0.5 * row_of(wind, r)
         for t in range(bins // TILE):
             grown[r, span(t), :] = laid[r, span(t), :] * jnp.exp(half_wind * coef[GROWTH, span(t), :])
@@ -193,43 +224,70 @@
     return s1 * flow + s2 * value
 
 
-def forward_kernel(
-    local, table, coef, laid, grown, sea, held, near_rows, far_rows, near_cols, far_cols,
-    slots, wind_parts, moved_0, masks, columns, sums,
+def forward_row(local, coef, laid, grown, masks, halos, columns, sums, moved_0, r, first, last):
+    bins = laid.shape[2]
+    s1, s2 = row_of(masks.at[0], r), row_of(masks.at[1], r)
+    parts = [[jnp.zeros((TILE, 128), F32)] * local for _ in range(4)]
+    for t in range(bins // TILE):
+        early, later = (
+            moved_of(laid.at[s], *(h if h is None else h.at[s] for h in halos), columns.at[s], coef, s1, s2, r, t, first, last)
+            for s in range(2)
+        )
+        moved_0[span(t), :] = early
+        term = grown[r, span(t), :] * later
+        values = later, early, term, coef[GROWTH, span(t), :] * term
+        for part, value in zip(parts, values):
+            accumulate(part, t, value)
+    for i, part in enumerate(parts):
+        for f in range(local):
+            sums[i * local + f, tile_at(r), :] = part[f]
+
+
+def clear_tiles(sums, rows):
+    for q in range(sums.shape[0]):
+        for r in rows:
+            sums[q, tile_at(r), :] = jnp.zeros((TILE, 128), F32)
+
+
+def inner_forward_kernel(
+    local, coef, laid, grown, sea, held, near_cols, far_cols, parts, moved_0, joined, masks, sums
 ):
-    _, rows, bins, _ = laid.shape
+    _, rows, _, _ = laid.shape
     set_masks(sea, held, masks)
     for s in range(2):
-        join_columns(near_cols.at[s], far_cols.at[s], columns.at[s])
-    zero = jnp.zeros((TILE, 128), F32)
+        join_columns(near_cols.at[s], far_cols.at[s], joined.at[s])
+    clear_tiles(sums, (0, rows - 1))
 
     def body(r, first, last):
-        s1, s2 = row_of(masks.at[0], r), row_of(masks.at[1], r)
-        parts = [[zero] * local for _ in range(4)]
-        for t in range(bins // TILE):
-            early, later = (
-                moved_of(laid.at[s], near_rows.at[s], far_rows.at[s], columns.at[s], coef, s1, s2, r, t, first, last)
-                for s in range(2)
-            )
-            moved_0[r, span(t), :] = early
-            term = grown[r, span(t), :] * later
-            values = later, early, term, coef[GROWTH, span(t), :] * term
-            for part, value in zip(parts, values):
-                accumulate(part, t, value)
-        at = r * TILE if isinstance(r, int) else pl.multiple_of(r * TILE, TILE)
-        for i, part in enumerate(parts):
-            for f in range(local):
-                sums[i * local + f, pl.ds(at, TILE), :] = part[f]
-
-    over_rows(rows, body)
+        forward_row(local, coef, laid, grown, masks, (None, None), joined, sums, moved_0.at[r], r, first, last)
+
+    inner_rows(rows, body)
+    for q in range(parts.shape[0]):
+        parts[q] = gathered(sums, q)
+
+
+def outer_forward_kernel(
+    local, table, coef, laid, grown, sea, held, joined, parts, near_rows, far_rows,
+    slots, wind_parts, moved_0, masks, sums,
+):
+    _, rows, _, _ = laid.shape
+    set_masks(sea, held, masks)
+    clear_tiles(sums, range(1, rows - 1))
+
+    def body(r, first, last):
+        halos = near_rows, far_rows
+        out = moved_0.at[int(last)]
+        forward_row(local, coef, laid, grown, masks, halos, joined, sums, out, r, first, last)
+
+    outer_rows(rows, body)
     totals = [jnp.zeros((rows, 128), F32)] * 4
     for f in range(local):
         freq, weight = bin_constants(table, f, local)
-        later, early = gathered(sums, f), gathered(sums, local + f)
+        later, early = (parts[i * local + f] + gathered(sums, i * local + f) for i in range(2))
         terms = weight * later, weight * freq * later, weight * early, weight * freq * early
         totals = [total + term for total, term in zip(totals, terms)]
-        wind_parts[f] = gathered(sums, 3 * local + f)
-    totals = totals + [gathered(sums, 2 * local + f) for f in range(local)]
+        wind_parts[f] = parts[3 * local + f] + gathered(sums, 3 * local + f)
+    totals = totals + [parts[2 * local + f] + gathered(sums, 2 * local + f) for f in range(local)]
     for i, value in enumerate(totals):
         for peer in range(slots.shape[0]):
             slots[peer, i] = value
@@ -251,7 +309,7 @@
         rests[f] = weight * by_energy + (weight * freq) * by_first
 
 
-def lam_rows(local, source, masks, decays, rests, lam, near_rows, far_rows, cols, packed):
+def lam_rows(local, source, outer, masks, decays, rests, lam, near_rows, far_rows, cols, packed):
     rows, bins, _ = lam.shape
     for g in range(packed.shape[0]):
         packed[g] = jnp.zeros((TILE, 128), F32)
@@ -262,7 +320,8 @@
         rest = [row_of(rests.at[f], r) for f in range(local)]
         columns = [packed[g] for g in range(packed.shape[0])]
         for t in range(bins // TILE):
-            value = source[r, span(t), :] * pick(decay, t) + pick(rest, t)
+            known = outer[int(last), span(t), :] if outer is not None and (first or last) else source[r, span(t), :]
+            value = known * pick(decay, t) + pick(rest, t)
             lam[r, span(t), :] = value
             flow = s1 * value
             pack_columns(columns, flow, r, t)
@@ -270,7 +329,8 @@
         for g in range(packed.shape[0]):
             packed[g] = columns[g]
 
-    over_rows(rows, body)
+    inner_rows(rows, body)
+    outer_rows(rows, body)
     for g in range(packed.shape[0]):
         cols[g] = packed[g]
 
@@ -300,7 +360,7 @@
     for f in range(local):
         wind = wind + 0.5 * decays[f] * wind_parts[f]
     wind_1[...] = wind
-    lam_rows(local, grown, masks, decays, rests, lam, near_rows, far_rows, cols, packed)
+    lam_rows(local, grown, None, masks, decays, rests, lam, near_rows, far_rows, cols, packed)
 
 
 def back_of(lam, near_rows, far_rows, columns, coef, masks, r, t, first, last):
@@ -325,46 +385,76 @@
     )
 
 
-def back_1_kernel(
-    local, table, coef, lam, moved_0, wind, sea, held, cells, wind_1, near_rows, far_rows, near_cols, far_cols,
-    grown, slots, masks, columns, decays, sums,
-):
-    rows, bins, _ = lam.shape
-    set_masks(sea, held, masks)
-    join_columns(near_cols, far_cols, columns)
+def set_decays(local, table, q, decays):
     for f in range(local):
         freq, _ = bin_constants(table, f, local)
-        decay = jnp.exp((-0.5 * freq) * cells[0])
+        decay = jnp.exp((-0.5 * freq) * q)
         decays[f] = (-0.5 * freq) * decay
         decays[local + f] = 0.5 * decay
-    zero = jnp.zeros((TILE, 128), F32)
+
+
+def back_row(local, coef, lam, moved_0, wind, masks, halos, columns, decays, sums, grown, r, first, last):
+    half_wind = 0.5 * row_of(wind, r)
+    for_q = [row_of(decays.at[f], r) for f in range(local)]
+    for_wind = [row_of(decays.at[local + f], r) for f in range(local)]
+    lam_q = lam_wind = jnp.zeros((TILE, 128), F32)
+    for t in range(lam.shape[1] // TILE):
+        density = back_of(lam, *halos, columns, coef, masks, r, t, first, last)
+        g = coef[GROWTH, span(t), :]
+        density = density * jnp.exp(half_wind * g)
+        grown[span(t), :] = density
+        term = density * moved_0[span(t), :]
+        lam_q = lam_q + pick(for_q, t) * term
+        lam_wind = lam_wind + pick(for_wind, t) * (g * term)
+    sums[0, tile_at(r), :] = lam_q
+    sums[1, tile_at(r), :] = lam_wind
+
+
+def inner_back_1_kernel(
+    local, table, coef, lam, moved_0, wind, sea, held, cells, near_cols, far_cols,
+    grown, parts, joined, masks, decays, sums,
+):
+    rows = lam.shape[0]
+    set_masks(sea, held, masks)
+    join_columns(near_cols, far_cols, joined)
+    set_decays(local, table, cells[0], decays)
+    clear_tiles(sums, (0, rows - 1))
 
     def body(r, first, last):
-        half_wind = 0.5 * row_of(wind, r)
-        for_q = [row_of(decays.at[f], r) for f in range(local)]
-        for_wind = [row_of(decays.at[local + f], r) for f in range(local)]
-        lam_q, lam_wind = zero, zero
-        for t in range(bins // TILE):
-            density = back_of(lam, near_rows, far_rows, columns, coef, masks, r, t, first, last)
-            g = coef[GROWTH, span(t), :]
-            density = density * jnp.exp(half_wind * g)
-            grown[r, span(t), :] = density
-            term = density * moved_0[r, span(t), :]
-            lam_q = lam_q + pick(for_q, t) * term
-            lam_wind = lam_wind + pick(for_wind, t) * (g * term)
-        at = r * TILE if isinstance(r, int) else pl.multiple_of(r * TILE, TILE)
-        sums[0, pl.ds(at, TILE), :] = lam_q
-        sums[1, pl.ds(at, TILE), :] = lam_wind
-
-    over_rows(rows, body)
-    lam_q, lam_wind = gathered(sums, 0), gathered(sums, 1) + wind_1[...]
+        back_row(
+            local, coef, lam, moved_0.at[r], wind, masks, (None, None), joined, decays, sums, grown.at[r], r, first, last
+        )
+
+    inner_rows(rows, body)
+    for q in range(2):
+        parts[q] = gathered(sums, q)
+
+
+def outer_back_1_kernel(
+    local, table, coef, lam, moved_0, wind, sea, held, cells, wind_1, joined, parts, near_rows, far_rows,
+    grown, slots, masks, decays, sums,
+):
+    rows = lam.shape[0]
+    set_masks(sea, held, masks)
+    set_decays(local, table, cells[0], decays)
+    clear_tiles(sums, range(1, rows - 1))
+
+    def body(r, first, last):
+        halos = near_rows, far_rows
+        i = int(last)
+        back_row(
+            local, coef, lam, moved_0.at[i], wind, masks, halos, joined, decays, sums, grown.at[i], r, first, last
+        )
+
+    outer_rows(rows, body)
+    lam_q, lam_wind = parts[0] + gathered(sums, 0), parts[1] + gathered(sums, 1) + wind_1[...]
     for peer in range(slots.shape[0]):
         slots[peer, 0] = lam_q
         slots[peer, 1] = lam_wind
 
 
 def lam_0_kernel(
-    local, table, grown, sea, held, cells, got,
+    local, table, grown, outer, sea, held, cells, got,
     lam, wind_total, near_rows, far_rows, cols, masks, decays, rests, packed,
 ):
     set_masks(sea, held, masks)
@@ -373,26 +463,34 @@
         lam_q, lam_wind = lam_q + got[peer, 0], lam_wind + got[peer, 1]
     wind_total[...] = lam_wind
     set_rates(local, table, cells[0], lam_q * cells[1], lam_q * cells[2], decays, rests)
-    lam_rows(local, grown, masks, decays, rests, lam, near_rows, far_rows, cols, packed)
-
-
-def back_0_kernel(
-    coef, lam, sea, held, near_rows, far_rows, near_cols, far_cols, out, laid, masks, columns, sent
-):
-    rows, bins, _ = lam.shape
-    set_masks(sea, held, masks)
-    join_columns(near_cols, far_cols, columns)
-    copies = [pltpu.make_async_copy(laid.at[r], out.at[:, r, :], sent.at[r]) for r in range(rows)]
-    for r in range(rows):
-        for t in range(bins // TILE):
+    lam_rows(local, grown, outer, masks, decays, rests, lam, near_rows, far_rows, cols, packed)
+
+
+def send_rows(rows, coef, lam, halos, columns, masks, out, laid, sent):
+    count = lam.shape[0]
+    copies = []
+    for r in rows:
+        for t in range(lam.shape[1] // TILE):
             laid[r, span(t), :] = back_of(
-                lam, near_rows, far_rows, columns, coef, masks, r, t, r == 0, r == rows - 1
+                lam, *halos, columns, coef, masks, r, t, r == 0, r == count - 1
             )
-        copies[r].start()
+        copies.append(pltpu.make_async_copy(laid.at[r], out.at[:, r, :], sent.at[r]))
+        copies[-1].start()
     for copy in copies:
         copy.wait()
 
 
+def inner_back_0_kernel(coef, lam, sea, held, near_cols, far_cols, out, joined, laid, masks, sent):
+    set_masks(sea, held, masks)
+    join_columns(near_cols, far_cols, joined)
+    send_rows(range(1, lam.shape[0] - 1), coef, lam, (None, None), joined, masks, out, laid, sent)
+
+
+def outer_back_0_kernel(coef, lam, sea, held, joined, near_rows, far_rows, inner, out, laid, masks, sent):
+    set_masks(sea, held, masks)
+    send_rows((0, lam.shape[0] - 1), coef, lam, (near_rows, far_rows), joined, masks, out, laid, sent)
+
+
 def swap(near, far, axis):
     count = lax.axis_size(axis)
 
@@ -403,16 +501,18 @@
 
 
 def exchange(near_rows, far_rows, cols):
-    return *swap(near_rows, far_rows, "gx"), *swap(cols, cols, "gy")
-
-
-def call(body, outs, specs, *args, out_specs=None, scratch=(), us=2, mib=40):
+    from_columns = swap(cols, cols, "gy")
+    return from_columns, swap(near_rows, far_rows, "gx")
+
+
+def call(body, outs, specs, *args, out_specs=None, scratch=(), us=2, mib=40, aliases=None):
     return pl.pallas_call(
         body,
         out_shape=[jax.ShapeDtypeStruct(shape, F32) for shape in outs],
         in_specs=specs,
         out_specs=out_specs or [VMEM] * len(outs),
         scratch_shapes=list(scratch),
+        input_output_aliases=aliases or {},
         cost_estimate=pl.CostEstimate(flops=us * 1000000, bytes_accessed=us * 1000000, transcendentals=0),
         compiler_params=pltpu.CompilerParams(vmem_limit_bytes=mib * 1024 * 1024),
     )(*args)
@@ -420,21 +520,6 @@
 
 def scratch(*shape):
     return pltpu.VMEM(shape, F32)
-
-
-def coefficients(growth, speed, code):
-    x, y = speed[0], speed[1]
-    next_x, next_y = code % 2 == 1, code // 2 == 1
-    values = [
-        1.0 - x - y,
-        jnp.where(next_x, 0.0, x),
-        jnp.where(next_x, x, 0.0),
-        jnp.where(next_y, 0.0, y),
-        jnp.where(next_y, y, 0.0),
-        growth,
-    ]
-    values = jnp.stack(values).reshape(len(values), -1, 1)
-    return jnp.broadcast_to(values, values.shape[:2] + (128,))
 
 
 def shards(trajectory, adjoint_seed, wind, growth, speed, code, sea, held):
@@ -446,8 +531,10 @@
 
     rows, cols, whole, cell = (bins, ny), (groups, TILE, ny), (nx, bins, ny), (nx, ny)
     edges = [rows, rows, cols]
-    masks, columns = scratch(2, *cell), scratch(*cols)
+    masks = scratch(2, *cell)
     decays, rests, packed = scratch(local, *cell), scratch(local, *cell), scratch(*cols)
+
+    sems, tiles = pltpu.SemaphoreType.DMA((nx,)), nx * TILE
 
     laid, *edge = call(
         edges_kernel,
@@ -455,23 +542,29 @@
         [HBM],
         trajectory.reshape(steps, bins, nx, ny),
         scratch=[pltpu.SemaphoreType.DMA((steps, nx))],
-        mib=40,
-    )
-    coef = coefficients(growth, speed, code)
-    (grown,) = call(
-        seed_kernel,
-        [whole],
-        [HBM, VMEM, VMEM],
-        adjoint_seed.reshape(bins, nx, ny), coef, wind,
-        scratch=[scratch(*whole), pltpu.SemaphoreType.DMA((nx,))],
-    )
-    halos = exchange(*edge)
-    slots, wind_parts, moved_0 = call(
-        functools.partial(forward_kernel, local),
-        [(peers, 4 + local) + cell, (local,) + cell, whole],
+    )
+    coef, grown = call(
+        functools.partial(prepare_kernel, local),
+        [(6,) + rows, whole],
+        [SMEM] * 3 + [HBM, VMEM],
+        growth, speed, code, adjoint_seed.reshape(bins, nx, ny), wind,
+        scratch=[scratch(*whole), sems],
+    )
+    from_columns, from_rows = exchange(*edge)
+    parts, moved_0, joined = call(
+        functools.partial(inner_forward_kernel, local),
+        [(4 * local,) + cell, whole, (steps,) + cols],
+        [VMEM] * 7,
+        coef, laid, grown, sea, held, *from_columns,
+        scratch=[masks, scratch(4 * local, tiles, ny)],
+        us=4,
+    )
+    slots, wind_parts, outer_moved_0 = call(
+        functools.partial(outer_forward_kernel, local),
+        [(peers, 4 + local) + cell, (local,) + cell, (2,) + rows],
         [SMEM] + [VMEM] * 9,
-        table, coef, laid, grown, sea, held, *halos,
-        scratch=[masks, scratch(steps, *cols), scratch(4 * local, nx * TILE, ny)],
+        table, coef, laid, grown, sea, held, joined, parts, *from_rows,
+        scratch=[masks, scratch(4 * local, tiles, ny)],
     )
     got = lax.all_to_all(slots, "sa", 0, 0)
     lam, wind_1, cells, *edge = call(
@@ -481,30 +574,48 @@
         table, grown, sea, held, got, wind_parts,
         scratch=[masks, decays, rests, packed],
     )
-    halos = exchange(*edge)
-    grown, slots = call(
-        functools.partial(back_1_kernel, local),
-        [whole, (peers, 2) + cell],
+    from_columns, from_rows = exchange(*edge)
+    grown, parts, joined = call(
+        functools.partial(inner_back_1_kernel, local),
+        [whole, (2,) + cell, cols],
+        [SMEM] + [VMEM] * 9,
+        table, coef, lam, moved_0, wind, sea, held, cells, *from_columns,
+        scratch=[masks, scratch(2 * local, *cell), scratch(2, tiles, ny)],
+        us=4,
+    )
+    outer, slots = call(
+        functools.partial(outer_back_1_kernel, local),
+        [(2,) + rows, (peers, 2) + cell],
         [SMEM] + [VMEM] * 12,
-        table, coef, lam, moved_0, wind, sea, held, cells, wind_1, *halos,
-        scratch=[masks, columns, scratch(2 * local, *cell), scratch(2, nx * TILE, ny)],
+        table, coef, lam, outer_moved_0, wind, sea, held, cells, wind_1, joined, parts, *from_rows,
+        scratch=[masks, scratch(2 * local, *cell), scratch(2, tiles, ny)],
     )
     got = lax.all_to_all(slots, "sa", 0, 0)
     lam, wind_total, *edge = call(
         functools.partial(lam_0_kernel, local),
         [whole, cell] + edges,
-        [SMEM] + [VMEM] * 5,
-        table, grown, sea, held, cells, got,
+        [SMEM] + [VMEM] * 6,
+        table, grown, outer, sea, held, cells, got,
         scratch=[masks, decays, rests, packed],
     )
-    halos = exchange(*edge)
+    from_columns, from_rows = exchange(*edge)
+    inner, joined = call(
+        inner_back_0_kernel,
+        [(bins, nx, ny), cols],
+        [VMEM] * 6,
+        coef, lam, sea, held, *from_columns,
+        out_specs=[HBM, VMEM],
+        scratch=[scratch(*whole), masks, sems],
+        us=4,
+    )
     (out,) = call(
-        back_0_kernel,
+        outer_back_0_kernel,
         [(bins, nx, ny)],
-        [VMEM] * 8,
-        coef, lam, sea, held, *halos,
+        [VMEM] * 7 + [HBM],
+        coef, lam, sea, held, joined, *from_rows, inner,
         out_specs=[HBM],
-        scratch=[scratch(*whole), masks, columns, pltpu.SemaphoreType.DMA((nx,))],
+        scratch=[scratch(*whole), masks, sems],
+        aliases={7: 0},
     )
     return out.reshape(local, dirs, nx, ny), wind_total
 

time: 112 us -> 102 us (0.911)
  local copies, waits for them, and re-layouts: 9.24 us -> 1.7 us
  other arithmetic: 1.76 us -> 0 us
    another operation x7 -> x0, local copies, waits for them, and re-layouts: 7.38 us -> none  [coefficients(): values = jnp.stack(values).reshape(len(values), -1, 1)]
    select_n x2 -> x0, other arithmetic: 1.18 us -> none  [the longest x1 0.6 us: coefficients(): jnp.where(next_y, y, 0.0)]
    pallas_call x7 -> x10, Pallas kernels: 20.3 us -> 20.5 us  [call(): pl.pallas_call(body, out_shape=[jax.ShapeDtypeStruct(shape, F32) for shap...]
  transfers between devices with their start and end apart: 12 -> 12, of which waited for: 2 -> 2; matrix products, arithmetic and copies ran while one was open for 8% -> 0% of each run, Pallas kernels for 1% -> 10%
where the time goes in v2:
time: 102 us
  starting transfers between devices  39.3 us (39%)
  blocking collectives  37.1 us (36%)
  Pallas kernels  20.5 us (20%)
  waiting for transfers between devices  2.32 us (2%)
  local copies, waits for them, and re-layouts  1.7 us (2%)
    all_to_all x2, blocking collectives, shards(): got = lax.all_to_all(slots, 'sa', 0, 0)  37.1 us
    ppermute x6, starting transfers between devices, swap(): lax.ppermute(far, axis, pairs(1))  25 us
    pallas_call x10, Pallas kernels, call(): pl.pallas_call(body, out_shape=[jax.ShapeDtypeStruct(shape, F32) for shap...  20.5 us
    ppermute x6, starting transfers between devices, swap(): lax.ppermute(near, axis, pairs(0))  14.3 us
    ppermute x6, waiting for transfers between devices, swap(): lax.ppermute(near, axis, pairs(0))  2.27 us
  transfers between devices with their start and end apart: 12, of which 2 were waited for; matrix products, arithmetic and copies ran while one was open for 0% of the time, Pallas kernels for 10%

profile of v2, /device:TPU:57, one launch (start us, length us, event | category | flops | bytes accessed | tf_op | source)
XLA Modules:
  0.0 101.9 jit_solution(11212007397216364888)
XLA Ops:
  0.6 0.0 copy-start
  0.6 1.7 %copy-done = f32[2,4,36,16,128]{4,3,2,1,0:T(8,128)S(1)} copy-done((f32[2,4,36,16,128]{4,3,2,1,0:T(8,128)S(1)}, f32[2,4,36,16,128]{4,3,2,1,0:T(8,128)}, u32[]{:S(2)}) %copy-start) | copy-done | bytes 2359320
  2.3 0.0 copy-start.1
  2.3 0.0 copy-start.4
  2.3 0.0 copy-start.6
  2.3 0.0 copy-start.7
  2.3 0.0 copy-start.8
  2.3 2.8 %shard_map.105 = (f32[2,16,144,128]{3,2,1,0:T(8,128)S(1)}, f32[2,144,128]{2,1,0:T(8,128)S(1)}, f32[2,144,128]{2,1,0:T(8,128)S(1)}, f32[2,5,8,128]{3,2,1,0:T(8,128)S(1)}) custom-call(f32[2,144,16,128]{3,2,1,0:T(8,128)S(1)} %bitcast.3), custom_call_target="tpu_custom_call" | custom-call | flops 2000000 | bytes 2000000 | tf_op jit(solution)/shard_map/pallas_call | solution.py:509
  5.2 0.0 copy-start.2
  5.2 0.0 copy-start.3
  5.2 3.0 %collective-permute-start.2 = (f32[2,144,128]{2,1,0:T(8,128)S(1)}, f32[2,144,128]{2,1,0:T(8,128)S(1)}, u32[]{:S(2)}, u32[]{:S(2)}) collective-permute-start(f32[2,144,128]{2,1,0:T(8,128)S(1)} %get-tuple-element.38), channel_id=1, source_target_pairs={{0,32},{32,0},{64,96},{96,64},{128,160},{160,128},{192,224},{224,1... | collective-permute-start | bytes 442376 | tf_op jit(solution)/shard_map/ppermute | solution.py:500
  8.2 2.6 %collective-permute-start.3 = (f32[2,144,128]{2,1,0:T(8,128)S(1)}, f32[2,144,128]{2,1,0:T(8,128)S(1)}, u32[]{:S(2)}, u32[]{:S(2)}) collective-permute-start(f32[2,144,128]{2,1,0:T(8,128)S(1)} %get-tuple-element.39), channel_id=1, source_target_pairs={{32,64},{64,32},{96,128},{128,96},{160,192},{192,160},{224,256},{2... | collective-permute-start | bytes 442376 | tf_op jit(solution)/shard_map/ppermute | solution.py:500
  10.7 5.5 %collective-permute-start.1 = (f32[2,5,8,128]{3,2,1,0:T(8,128)S(1)}, f32[2,5,8,128]{3,2,1,0:T(8,128)S(1)}, u32[]{:S(2)}, u32[]{:S(2)}) collective-permute-start(f32[2,5,8,128]{3,2,1,0:T(8,128)S(1)} %get-tuple-element.35), channel_id=1, source_target_pairs={{8,16},{16,8},{9,17},{17,9},{10,18},{18,10},{11,19},{19,11},{12,20... | collective-permute-start | bytes 122888 | tf_op jit(solution)/shard_map/ppermute | solution.py:500
  16.2 1.9 %collective-permute-start = (f32[2,5,8,128]{3,2,1,0:T(8,128)S(1)}, f32[2,5,8,128]{3,2,1,0:T(8,128)S(1)}, u32[]{:S(2)}, u32[]{:S(2)}) collective-permute-start(f32[2,5,8,128]{3,2,1,0:T(8,128)S(1)} %get-tuple-element.35), channel_id=1, source_target_pairs={{0,8},{8,0},{16,24},{24,16},{1,9},{9,1},{17,25},{25,17},{2,10},{10... | collective-permute-start | bytes 122888 | tf_op jit(solution)/shard_map/ppermute | solution.py:500
  18.2 0.0 copy-done.1
  18.2 0.0 copy-done.4
  18.2 0.0 copy-done.6
  18.2 0.0 copy-done.7
  18.2 0.0 copy-done.8
  18.2 2.9 %shard_map.104 = (f32[6,144,128]{2,1,0:T(8,128)S(1)}, f32[16,144,128]{2,1,0:T(8,128)S(1)}) custom-call(f32[4,36]{1,0:T(4,128)S(1)} %copy-done.7, f32[2,4,36]{2,1,0:T(4,128)S(1)} %copy-done.6, s32[4,36]{1,0:T(4,128)S(1)} %copy-done.8, f32[144,16,128]{2,1,0:T(8,128)S(1)} %bitcast.4, f32[16,128]{1,0:T(8,128)S(1)} %copy-done.4), custom_call_target="tpu_custom_call" | custom-call | flops 2000000 | bytes 2000000 | tf_op jit(solution)/shard_map/pallas_call | solution.py:509
  21.1 0.0 collective-permute-done.1.far_cols
  21.1 0.0 collective-permute-done.near_cols
  21.2 0.0 copy-done.2
  21.2 0.0 copy-done.3
  21.2 0.0 copy-start.5
  21.2 3.0 %shard_map.106 = (f32[16,16,128]{2,1,0:T(8,128)S(1)}, f32[16,144,128]{2,1,0:T(8,128)S(1)}, f32[2,5,8,128]{3,2,1,0:T(8,128)S(1)}) custom-call(f32[6,144,128]{2,1,0:T(8,128)S(1)} %get-tuple-element.32.coef, f32[2,16,144,128]{3,2,1,0:T(8,128)S(1)} %get-tuple-element.34.laid, f32[16,144,128]{2,1,0:T(8,128)S(1)} %get-tuple-element.33.grown, ...), custom_call_target="tpu_custom_call" | custom-call | flops 4000000 | bytes 4000000 | tf_op jit(solution)/shard_map/pallas_call | solution.py:509
  24.2 0.0 collective-permute-done.2.near_rows
  24.2 0.0 collective-permute-done.3.far_rows
  24.2 0.0 copy-done.5
  24.2 1.0 shard_map.107
  25.2 26.2 %all_to_all.10.got = f32[8,8,16,128]{3,2,1,0:T(8,128)S(1)} all-to-all(f32[8,8,16,128]{3,2,1,0:T(8,128)S(1)} %get-tuple-element.40), channel_id=1, replica_groups=mesh['gx'=16,'gy'=4,'sa'=8] {'sa'}, dimensions={0} | all-to-all | bytes 1048576 | tf_op jit(solution)/shard_map/all_to_all | solution.py:569
  51.4 2.0 %shard_map.108 = (f32[16,144,128]{2,1,0:T(8,128)S(1)}, f32[16,128]{1,0:T(8,128)S(1)}, f32[3,16,128]{2,1,0:T(8,128)S(1)}, f32[144,128]{1,0:T(8,128)S(1)}, f32[144...) custom-call(f32[2,32]{1,0:T(2,128)S(1)} %copy-done.5, f32[16,144,128]{2,1,0:T(8,128)S(1)} %get-tuple-element.33.grown, ...), custom_call_target="tpu_custom_call" | custom-call | flops 2000000 | bytes 2000000 | tf_op jit(solution)/shard_map/pallas_call | solution.py:509
  53.4 3.7 %collective-permute-start.6 = (f32[144,128]{1,0:T(8,128)S(1)}, f32[144,128]{1,0:T(8,128)S(1)}, u32[]{:S(2)}, u32[]{:S(2)}) collective-permute-start(f32[144,128]{1,0:T(8,128)S(1)} %get-tuple-element.51), channel_id=1, source_target_pairs={{0,32},{32,0},{64,96},{96,64},{128,160},{160,128},{192,224},{224,1... | collective-permute-start | bytes 221192 | tf_op jit(solution)/shard_map/ppermute | solution.py:500
  57.1 2.8 %collective-permute-start.7 = (f32[144,128]{1,0:T(8,128)S(1)}, f32[144,128]{1,0:T(8,128)S(1)}, u32[]{:S(2)}, u32[]{:S(2)}) collective-permute-start(f32[144,128]{1,0:T(8,128)S(1)} %get-tuple-element.52), channel_id=1, source_target_pairs={{32,64},{64,32},{96,128},{128,96},{160,192},{192,160},{224,256},{2... | collective-permute-start | bytes 221192 | tf_op jit(solution)/shard_map/ppermute | solution.py:500
  59.9 4.9 %collective-permute-start.5 = (f32[5,8,128]{2,1,0:T(8,128)S(1)}, f32[5,8,128]{2,1,0:T(8,128)S(1)}, u32[]{:S(2)}, u32[]{:S(2)}) collective-permute-start(f32[5,8,128]{2,1,0:T(8,128)S(1)} %get-tuple-element.45), channel_id=1, source_target_pairs={{8,16},{16,8},{9,17},{17,9},{10,18},{18,10},{11,19},{19,11},{12,20... | collective-permute-start | bytes 61448 | tf_op jit(solution)/shard_map/ppermute | solution.py:500
  64.8 1.9 %collective-permute-start.4 = (f32[5,8,128]{2,1,0:T(8,128)S(1)}, f32[5,8,128]{2,1,0:T(8,128)S(1)}, u32[]{:S(2)}, u32[]{:S(2)}) collective-permute-start(f32[5,8,128]{2,1,0:T(8,128)S(1)} %get-tuple-element.45), channel_id=1, source_target_pairs={{0,8},{8,0},{16,24},{24,16},{1,9},{9,1},{17,25},{25,17},{2,10},{10... | collective-permute-start | bytes 61448 | tf_op jit(solution)/shard_map/ppermute | solution.py:500
  66.8 0.0 collective-permute-done.5.far_cols
  66.8 1.1 %collective-permute-done.4.near_cols = f32[5,8,128]{2,1,0:T(8,128)S(1)} collective-permute-done((f32[5,8,128]{2,1,0:T(8,128)S(1)}, f32[5,8,128]{2,1,0:T(8,128)S(1)}, u32[]{:S(2)}, u32[]{:S(2)}) %collective-permute-start.4) | collective-permute-done | bytes 20512 | tf_op jit(solution)/shard_map/ppermute | solution.py:500
  67.9 2.6 %shard_map.109 = (f32[16,144,128]{2,1,0:T(8,128)S(1)}, f32[2,16,128]{2,1,0:T(8,128)S(1)}, f32[5,8,128]{2,1,0:T(8,128)S(1)}) custom-call(f32[2,32]{1,0:T(2,128)S(1)} %copy-done.5, f32[6,144,128]{2,1,0:T(8,128)S(1)} %get-tuple-element.32.coef, f32[16,144,128]{2,1,0:T(8,128)S(1)} %get-tuple-element.42.lam, f32[16,144,128]{2,1,0:T(8,128)S(1)} %get-tuple-element.43.moved_0, ...), custom_call_target="tpu_custom_call" | custom-call | flops 4000000 | bytes 4000000 | tf_op jit(solution)/shard_map/pallas_call | solution.py:509
  70.6 0.0 collective-permute-done.6.near_rows
  70.6 0.0 collective-permute-done.7.far_rows
  70.6 0.8 shard_map.110
  71.4 11.0 %all_to_all.11.got = f32[8,2,16,128]{3,2,1,0:T(8,128)S(1)} all-to-all(f32[8,2,16,128]{3,2,1,0:T(8,128)S(1)} %get-tuple-element.54), channel_id=1, replica_groups=mesh['gx'=16,'gy'=4,'sa'=8] {'sa'}, dimensions={0} | all-to-all | bytes 262144 | tf_op jit(solution)/shard_map/all_to_all | solution.py:593
  82.4 2.5 %shard_map.111 = (f32[16,144,128]{2,1,0:T(8,128)S(1)}, f32[16,128]{1,0:T(8,128)}, f32[144,128]{1,0:T(8,128)S(1)}, f32[144,128]{1,0:T(8,128)S(1)}, f32[5,8,128]{2,1,0:T(8,128)S(1)}) custom-call(f32[2,32]{1,0:T(2,128)S(1)} %copy-done.5, f32[16,144,128]{2,1,0:T(8,128)S(1)} %get-tuple-element.46.grown, f32[2,144,128]{2,1,0:T(8,128)S(1)} %get-tuple-element.53.outer, ...), custom_call_target="tpu_custom_call" | custom-call | flops 2000000 | bytes 2000000 | tf_op jit(solution)/shard_map/pallas_call | solution.py:509
  84.9 1.9 %collective-permute-start.10 = (f32[144,128]{1,0:T(8,128)S(1)}, f32[144,128]{1,0:T(8,128)S(1)}, u32[]{:S(2)}, u32[]{:S(2)}) collective-permute-start(f32[144,128]{1,0:T(8,128)S(1)} %get-tuple-element.58), channel_id=1, source_target_pairs={{0,32},{32,0},{64,96},{96,64},{128,160},{160,128},{192,224},{224,1... | collective-permute-start | bytes 221192 | tf_op jit(solution)/shard_map/ppermute | solution.py:500
  86.8 4.1 %collective-permute-start.11 = (f32[144,128]{1,0:T(8,128)S(1)}, f32[144,128]{1,0:T(8,128)S(1)}, u32[]{:S(2)}, u32[]{:S(2)}) collective-permute-start(f32[144,128]{1,0:T(8,128)S(1)} %get-tuple-element.59), channel_id=1, source_target_pairs={{32,64},{64,32},{96,128},{128,96},{160,192},{192,160},{224,256},{2... | collective-permute-start | bytes 221192 | tf_op jit(solution)/shard_map/ppermute | solution.py:500
  90.9 5.1 %collective-permute-start.9 = (f32[5,8,128]{2,1,0:T(8,128)S(1)}, f32[5,8,128]{2,1,0:T(8,128)S(1)}, u32[]{:S(2)}, u32[]{:S(2)}) collective-permute-start(f32[5,8,128]{2,1,0:T(8,128)S(1)} %get-tuple-element.56), channel_id=1, source_target_pairs={{8,16},{16,8},{9,17},{17,9},{10,18},{18,10},{11,19},{19,11},{12,20... | collective-permute-start | bytes 61448 | tf_op jit(solution)/shard_map/ppermute | solution.py:500
  96.1 1.9 %collective-permute-start.8 = (f32[5,8,128]{2,1,0:T(8,128)S(1)}, f32[5,8,128]{2,1,0:T(8,128)S(1)}, u32[]{:S(2)}, u32[]{:S(2)}) collective-permute-start(f32[5,8,128]{2,1,0:T(8,128)S(1)} %get-tuple-element.56), channel_id=1, source_target_pairs={{0,8},{8,0},{16,24},{24,16},{1,9},{9,1},{17,25},{25,17},{2,10},{10... | collective-permute-start | bytes 61448 | tf_op jit(solution)/shard_map/ppermute | solution.py:500
  98.0 0.0 collective-permute-done.9.far_cols
  98.0 1.1 %collective-permute-done.8.near_cols = f32[5,8,128]{2,1,0:T(8,128)S(1)} collective-permute-done((f32[5,8,128]{2,1,0:T(8,128)S(1)}, f32[5,8,128]{2,1,0:T(8,128)S(1)}, u32[]{:S(2)}, u32[]{:S(2)}) %collective-permute-start.8) | collective-permute-done | bytes 20512 | tf_op jit(solution)/shard_map/ppermute | solution.py:500
  99.2 1.8 %shard_map.112 = (f32[144,16,128]{2,1,0:T(8,128)}, f32[5,8,128]{2,1,0:T(8,128)S(1)}) custom-call(f32[6,144,128]{2,1,0:T(8,128)S(1)} %get-tuple-element.32.coef, f32[16,144,128]{2,1,0:T(8,128)S(1)} %get-tuple-element.55.lam, s32[16,128]{1,0:T(8,128)S(1)} %copy-done.2, s32[16,128]{1,0:T(8,128)S(1)} %copy-done.3, ...), custom_call_target="tpu_custom_call" | custom-call | flops 4000000 | bytes 4000000 | tf_op jit(solution)/shard_map/pallas_call | solution.py:509
  100.9 0.0 collective-permute-done.10.near_rows
  100.9 0.0 collective-permute-done.11.far_rows
  101.0 1.0 shard_map.113
Async XLA Ops:
  0.6 1.7 %copy-start = (f32[2,4,36,16,128]{4,3,2,1,0:T(8,128)S(1)}, f32[2,4,36,16,128]{4,3,2,1,0:T(8,128)}, u32[]{:S(2)}) copy-start(f32[2,4,36,16,128]{4,3,2,1,0:T(8,128)} %param.9) | copy-start | bytes 7077892
  2.3 15.9 %copy-start.1 = (f32[4,36,16,128]{3,2,1,0:T(8,128)S(1)}, f32[4,36,16,128]{3,2,1,0:T(8,128)}, u32[]{:S(2)}) copy-start(f32[4,36,16,128]{3,2,1,0:T(8,128)} %param.10) | copy-start | bytes 3538948
  2.3 15.9 %copy-start.4 = (f32[16,128]{1,0:T(8,128)S(1)}, f32[16,128]{1,0:T(8,128)}, u32[]{:S(2)}) copy-start(f32[16,128]{1,0:T(8,128)} %wind.5) | copy-start | bytes 24580
  2.3 15.9 %copy-start.6 = (f32[2,4,36]{2,1,0:T(4,128)S(1)}, f32[2,4,36]{2,1,0:T(4,128)}, u32[]{:S(2)}) copy-start(f32[2,4,36]{2,1,0:T(4,128)} %speed.1) | copy-start | bytes 3460
  2.3 15.9 %copy-start.7 = (f32[4,36]{1,0:T(4,128)S(1)}, f32[4,36]{1,0:T(4,128)}, u32[]{:S(2)}) copy-start(f32[4,36]{1,0:T(4,128)} %growth.1) | copy-start | bytes 1732
  2.3 15.9 %copy-start.8 = (s32[4,36]{1,0:T(4,128)S(1)}, s32[4,36]{1,0:T(4,128)}, u32[]{:S(2)}) copy-start(s32[4,36]{1,0:T(4,128)} %code.1) | copy-start | bytes 1732
  5.2 16.0 %copy-start.2 = (s32[16,128]{1,0:T(8,128)S(1)}, s32[16,128]{1,0:T(8,128)}, u32[]{:S(2)}) copy-start(s32[16,128]{1,0:T(8,128)} %sea.15) | copy-start | bytes 24580
  5.2 16.0 %copy-start.3 = (s32[16,128]{1,0:T(8,128)S(1)}, s32[16,128]{1,0:T(8,128)}, u32[]{:S(2)}) copy-start(s32[16,128]{1,0:T(8,128)} %held.15) | copy-start | bytes 24580
  5.2 19.0 %collective-permute-start.2 = (f32[2,144,128]{2,1,0:T(8,128)S(1)}, f32[2,144,128]{2,1,0:T(8,128)S(1)}, u32[]{:S(2)}, u32[]{:S(2)}) collective-permute-start(f32[2,144,128]{2,1,0:T(8,128)S(1)} %get-tuple-element.38), channel_id=1, source_target_pairs={{0,32},{32,0},{64,96},{96,64},{128,160},{160,128},{192,224},{224,1... | collective-permute-start | bytes 442376 | tf_op jit(solution)/shard_map/ppermute | solution.py:500
  8.2 16.0 %collective-permute-start.3 = (f32[2,144,128]{2,1,0:T(8,128)S(1)}, f32[2,144,128]{2,1,0:T(8,128)S(1)}, u32[]{:S(2)}, u32[]{:S(2)}) collective-permute-start(f32[2,144,128]{2,1,0:T(8,128)S(1)} %get-tuple-element.39), channel_id=1, source_target_pairs={{32,64},{64,32},{96,128},{128,96},{160,192},{192,160},{224,256},{2... | collective-permute-start | bytes 442376 | tf_op jit(solution)/shard_map/ppermute | solution.py:500
  10.7 10.4 %collective-permute-start.1 = (f32[2,5,8,128]{3,2,1,0:T(8,128)S(1)}, f32[2,5,8,128]{3,2,1,0:T(8,128)S(1)}, u32[]{:S(2)}, u32[]{:S(2)}) collective-permute-start(f32[2,5,8,128]{3,2,1,0:T(8,128)S(1)} %get-tuple-element.35), channel_id=1, source_target_pairs={{8,16},{16,8},{9,17},{17,9},{10,18},{18,10},{11,19},{19,11},{12,20... | collective-permute-start | bytes 122888 | tf_op jit(solution)/shard_map/ppermute | solution.py:500
  16.2 4.9 %collective-permute-start = (f32[2,5,8,128]{3,2,1,0:T(8,128)S(1)}, f32[2,5,8,128]{3,2,1,0:T(8,128)S(1)}, u32[]{:S(2)}, u32[]{:S(2)}) collective-permute-start(f32[2,5,8,128]{3,2,1,0:T(8,128)S(1)} %get-tuple-element.35), channel_id=1, source_target_pairs={{0,8},{8,0},{16,24},{24,16},{1,9},{9,1},{17,25},{25,17},{2,10},{10... | collective-permute-start | bytes 122888 | tf_op jit(solution)/shard_map/ppermute | solution.py:500
  21.2 3.0 %copy-start.5 = (f32[2,32]{1,0:T(2,128)S(1)}, f32[2,32]{1,0:T(2,128)}, u32[]{:S(2)}) copy-start(f32[2,32]{1,0:T(2,128)} %constant.2.clone.table) | copy-start | bytes 772
  53.4 17.1 %collective-permute-start.6 = (f32[144,128]{1,0:T(8,128)S(1)}, f32[144,128]{1,0:T(8,128)S(1)}, u32[]{:S(2)}, u32[]{:S(2)}) collective-permute-start(f32[144,128]{1,0:T(8,128)S(1)} %get-tuple-element.51), channel_id=1, source_target_pairs={{0,32},{32,0},{64,96},{96,64},{128,160},{160,128},{192,224},{224,1... | collective-permute-start | bytes 221192 | tf_op jit(solution)/shard_map/ppermute | solution.py:500
  57.1 13.4 %collective-permute-start.7 = (f32[144,128]{1,0:T(8,128)S(1)}, f32[144,128]{1,0:T(8,128)S(1)}, u32[]{:S(2)}, u32[]{:S(2)}) collective-permute-start(f32[144,128]{1,0:T(8,128)S(1)} %get-tuple-element.52), channel_id=1, source_target_pairs={{32,64},{64,32},{96,128},{128,96},{160,192},{192,160},{224,256},{2... | collective-permute-start | bytes 221192 | tf_op jit(solution)/shard_map/ppermute | solution.py:500
  59.9 6.9 %collective-permute-start.5 = (f32[5,8,128]{2,1,0:T(8,128)S(1)}, f32[5,8,128]{2,1,0:T(8,128)S(1)}, u32[]{:S(2)}, u32[]{:S(2)}) collective-permute-start(f32[5,8,128]{2,1,0:T(8,128)S(1)} %get-tuple-element.45), channel_id=1, source_target_pairs={{8,16},{16,8},{9,17},{17,9},{10,18},{18,10},{11,19},{19,11},{12,20... | collective-permute-start | bytes 61448 | tf_op jit(solution)/shard_map/ppermute | solution.py:500
  64.8 3.1 %collective-permute-start.4 = (f32[5,8,128]{2,1,0:T(8,128)S(1)}, f32[5,8,128]{2,1,0:T(8,128)S(1)}, u32[]{:S(2)}, u32[]{:S(2)}) collective-permute-start(f32[5,8,128]{2,1,0:T(8,128)S(1)} %get-tuple-element.45), channel_id=1, source_target_pairs={{0,8},{8,0},{16,24},{24,16},{1,9},{9,1},{17,25},{25,17},{2,10},{10... | collective-permute-start | bytes 61448 | tf_op jit(solution)/shard_map/ppermute | solution.py:500
  84.9 16.0 %collective-permute-start.10 = (f32[144,128]{1,0:T(8,128)S(1)}, f32[144,128]{1,0:T(8,128)S(1)}, u32[]{:S(2)}, u32[]{:S(2)}) collective-permute-start(f32[144,128]{1,0:T(8,128)S(1)} %get-tuple-element.58), channel_id=1, source_target_pairs={{0,32},{32,0},{64,96},{96,64},{128,160},{160,128},{192,224},{224,1... | collective-permute-start | bytes 221192 | tf_op jit(solution)/shard_map/ppermute | solution.py:500
  86.8 14.1 %collective-permute-start.11 = (f32[144,128]{1,0:T(8,128)S(1)}, f32[144,128]{1,0:T(8,128)S(1)}, u32[]{:S(2)}, u32[]{:S(2)}) collective-permute-start(f32[144,128]{1,0:T(8,128)S(1)} %get-tuple-element.59), channel_id=1, source_target_pairs={{32,64},{64,32},{96,128},{128,96},{160,192},{192,160},{224,256},{2... | collective-permute-start | bytes 221192 | tf_op jit(solution)/shard_map/ppermute | solution.py:500
  90.9 7.1 %collective-permute-start.9 = (f32[5,8,128]{2,1,0:T(8,128)S(1)}, f32[5,8,128]{2,1,0:T(8,128)S(1)}, u32[]{:S(2)}, u32[]{:S(2)}) collective-permute-start(f32[5,8,128]{2,1,0:T(8,128)S(1)} %get-tuple-element.56), channel_id=1, source_target_pairs={{8,16},{16,8},{9,17},{17,9},{10,18},{18,10},{11,19},{19,11},{12,20... | collective-permute-start | bytes 61448 | tf_op jit(solution)/shard_map/ppermute | solution.py:500
  96.1 3.1 %collective-permute-start.8 = (f32[5,8,128]{2,1,0:T(8,128)S(1)}, f32[5,8,128]{2,1,0:T(8,128)S(1)}, u32[]{:S(2)}, u32[]{:S(2)}) collective-permute-start(f32[5,8,128]{2,1,0:T(8,128)S(1)} %get-tuple-element.56), channel_id=1, source_target_pairs={{0,8},{8,0},{16,24},{24,16},{1,9},{9,1},{17,25},{25,17},{2,10},{10... | collective-permute-start | bytes 61448 | tf_op jit(solution)/shard_map/ppermute | solution.py:500

commit v3 on v2

--- a/solution.py
+++ b/solution.py
@@ -71,11 +71,12 @@
 
 
 def inner_rows(count, body):
-    def inner(r, carry):
-        body(r, False, False)
+    def pair(i, carry):
+        body(2 * i + 1, False, False)
+        body(2 * i + 2, False, False)
         return carry
 
-    lax.fori_loop(1, count - 1, inner, 0)
+    lax.fori_loop(0, (count - 2) // 2, pair, 0)
 
 
 def outer_rows(count, body):
@@ -230,7 +231,7 @@
     parts = [[jnp.zeros((TILE, 128), F32)] * local for _ in range(4)]
     for t in range(bins // TILE):
         early, later = (
-            moved_of(laid.at[s], *(h if h is None else h.at[s] for h in halos), columns.at[s], coef, s1, s2, r, t, first, last)
+            moved_of(laid.at[s], *(h.at[s] for h in halos), columns.at[s], coef, s1, s2, r, t, first, last)
             for s in range(2)
         )
         moved_0[span(t), :] = early
@@ -243,51 +244,29 @@
             sums[i * local + f, tile_at(r), :] = part[f]
 
 
-def clear_tiles(sums, rows):
-    for q in range(sums.shape[0]):
-        for r in rows:
-            sums[q, tile_at(r), :] = jnp.zeros((TILE, 128), F32)
-
-
-def inner_forward_kernel(
-    local, coef, laid, grown, sea, held, near_cols, far_cols, parts, moved_0, joined, masks, sums
+def forward_kernel(
+    local, table, coef, laid, grown, sea, held, near_cols, far_cols, near_rows, far_rows,
+    slots, wind_parts, moved_0, joined, masks, sums,
 ):
     _, rows, _, _ = laid.shape
     set_masks(sea, held, masks)
     for s in range(2):
         join_columns(near_cols.at[s], far_cols.at[s], joined.at[s])
-    clear_tiles(sums, (0, rows - 1))
-
-    def body(r, first, last):
-        forward_row(local, coef, laid, grown, masks, (None, None), joined, sums, moved_0.at[r], r, first, last)
-
-    inner_rows(rows, body)
-    for q in range(parts.shape[0]):
-        parts[q] = gathered(sums, q)
-
-
-def outer_forward_kernel(
-    local, table, coef, laid, grown, sea, held, joined, parts, near_rows, far_rows,
-    slots, wind_parts, moved_0, masks, sums,
-):
-    _, rows, _, _ = laid.shape
-    set_masks(sea, held, masks)
-    clear_tiles(sums, range(1, rows - 1))
 
     def body(r, first, last):
         halos = near_rows, far_rows
-        out = moved_0.at[int(last)]
-        forward_row(local, coef, laid, grown, masks, halos, joined, sums, out, r, first, last)
-
+        forward_row(local, coef, laid, grown, masks, halos, joined, sums, moved_0.at[r], r, first, last)
+
+    inner_rows(rows, body)
     outer_rows(rows, body)
     totals = [jnp.zeros((rows, 128), F32)] * 4
     for f in range(local):
         freq, weight = bin_constants(table, f, local)
-        later, early = (parts[i * local + f] + gathered(sums, i * local + f) for i in range(2))
+        later, early = gathered(sums, f), gathered(sums, local + f)
         terms = weight * later, weight * freq * later, weight * early, weight * freq * early
         totals = [total + term for total, term in zip(totals, terms)]
-        wind_parts[f] = parts[3 * local + f] + gathered(sums, 3 * local + f)
-    totals = totals + [parts[2 * local + f] + gathered(sums, 2 * local + f) for f in range(local)]
+        wind_parts[f] = gathered(sums, 3 * local + f)
+    totals = totals + [gathered(sums, 2 * local + f) for f in range(local)]
     for i, value in enumerate(totals):
         for peer in range(slots.shape[0]):
             slots[peer, i] = value
@@ -302,6 +281,13 @@
     return q, q / energy * (1.0 - 6.0 * inverse), q / first * (8.0 * inverse - 1.0)
 
 
+def total_of(got, i):
+    value = got[0, i]
+    for peer in range(1, got.shape[0]):
+        value = value + got[peer, i]
+    return value
+
+
 def set_rates(local, table, q, by_energy, by_first, decays, rests):
     for f in range(local):
         freq, weight = bin_constants(table, f, local)
@@ -309,7 +295,7 @@
         rests[f] = weight * by_energy + (weight * freq) * by_first
 
 
-def lam_rows(local, source, outer, masks, decays, rests, lam, near_rows, far_rows, cols, packed):
+def lam_rows(local, source, masks, decays, rests, lam, near_rows, far_rows, cols, packed):
     rows, bins, _ = lam.shape
     for g in range(packed.shape[0]):
         packed[g] = jnp.zeros((TILE, 128), F32)
@@ -320,8 +306,7 @@
         rest = [row_of(rests.at[f], r) for f in range(local)]
         columns = [packed[g] for g in range(packed.shape[0])]
         for t in range(bins // TILE):
-            known = outer[int(last), span(t), :] if outer is not None and (first or last) else source[r, span(t), :]
-            value = known * pick(decay, t) + pick(rest, t)
+            value = source[r, span(t), :] * pick(decay, t) + pick(rest, t)
             lam[r, span(t), :] = value
             flow = s1 * value
             pack_columns(columns, flow, r, t)
@@ -341,15 +326,8 @@
 ):
     peers = got.shape[0]
     set_masks(sea, held, masks)
-
-    def total(i):
-        value = got[0, i]
-        for peer in range(1, peers):
-            value = value + got[peer, i]
-        return value
-
-    q, by_energy, by_first = rates(1.0 + total(0), 1.0 + total(1))
-    cells[0], cells[1], cells[2] = rates(1.0 + total(2), 1.0 + total(3))
+    q, by_energy, by_first = rates(1.0 + total_of(got, 0), 1.0 + total_of(got, 1))
+    cells[0], cells[1], cells[2] = rates(1.0 + total_of(got, 2), 1.0 + total_of(got, 3))
     lam_q = jnp.zeros_like(q)
     for peer in range(peers):
         for f in range(local):
@@ -360,7 +338,7 @@
     for f in range(local):
         wind = wind + 0.5 * decays[f] * wind_parts[f]
     wind_1[...] = wind
-    lam_rows(local, grown, None, masks, decays, rests, lam, near_rows, far_rows, cols, packed)
+    lam_rows(local, grown, masks, decays, rests, lam, near_rows, far_rows, cols, packed)
 
 
 def back_of(lam, near_rows, far_rows, columns, coef, masks, r, t, first, last):
@@ -410,85 +388,53 @@
     sums[1, tile_at(r), :] = lam_wind
 
 
-def inner_back_1_kernel(
-    local, table, coef, lam, moved_0, wind, sea, held, cells, near_cols, far_cols,
-    grown, parts, joined, masks, decays, sums,
+def back_1_kernel(
+    local, table, coef, lam, moved_0, wind, sea, held, cells, wind_1,
+    near_cols, far_cols, near_rows, far_rows,
+    grown, slots, joined, masks, decays, sums,
 ):
     rows = lam.shape[0]
     set_masks(sea, held, masks)
     join_columns(near_cols, far_cols, joined)
     set_decays(local, table, cells[0], decays)
-    clear_tiles(sums, (0, rows - 1))
 
     def body(r, first, last):
-        back_row(
-            local, coef, lam, moved_0.at[r], wind, masks, (None, None), joined, decays, sums, grown.at[r], r, first, last
-        )
+        halos = near_rows, far_rows
+        back_row(local, coef, lam, moved_0.at[r], wind, masks, halos, joined, decays, sums, grown.at[r], r, first, last)
 
     inner_rows(rows, body)
-    for q in range(2):
-        parts[q] = gathered(sums, q)
-
-
-def outer_back_1_kernel(
-    local, table, coef, lam, moved_0, wind, sea, held, cells, wind_1, joined, parts, near_rows, far_rows,
-    grown, slots, masks, decays, sums,
+    outer_rows(rows, body)
+    lam_q, lam_wind = gathered(sums, 0), gathered(sums, 1) + wind_1[...]
+    for peer in range(slots.shape[0]):
+        slots[peer, 0] = lam_q
+        slots[peer, 1] = lam_wind
+
+
+def lam_0_kernel(
+    local, table, grown, sea, held, cells, got,
+    lam, near_rows, far_rows, cols, masks, decays, rests, packed,
+):
+    set_masks(sea, held, masks)
+    lam_q = total_of(got, 0)
+    set_rates(local, table, cells[0], lam_q * cells[1], lam_q * cells[2], decays, rests)
+    lam_rows(local, grown, masks, decays, rests, lam, near_rows, far_rows, cols, packed)
+
+
+def back_0_kernel(
+    coef, lam, sea, held, got, near_cols, far_cols, near_rows, far_rows, out, wind_total, joined, laid, masks, sent
 ):
     rows = lam.shape[0]
     set_masks(sea, held, masks)
-    set_decays(local, table, cells[0], decays)
-    clear_tiles(sums, range(1, rows - 1))
-
-    def body(r, first, last):
-        halos = near_rows, far_rows
-        i = int(last)
-        back_row(
-            local, coef, lam, moved_0.at[i], wind, masks, halos, joined, decays, sums, grown.at[i], r, first, last
-        )
-
-    outer_rows(rows, body)
-    lam_q, lam_wind = parts[0] + gathered(sums, 0), parts[1] + gathered(sums, 1) + wind_1[...]
-    for peer in range(slots.shape[0]):
-        slots[peer, 0] = lam_q
-        slots[peer, 1] = lam_wind
-
-
-def lam_0_kernel(
-    local, table, grown, outer, sea, held, cells, got,
-    lam, wind_total, near_rows, far_rows, cols, masks, decays, rests, packed,
-):
-    set_masks(sea, held, masks)
-    lam_q, lam_wind = got[0, 0], got[0, 1]
-    for peer in range(1, got.shape[0]):
-        lam_q, lam_wind = lam_q + got[peer, 0], lam_wind + got[peer, 1]
-    wind_total[...] = lam_wind
-    set_rates(local, table, cells[0], lam_q * cells[1], lam_q * cells[2], decays, rests)
-    lam_rows(local, grown, outer, masks, decays, rests, lam, near_rows, far_rows, cols, packed)
-
-
-def send_rows(rows, coef, lam, halos, columns, masks, out, laid, sent):
-    count = lam.shape[0]
-    copies = []
-    for r in rows:
+    join_columns(near_cols, far_cols, joined)
+    wind_total[...] = total_of(got, 1)
+    copies = [pltpu.make_async_copy(laid.at[r], out.at[:, r, :], sent.at[r]) for r in range(rows)]
+    halos = near_rows, far_rows
+    for r in range(rows):
         for t in range(lam.shape[1] // TILE):
-            laid[r, span(t), :] = back_of(
-                lam, *halos, columns, coef, masks, r, t, r == 0, r == count - 1
-            )
-        copies.append(pltpu.make_async_copy(laid.at[r], out.at[:, r, :], sent.at[r]))
-        copies[-1].start()
+            laid[r, span(t), :] = back_of(lam, *halos, joined, coef, masks, r, t, r == 0, r == rows - 1)
+        copies[r].start()
     for copy in copies:
         copy.wait()
-
-
-def inner_back_0_kernel(coef, lam, sea, held, near_cols, far_cols, out, joined, laid, masks, sent):
-    set_masks(sea, held, masks)
-    join_columns(near_cols, far_cols, joined)
-    send_rows(range(1, lam.shape[0] - 1), coef, lam, (None, None), joined, masks, out, laid, sent)
-
-
-def outer_back_0_kernel(coef, lam, sea, held, joined, near_rows, far_rows, inner, out, laid, masks, sent):
-    set_masks(sea, held, masks)
-    send_rows((0, lam.shape[0] - 1), coef, lam, (near_rows, far_rows), joined, masks, out, laid, sent)
 
 
 def swap(near, far, axis):
@@ -505,14 +451,13 @@
     return from_columns, swap(near_rows, far_rows, "gx")
 
 
-def call(body, outs, specs, *args, out_specs=None, scratch=(), us=2, mib=40, aliases=None):
+def call(body, outs, specs, *args, out_specs=None, scratch=(), us=2, mib=40):
     return pl.pallas_call(
         body,
         out_shape=[jax.ShapeDtypeStruct(shape, F32) for shape in outs],
         in_specs=specs,
         out_specs=out_specs or [VMEM] * len(outs),
         scratch_shapes=list(scratch),
-        input_output_aliases=aliases or {},
         cost_estimate=pl.CostEstimate(flops=us * 1000000, bytes_accessed=us * 1000000, transcendentals=0),
         compiler_params=pltpu.CompilerParams(vmem_limit_bytes=mib * 1024 * 1024),
     )(*args)
@@ -540,7 +485,7 @@
         edges_kernel,
         [(steps,) + shape for shape in [whole] + edges],
         [HBM],
-        trajectory.reshape(steps, bins, nx, ny),
+        pltpu.with_memory_space_constraint(trajectory.reshape(steps, bins, nx, ny), pltpu.HBM),
         scratch=[pltpu.SemaphoreType.DMA((steps, nx))],
     )
     coef, grown = call(
@@ -551,20 +496,13 @@
         scratch=[scratch(*whole), sems],
     )
     from_columns, from_rows = exchange(*edge)
-    parts, moved_0, joined = call(
-        functools.partial(inner_forward_kernel, local),
-        [(4 * local,) + cell, whole, (steps,) + cols],
-        [VMEM] * 7,
-        coef, laid, grown, sea, held, *from_columns,
-        scratch=[masks, scratch(4 * local, tiles, ny)],
+    slots, wind_parts, moved_0 = call(
+        functools.partial(forward_kernel, local),
+        [(peers, 4 + local) + cell, (local,) + cell, whole],
+        [SMEM] + [VMEM] * 9,
+        table, coef, laid, grown, sea, held, *from_columns, *from_rows,
+        scratch=[scratch(steps, *cols), masks, scratch(4 * local, tiles, ny)],
         us=4,
-    )
-    slots, wind_parts, outer_moved_0 = call(
-        functools.partial(outer_forward_kernel, local),
-        [(peers, 4 + local) + cell, (local,) + cell, (2,) + rows],
-        [SMEM] + [VMEM] * 9,
-        table, coef, laid, grown, sea, held, joined, parts, *from_rows,
-        scratch=[masks, scratch(4 * local, tiles, ny)],
     )
     got = lax.all_to_all(slots, "sa", 0, 0)
     lam, wind_1, cells, *edge = call(
@@ -575,47 +513,30 @@
         scratch=[masks, decays, rests, packed],
     )
     from_columns, from_rows = exchange(*edge)
-    grown, parts, joined = call(
-        functools.partial(inner_back_1_kernel, local),
-        [whole, (2,) + cell, cols],
-        [SMEM] + [VMEM] * 9,
-        table, coef, lam, moved_0, wind, sea, held, cells, *from_columns,
-        scratch=[masks, scratch(2 * local, *cell), scratch(2, tiles, ny)],
-        us=4,
-    )
-    outer, slots = call(
-        functools.partial(outer_back_1_kernel, local),
-        [(2,) + rows, (peers, 2) + cell],
+    grown, slots = call(
+        functools.partial(back_1_kernel, local),
+        [whole, (peers, 2) + cell],
         [SMEM] + [VMEM] * 12,
-        table, coef, lam, outer_moved_0, wind, sea, held, cells, wind_1, joined, parts, *from_rows,
-        scratch=[masks, scratch(2 * local, *cell), scratch(2, tiles, ny)],
+        table, coef, lam, moved_0, wind, sea, held, cells, wind_1, *from_columns, *from_rows,
+        scratch=[scratch(*cols), masks, scratch(2 * local, *cell), scratch(2, tiles, ny)],
+        us=3,
     )
     got = lax.all_to_all(slots, "sa", 0, 0)
-    lam, wind_total, *edge = call(
+    lam, *edge = call(
         functools.partial(lam_0_kernel, local),
-        [whole, cell] + edges,
-        [SMEM] + [VMEM] * 6,
-        table, grown, outer, sea, held, cells, got,
+        [whole] + edges,
+        [SMEM] + [VMEM] * 5,
+        table, grown, sea, held, cells, got,
         scratch=[masks, decays, rests, packed],
     )
     from_columns, from_rows = exchange(*edge)
-    inner, joined = call(
-        inner_back_0_kernel,
-        [(bins, nx, ny), cols],
-        [VMEM] * 6,
-        coef, lam, sea, held, *from_columns,
+    out, wind_total = call(
+        back_0_kernel,
+        [(bins, nx, ny), cell],
+        [VMEM] * 9,
+        coef, lam, sea, held, got, *from_columns, *from_rows,
         out_specs=[HBM, VMEM],
-        scratch=[scratch(*whole), masks, sems],
-        us=4,
-    )
-    (out,) = call(
-        outer_back_0_kernel,
-        [(bins, nx, ny)],
-        [VMEM] * 7 + [HBM],
-        coef, lam, sea, held, joined, *from_rows, inner,
-        out_specs=[HBM],
-        scratch=[scratch(*whole), masks, sems],
-        aliases={7: 0},
+        scratch=[scratch(*cols), scratch(*whole), masks, sems],
     )
     return out.reshape(local, dirs, nx, ny), wind_total
 

time: 102 us -> 96.9 us (0.950)
  Pallas kernels: 20.5 us -> 16.4 us
  local copies, waits for them, and re-layouts: 1.7 us -> 0.04 us
    pallas_call x10 -> x7, Pallas kernels: 20.5 us -> 16.4 us  [call(): pl.pallas_call(body, out_shape=[jax.ShapeDtypeStruct(shape, F32) for shap...]
    unnamed x18 -> x16, local copies, waits for them, and re-layouts: 1.7 us -> 0.04 us
  transfers between devices with their start and end apart: 12 -> 12, of which waited for: 2 -> 2; matrix products, arithmetic and copies ran while one was open for 0% -> 0% of each run, Pallas kernels for 10% -> 3%
where the time goes in v3:
time: 96.9 us; the launch traced here: 96.3 us
  starting transfers between devices  39.4 us (41%)
  blocking collectives  37.2 us (38%)
  Pallas kernels  16.4 us (17%)
  waiting for transfers between devices  2.32 us (2%)
    all_to_all x2, blocking collectives, shards(): got = lax.all_to_all(slots, 'sa', 0, 0)  37.2 us
    ppermute x6, starting transfers between devices, swap(): lax.ppermute(far, axis, pairs(1))  25 us
    pallas_call x7, Pallas kernels, call(): pl.pallas_call(body, out_shape=[jax.ShapeDtypeStruct(shape, F32) for shap...  16.4 us
    ppermute x6, starting transfers between devices, swap(): lax.ppermute(near, axis, pairs(0))  14.5 us
    ppermute x6, waiting for transfers between devices, swap(): lax.ppermute(near, axis, pairs(0))  2.27 us
  transfers between devices with their start and end apart: 12, of which 2 were waited for; matrix products, arithmetic and copies ran while one was open for 0% of the time, Pallas kernels for 3%

profile of v3, /device:TPU:57, one launch (start us, length us, event | category | flops | bytes accessed | tf_op | source)
XLA Modules:
  0.0 96.3 jit_solution(7356910110529226179)
XLA Ops:
  0.6 0.0 copy-start
  0.6 0.0 copy-start.3
  0.7 0.0 copy-start.5
  0.7 0.0 copy-start.6
  0.7 0.0 copy-start.7
  0.7 2.6 %shard_map.105 = (f32[2,16,144,128]{3,2,1,0:T(8,128)S(1)}, f32[2,144,128]{2,1,0:T(8,128)S(1)}, f32[2,144,128]{2,1,0:T(8,128)S(1)}, f32[2,5,8,128]{3,2,1,0:T(8,128)S(1)}) custom-call(f32[2,144,16,128]{3,2,1,0:T(8,128)} %bitcast.4), custom_call_target="tpu_custom_call" | custom-call | flops 2000000 | bytes 2000000 | tf_op jit(solution)/shard_map/pallas_call | solution.py:455
  3.3 0.0 copy-start.1
  3.3 0.0 copy-start.2
  3.3 0.0 copy-start.4
  3.3 3.1 %collective-permute-start.2 = (f32[2,144,128]{2,1,0:T(8,128)S(1)}, f32[2,144,128]{2,1,0:T(8,128)S(1)}, u32[]{:S(2)}, u32[]{:S(2)}) collective-permute-start(f32[2,144,128]{2,1,0:T(8,128)S(1)} %get-tuple-element.29), channel_id=1, source_target_pairs={{0,32},{32,0},{64,96},{96,64},{128,160},{160,128},{192,224},{224,1... | collective-permute-start | bytes 442376 | tf_op jit(solution)/shard_map/ppermute | solution.py:446
  6.4 2.6 %collective-permute-start.3 = (f32[2,144,128]{2,1,0:T(8,128)S(1)}, f32[2,144,128]{2,1,0:T(8,128)S(1)}, u32[]{:S(2)}, u32[]{:S(2)}) collective-permute-start(f32[2,144,128]{2,1,0:T(8,128)S(1)} %get-tuple-element.30), channel_id=1, source_target_pairs={{32,64},{64,32},{96,128},{128,96},{160,192},{192,160},{224,256},{2... | collective-permute-start | bytes 442376 | tf_op jit(solution)/shard_map/ppermute | solution.py:446
  9.0 5.5 %collective-permute-start.1 = (f32[2,5,8,128]{3,2,1,0:T(8,128)S(1)}, f32[2,5,8,128]{3,2,1,0:T(8,128)S(1)}, u32[]{:S(2)}, u32[]{:S(2)}) collective-permute-start(f32[2,5,8,128]{3,2,1,0:T(8,128)S(1)} %get-tuple-element.28), channel_id=1, source_target_pairs={{8,16},{16,8},{9,17},{17,9},{10,18},{18,10},{11,19},{19,11},{12,20... | collective-permute-start | bytes 122888 | tf_op jit(solution)/shard_map/ppermute | solution.py:446
  14.5 1.9 %collective-permute-start = (f32[2,5,8,128]{3,2,1,0:T(8,128)S(1)}, f32[2,5,8,128]{3,2,1,0:T(8,128)S(1)}, u32[]{:S(2)}, u32[]{:S(2)}) collective-permute-start(f32[2,5,8,128]{3,2,1,0:T(8,128)S(1)} %get-tuple-element.28), channel_id=1, source_target_pairs={{0,8},{8,0},{16,24},{24,16},{1,9},{9,1},{17,25},{25,17},{2,10},{10... | collective-permute-start | bytes 122888 | tf_op jit(solution)/shard_map/ppermute | solution.py:446
  16.4 0.0 copy-done
  16.4 0.0 copy-done.3
  16.4 0.0 copy-done.5
  16.4 0.0 copy-done.6
  16.4 0.0 copy-done.7
  16.4 2.9 %shard_map.104 = (f32[6,144,128]{2,1,0:T(8,128)S(1)}, f32[16,144,128]{2,1,0:T(8,128)S(1)}) custom-call(f32[4,36]{1,0:T(4,128)S(1)} %copy-done.6, f32[2,4,36]{2,1,0:T(4,128)S(1)} %copy-done.5, s32[4,36]{1,0:T(4,128)S(1)} %copy-done.7, f32[144,16,128]{2,1,0:T(8,128)S(1)} %bitcast.3, f32[16,128]{1,0:T(8,128)S(1)} %copy-done.3), custom_call_target="tpu_custom_call" | custom-call | flops 2000000 | bytes 2000000 | tf_op jit(solution)/shard_map/pallas_call | solution.py:455
  19.4 0.0 collective-permute-done.1.far_cols
  19.4 0.0 collective-permute-done.near_cols
  19.4 0.0 collective-permute-done.2.near_rows
  19.4 0.0 collective-permute-done.3.far_rows
  19.4 0.0 copy-done.1
  19.4 0.0 copy-done.2
  19.4 0.0 copy-done.4
  19.4 3.3 %shard_map.106 = (f32[8,8,16,128]{3,2,1,0:T(8,128)S(1)}, f32[4,16,128]{2,1,0:T(8,128)S(1)}, f32[16,144,128]{2,1,0:T(8,128)S(1)}) custom-call(f32[2,32]{1,0:T(2,128)S(1)} %copy-done.4, f32[6,144,128]{2,1,0:T(8,128)S(1)} %get-tuple-element.25.coef, f32[2,16,144,128]{3,2,1,0:T(8,128)S(1)} %get-tuple-element.27.laid, ...), custom_call_target="tpu_custom_call" | custom-call | flops 4000000 | bytes 4000000 | tf_op jit(solution)/shard_map/pallas_call | solution.py:455
  22.7 26.2 %all_to_all.10.got = f32[8,8,16,128]{3,2,1,0:T(8,128)S(1)} all-to-all(f32[8,8,16,128]{3,2,1,0:T(8,128)S(1)} %get-tuple-element.31), channel_id=1, replica_groups=mesh['gx'=16,'gy'=4,'sa'=8] {'sa'}, dimensions={0} | all-to-all | bytes 1048576 | tf_op jit(solution)/shard_map/all_to_all | solution.py:507
  48.9 1.5 %shard_map.107 = (f32[16,144,128]{2,1,0:T(8,128)S(1)}, f32[16,128]{1,0:T(8,128)S(1)}, f32[3,16,128]{2,1,0:T(8,128)S(1)}, f32[144,128]{1,0:T(8,128)S(1)}, f32[144...) custom-call(f32[2,32]{1,0:T(2,128)S(1)} %copy-done.4, f32[16,144,128]{2,1,0:T(8,128)S(1)} %get-tuple-element.26.grown, ...), custom_call_target="tpu_custom_call" | custom-call | flops 2000000 | bytes 2000000 | tf_op jit(solution)/shard_map/pallas_call | solution.py:455
  50.4 3.7 %collective-permute-start.6 = (f32[144,128]{1,0:T(8,128)S(1)}, f32[144,128]{1,0:T(8,128)S(1)}, u32[]{:S(2)}, u32[]{:S(2)}) collective-permute-start(f32[144,128]{1,0:T(8,128)S(1)} %get-tuple-element.38), channel_id=1, source_target_pairs={{0,32},{32,0},{64,96},{96,64},{128,160},{160,128},{192,224},{224,1... | collective-permute-start | bytes 221192 | tf_op jit(solution)/shard_map/ppermute | solution.py:446
  54.1 2.8 %collective-permute-start.7 = (f32[144,128]{1,0:T(8,128)S(1)}, f32[144,128]{1,0:T(8,128)S(1)}, u32[]{:S(2)}, u32[]{:S(2)}) collective-permute-start(f32[144,128]{1,0:T(8,128)S(1)} %get-tuple-element.39), channel_id=1, source_target_pairs={{32,64},{64,32},{96,128},{128,96},{160,192},{192,160},{224,256},{2... | collective-permute-start | bytes 221192 | tf_op jit(solution)/shard_map/ppermute | solution.py:446
  56.9 4.9 %collective-permute-start.5 = (f32[5,8,128]{2,1,0:T(8,128)S(1)}, f32[5,8,128]{2,1,0:T(8,128)S(1)}, u32[]{:S(2)}, u32[]{:S(2)}) collective-permute-start(f32[5,8,128]{2,1,0:T(8,128)S(1)} %get-tuple-element.37), channel_id=1, source_target_pairs={{8,16},{16,8},{9,17},{17,9},{10,18},{18,10},{11,19},{19,11},{12,20... | collective-permute-start | bytes 61448 | tf_op jit(solution)/shard_map/ppermute | solution.py:446
  61.8 1.9 %collective-permute-start.4 = (f32[5,8,128]{2,1,0:T(8,128)S(1)}, f32[5,8,128]{2,1,0:T(8,128)S(1)}, u32[]{:S(2)}, u32[]{:S(2)}) collective-permute-start(f32[5,8,128]{2,1,0:T(8,128)S(1)} %get-tuple-element.37), channel_id=1, source_target_pairs={{0,8},{8,0},{16,24},{24,16},{1,9},{9,1},{17,25},{25,17},{2,10},{10... | collective-permute-start | bytes 61448 | tf_op jit(solution)/shard_map/ppermute | solution.py:446
  63.7 0.0 collective-permute-done.5.far_cols
  63.8 1.1 %collective-permute-done.4.near_cols = f32[5,8,128]{2,1,0:T(8,128)S(1)} collective-permute-done((f32[5,8,128]{2,1,0:T(8,128)S(1)}, f32[5,8,128]{2,1,0:T(8,128)S(1)}, u32[]{:S(2)}, u32[]{:S(2)}) %collective-permute-start.4) | collective-permute-done | bytes 20512 | tf_op jit(solution)/shard_map/ppermute | solution.py:446
  64.9 0.0 collective-permute-done.6.near_rows
  64.9 0.0 collective-permute-done.7.far_rows
  64.9 2.3 %shard_map.108 = (f32[16,144,128]{2,1,0:T(8,128)S(1)}, f32[8,2,16,128]{3,2,1,0:T(8,128)S(1)}) custom-call(f32[2,32]{1,0:T(2,128)S(1)} %copy-done.4, f32[6,144,128]{2,1,0:T(8,128)S(1)} %get-tuple-element.25.coef, f32[16,144,128]{2,1,0:T(8,128)S(1)} %get-tuple-element.33.lam, f32[16,144,128]{2,1,0:T(8,128)S(1)} %get-tuple-element.34.moved_0, ...), custom_call_target="tpu_custom_call" | custom-call | flops 3000000 | bytes 3000000 | tf_op jit(solution)/shard_map/pallas_call | solution.py:455
  67.2 11.0 %all_to_all.11.got = f32[8,2,16,128]{3,2,1,0:T(8,128)S(1)} all-to-all(f32[8,2,16,128]{3,2,1,0:T(8,128)S(1)} %get-tuple-element.41), channel_id=1, replica_groups=mesh['gx'=16,'gy'=4,'sa'=8] {'sa'}, dimensions={0} | all-to-all | bytes 262144 | tf_op jit(solution)/shard_map/all_to_all | solution.py:524
  78.2 1.5 %shard_map.109 = (f32[16,144,128]{2,1,0:T(8,128)S(1)}, f32[144,128]{1,0:T(8,128)S(1)}, f32[144,128]{1,0:T(8,128)S(1)}, f32[5,8,128]{2,1,0:T(8,128)S(1)}) custom-call(f32[2,32]{1,0:T(2,128)S(1)} %copy-done.4, f32[16,144,128]{2,1,0:T(8,128)S(1)} %get-tuple-element.40.grown, s32[16,128]{1,0:T(8,128)S(1)} %copy-done.1, s32[16,128]{1,0:T(8,128)S(1)} %copy-done.2, ...), custom_call_target="tpu_custom_call" | custom-call | flops 2000000 | bytes 2000000 | tf_op jit(solution)/shard_map/pallas_call | solution.py:455
  79.6 1.9 %collective-permute-start.10 = (f32[144,128]{1,0:T(8,128)S(1)}, f32[144,128]{1,0:T(8,128)S(1)}, u32[]{:S(2)}, u32[]{:S(2)}) collective-permute-start(f32[144,128]{1,0:T(8,128)S(1)} %get-tuple-element.44), channel_id=1, source_target_pairs={{0,32},{32,0},{64,96},{96,64},{128,160},{160,128},{192,224},{224,1... | collective-permute-start | bytes 221192 | tf_op jit(solution)/shard_map/ppermute | solution.py:446
  81.6 4.1 %collective-permute-start.11 = (f32[144,128]{1,0:T(8,128)S(1)}, f32[144,128]{1,0:T(8,128)S(1)}, u32[]{:S(2)}, u32[]{:S(2)}) collective-permute-start(f32[144,128]{1,0:T(8,128)S(1)} %get-tuple-element.45), channel_id=1, source_target_pairs={{32,64},{64,32},{96,128},{128,96},{160,192},{192,160},{224,256},{2... | collective-permute-start | bytes 221192 | tf_op jit(solution)/shard_map/ppermute | solution.py:446
  85.7 5.1 %collective-permute-start.9 = (f32[5,8,128]{2,1,0:T(8,128)S(1)}, f32[5,8,128]{2,1,0:T(8,128)S(1)}, u32[]{:S(2)}, u32[]{:S(2)}) collective-permute-start(f32[5,8,128]{2,1,0:T(8,128)S(1)} %get-tuple-element.43), channel_id=1, source_target_pairs={{8,16},{16,8},{9,17},{17,9},{10,18},{18,10},{11,19},{19,11},{12,20... | collective-permute-start | bytes 61448 | tf_op jit(solution)/shard_map/ppermute | solution.py:446
  90.8 1.9 %collective-permute-start.8 = (f32[5,8,128]{2,1,0:T(8,128)S(1)}, f32[5,8,128]{2,1,0:T(8,128)S(1)}, u32[]{:S(2)}, u32[]{:S(2)}) collective-permute-start(f32[5,8,128]{2,1,0:T(8,128)S(1)} %get-tuple-element.43), channel_id=1, source_target_pairs={{0,8},{8,0},{16,24},{24,16},{1,9},{9,1},{17,25},{25,17},{2,10},{10... | collective-permute-start | bytes 61448 | tf_op jit(solution)/shard_map/ppermute | solution.py:446
  92.8 0.0 collective-permute-done.9.far_cols
  92.8 1.1 %collective-permute-done.8.near_cols = f32[5,8,128]{2,1,0:T(8,128)S(1)} collective-permute-done((f32[5,8,128]{2,1,0:T(8,128)S(1)}, f32[5,8,128]{2,1,0:T(8,128)S(1)}, u32[]{:S(2)}, u32[]{:S(2)}) %collective-permute-start.8) | collective-permute-done | bytes 20512 | tf_op jit(solution)/shard_map/ppermute | solution.py:446
  93.9 0.0 collective-permute-done.10.near_rows
  93.9 0.0 collective-permute-done.11.far_rows
  93.9 2.4 %shard_map.110 = (f32[144,16,128]{2,1,0:T(8,128)}, f32[16,128]{1,0:T(8,128)}) custom-call(f32[6,144,128]{2,1,0:T(8,128)S(1)} %get-tuple-element.25.coef, f32[16,144,128]{2,1,0:T(8,128)S(1)} %get-tuple-element.42.lam, s32[16,128]{1,0:T(8,128)S(1)} %copy-done.1, s32[16,128]{1,0:T(8,128)S(1)} %copy-done.2, f32[8,2,16,128]{3,2,1,0:T(8,128)S(1)} %all_to_all.11.got, ...), custom_call_target="tpu_custom_call" | custom-call | flops 2000000 | bytes 2000000 | tf_op jit(solution)/shard_map/pallas_call | solution.py:455
Async XLA Ops:
  0.6 15.8 %copy-start = (f32[4,36,16,128]{3,2,1,0:T(8,128)S(1)}, f32[4,36,16,128]{3,2,1,0:T(8,128)}, u32[]{:S(2)}) copy-start(f32[4,36,16,128]{3,2,1,0:T(8,128)} %param.10) | copy-start | bytes 3538948
  0.6 15.8 %copy-start.3 = (f32[16,128]{1,0:T(8,128)S(1)}, f32[16,128]{1,0:T(8,128)}, u32[]{:S(2)}) copy-start(f32[16,128]{1,0:T(8,128)} %wind.3) | copy-start | bytes 24580
  0.7 15.8 %copy-start.5 = (f32[2,4,36]{2,1,0:T(4,128)S(1)}, f32[2,4,36]{2,1,0:T(4,128)}, u32[]{:S(2)}) copy-start(f32[2,4,36]{2,1,0:T(4,128)} %speed.1) | copy-start | bytes 3460
  0.7 15.8 %copy-start.6 = (f32[4,36]{1,0:T(4,128)S(1)}, f32[4,36]{1,0:T(4,128)}, u32[]{:S(2)}) copy-start(f32[4,36]{1,0:T(4,128)} %growth.1) | copy-start | bytes 1732
  0.7 15.8 %copy-start.7 = (s32[4,36]{1,0:T(4,128)S(1)}, s32[4,36]{1,0:T(4,128)}, u32[]{:S(2)}) copy-start(s32[4,36]{1,0:T(4,128)} %code.1) | copy-start | bytes 1732
  3.3 16.2 %copy-start.1 = (s32[16,128]{1,0:T(8,128)S(1)}, s32[16,128]{1,0:T(8,128)}, u32[]{:S(2)}) copy-start(s32[16,128]{1,0:T(8,128)} %sea.9) | copy-start | bytes 24580
  3.3 16.2 %copy-start.2 = (s32[16,128]{1,0:T(8,128)S(1)}, s32[16,128]{1,0:T(8,128)}, u32[]{:S(2)}) copy-start(s32[16,128]{1,0:T(8,128)} %held.9) | copy-start | bytes 24580
  3.3 16.2 %copy-start.4 = (f32[2,32]{1,0:T(2,128)S(1)}, f32[2,32]{1,0:T(2,128)}, u32[]{:S(2)}) copy-start(f32[2,32]{1,0:T(2,128)} %constant.2.clone.table) | copy-start | bytes 772
  3.3 16.1 %collective-permute-start.2 = (f32[2,144,128]{2,1,0:T(8,128)S(1)}, f32[2,144,128]{2,1,0:T(8,128)S(1)}, u32[]{:S(2)}, u32[]{:S(2)}) collective-permute-start(f32[2,144,128]{2,1,0:T(8,128)S(1)} %get-tuple-element.29), channel_id=1, source_target_pairs={{0,32},{32,0},{64,96},{96,64},{128,160},{160,128},{192,224},{224,1... | collective-permute-start | bytes 442376 | tf_op jit(solution)/shard_map/ppermute | solution.py:446
  6.4 13.0 %collective-permute-start.3 = (f32[2,144,128]{2,1,0:T(8,128)S(1)}, f32[2,144,128]{2,1,0:T(8,128)S(1)}, u32[]{:S(2)}, u32[]{:S(2)}) collective-permute-start(f32[2,144,128]{2,1,0:T(8,128)S(1)} %get-tuple-element.30), channel_id=1, source_target_pairs={{32,64},{64,32},{96,128},{128,96},{160,192},{192,160},{224,256},{2... | collective-permute-start | bytes 442376 | tf_op jit(solution)/shard_map/ppermute | solution.py:446
  9.0 10.4 %collective-permute-start.1 = (f32[2,5,8,128]{3,2,1,0:T(8,128)S(1)}, f32[2,5,8,128]{3,2,1,0:T(8,128)S(1)}, u32[]{:S(2)}, u32[]{:S(2)}) collective-permute-start(f32[2,5,8,128]{3,2,1,0:T(8,128)S(1)} %get-tuple-element.28), channel_id=1, source_target_pairs={{8,16},{16,8},{9,17},{17,9},{10,18},{18,10},{11,19},{19,11},{12,20... | collective-permute-start | bytes 122888 | tf_op jit(solution)/shard_map/ppermute | solution.py:446
  14.5 4.9 %collective-permute-start = (f32[2,5,8,128]{3,2,1,0:T(8,128)S(1)}, f32[2,5,8,128]{3,2,1,0:T(8,128)S(1)}, u32[]{:S(2)}, u32[]{:S(2)}) collective-permute-start(f32[2,5,8,128]{3,2,1,0:T(8,128)S(1)} %get-tuple-element.28), channel_id=1, source_target_pairs={{0,8},{8,0},{16,24},{24,16},{1,9},{9,1},{17,25},{25,17},{2,10},{10... | collective-permute-start | bytes 122888 | tf_op jit(solution)/shard_map/ppermute | solution.py:446
  50.4 14.5 %collective-permute-start.6 = (f32[144,128]{1,0:T(8,128)S(1)}, f32[144,128]{1,0:T(8,128)S(1)}, u32[]{:S(2)}, u32[]{:S(2)}) collective-permute-start(f32[144,128]{1,0:T(8,128)S(1)} %get-tuple-element.38), channel_id=1, source_target_pairs={{0,32},{32,0},{64,96},{96,64},{128,160},{160,128},{192,224},{224,1... | collective-permute-start | bytes 221192 | tf_op jit(solution)/shard_map/ppermute | solution.py:446
  54.1 10.8 %collective-permute-start.7 = (f32[144,128]{1,0:T(8,128)S(1)}, f32[144,128]{1,0:T(8,128)S(1)}, u32[]{:S(2)}, u32[]{:S(2)}) collective-permute-start(f32[144,128]{1,0:T(8,128)S(1)} %get-tuple-element.39), channel_id=1, source_target_pairs={{32,64},{64,32},{96,128},{128,96},{160,192},{192,160},{224,256},{2... | collective-permute-start | bytes 221192 | tf_op jit(solution)/shard_map/ppermute | solution.py:446
  56.9 6.9 %collective-permute-start.5 = (f32[5,8,128]{2,1,0:T(8,128)S(1)}, f32[5,8,128]{2,1,0:T(8,128)S(1)}, u32[]{:S(2)}, u32[]{:S(2)}) collective-permute-start(f32[5,8,128]{2,1,0:T(8,128)S(1)} %get-tuple-element.37), channel_id=1, source_target_pairs={{8,16},{16,8},{9,17},{17,9},{10,18},{18,10},{11,19},{19,11},{12,20... | collective-permute-start | bytes 61448 | tf_op jit(solution)/shard_map/ppermute | solution.py:446
  61.8 3.1 %collective-permute-start.4 = (f32[5,8,128]{2,1,0:T(8,128)S(1)}, f32[5,8,128]{2,1,0:T(8,128)S(1)}, u32[]{:S(2)}, u32[]{:S(2)}) collective-permute-start(f32[5,8,128]{2,1,0:T(8,128)S(1)} %get-tuple-element.37), channel_id=1, source_target_pairs={{0,8},{8,0},{16,24},{24,16},{1,9},{9,1},{17,25},{25,17},{2,10},{10... | collective-permute-start | bytes 61448 | tf_op jit(solution)/shard_map/ppermute | solution.py:446
  79.6 14.3 %collective-permute-start.10 = (f32[144,128]{1,0:T(8,128)S(1)}, f32[144,128]{1,0:T(8,128)S(1)}, u32[]{:S(2)}, u32[]{:S(2)}) collective-permute-start(f32[144,128]{1,0:T(8,128)S(1)} %get-tuple-element.44), channel_id=1, source_target_pairs={{0,32},{32,0},{64,96},{96,64},{128,160},{160,128},{192,224},{224,1... | collective-permute-start | bytes 221192 | tf_op jit(solution)/shard_map/ppermute | solution.py:446
  81.6 12.4 %collective-permute-start.11 = (f32[144,128]{1,0:T(8,128)S(1)}, f32[144,128]{1,0:T(8,128)S(1)}, u32[]{:S(2)}, u32[]{:S(2)}) collective-permute-start(f32[144,128]{1,0:T(8,128)S(1)} %get-tuple-element.45), channel_id=1, source_target_pairs={{32,64},{64,32},{96,128},{128,96},{160,192},{192,160},{224,256},{2... | collective-permute-start | bytes 221192 | tf_op jit(solution)/shard_map/ppermute | solution.py:446
  85.7 7.1 %collective-permute-start.9 = (f32[5,8,128]{2,1,0:T(8,128)S(1)}, f32[5,8,128]{2,1,0:T(8,128)S(1)}, u32[]{:S(2)}, u32[]{:S(2)}) collective-permute-start(f32[5,8,128]{2,1,0:T(8,128)S(1)} %get-tuple-element.43), channel_id=1, source_target_pairs={{8,16},{16,8},{9,17},{17,9},{10,18},{18,10},{11,19},{19,11},{12,20... | collective-permute-start | bytes 61448 | tf_op jit(solution)/shard_map/ppermute | solution.py:446
  90.8 3.1 %collective-permute-start.8 = (f32[5,8,128]{2,1,0:T(8,128)S(1)}, f32[5,8,128]{2,1,0:T(8,128)S(1)}, u32[]{:S(2)}, u32[]{:S(2)}) collective-permute-start(f32[5,8,128]{2,1,0:T(8,128)S(1)} %get-tuple-element.43), channel_id=1, source_target_pairs={{0,8},{8,0},{16,24},{24,16},{1,9},{9,1},{17,25},{25,17},{2,10},{10... | collective-permute-start | bytes 61448 | tf_op jit(solution)/shard_map/ppermute | solution.py:446

commit v4 on v3

--- a/solution.py
+++ b/solution.py
@@ -151,6 +151,30 @@
     for k in range(1, TILE):
         total = total + sums[q, pl.ds(k, rows, TILE), :]
     return total
+
+
+def block_of(lane):
+    return lax.rem(lane + 1, 128) // 32
+
+
+def edge_map(cell):
+    lane = lanes_of((1, 128))
+    packed = jnp.zeros((1, 128), F32)
+    for r in range(cell.shape[0]):
+        here = (lane == 2 * r) | (lane == (2 * r + 127) % 128)
+        packed = jnp.where(here, pltpu.roll(cell[r : r + 1, :], 2 * r, 1), packed)
+    out = packed
+    for k in range(1, PACK):
+        out = jnp.where(block_of(lane) == k, pltpu.roll(packed, 32 * k, 1), out)
+    return out
+
+
+def pick_group(values, g, tiles):
+    block = block_of(lanes_of((TILE, 128)))
+    out = jnp.broadcast_to(pick(values, g * PACK), block.shape)
+    for k in range(1, min(PACK, tiles - g * PACK)):
+        out = jnp.where(block == k, pick(values, g * PACK + k), out)
+    return out
 
 
 def edges_kernel(state, laid, near_rows, far_rows, cols, arrived):
@@ -178,7 +202,7 @@
             cols[s, g] = packed[s][g]
 
 
-def prepare_kernel(local, growth, speed, code, seed, wind, coef, grown, laid, arrived):
+def prepare_kernel(local, growth, speed, code, seed, wind, coef, grown, edge_cols, laid, arrived):
     rows, bins, lanes = grown.shape
     copies = [pltpu.make_async_copy(seed.at[:, r, :], laid.at[r], arrived.at[r]) for r in range(rows)]
     for copy in copies:
@@ -201,13 +225,18 @@
         return carry
 
     lax.fori_loop(0, DIRS, fill, 0)
+    packed = [jnp.zeros((TILE, lanes), F32)] * edge_cols.shape[0]
     for r in range(rows):
         if r % WAITS == 0:
             for copy in copies[r : r + WAITS]:
                 copy.wait()
         half_wind = 0.5 * row_of(wind, r)
         for t in range(bins // TILE):
-            grown[r, span(t), :] = laid[r, span(t), :] * jnp.exp(half_wind * coef[GROWTH, span(t), :])
+            value = laid[r, span(t), :] * jnp.exp(half_wind * coef[GROWTH, span(t), :])
+            grown[r, span(t), :] = value
+            pack_columns(packed, value, r, t)
+    for g in range(edge_cols.shape[0]):
+        edge_cols[g] = packed[g]
 
 
 def moved_of(laid, near_rows, far_rows, columns, coef, s1, s2, r, t, first, last):
@@ -288,41 +317,32 @@
     return value
 
 
-def set_rates(local, table, q, by_energy, by_first, decays, rests):
+def lam_edges(local, table, grown, edge_cols, masks, q, by_energy, by_first, decays, rests, near_rows, far_rows, cols):
+    rows, bins, _ = grown.shape
+    packed_q, packed_energy, packed_first = edge_map(q), edge_map(by_energy), edge_map(by_first)
+    packed_s1 = edge_map(masks[0])
+    decay, rest = [], []
     for f in range(local):
         freq, weight = bin_constants(table, f, local)
         decays[f] = jnp.exp((-0.5 * freq) * q)
         rests[f] = weight * by_energy + (weight * freq) * by_first
-
-
-def lam_rows(local, source, masks, decays, rests, lam, near_rows, far_rows, cols, packed):
-    rows, bins, _ = lam.shape
-    for g in range(packed.shape[0]):
-        packed[g] = jnp.zeros((TILE, 128), F32)
-
-    def body(r, first, last):
+        decay.append(jnp.exp((-0.5 * freq) * packed_q))
+        rest.append(weight * packed_energy + (weight * freq) * packed_first)
+    tiles = bins // TILE
+    for g in range(cols.shape[0]):
+        cols[g] = packed_s1 * (edge_cols[g] * pick_group(decay, g, tiles) + pick_group(rest, g, tiles))
+    for r in (0, rows - 1):
         s1 = row_of(masks.at[0], r)
         decay = [row_of(decays.at[f], r) for f in range(local)]
         rest = [row_of(rests.at[f], r) for f in range(local)]
-        columns = [packed[g] for g in range(packed.shape[0])]
-        for t in range(bins // TILE):
-            value = source[r, span(t), :] * pick(decay, t) + pick(rest, t)
-            lam[r, span(t), :] = value
-            flow = s1 * value
-            pack_columns(columns, flow, r, t)
-            put_rows(near_rows, far_rows, t, flow, first, last)
-        for g in range(packed.shape[0]):
-            packed[g] = columns[g]
-
-    inner_rows(rows, body)
-    outer_rows(rows, body)
-    for g in range(packed.shape[0]):
-        cols[g] = packed[g]
+        for t in range(tiles):
+            flow = s1 * (grown[r, span(t), :] * pick(decay, t) + pick(rest, t))
+            put_rows(near_rows, far_rows, t, flow, r == 0, r > 0)
 
 
 def lam_1_kernel(
-    local, table, grown, sea, held, got, wind_parts,
-    lam, wind_1, cells, near_rows, far_rows, cols, masks, decays, rests, packed,
+    local, table, grown, edge_cols, sea, held, got, wind_parts,
+    decays, rests, wind_1, cells, near_rows, far_rows, cols, masks,
 ):
     peers = got.shape[0]
     set_masks(sea, held, masks)
@@ -333,31 +353,58 @@
         for f in range(local):
             freq = float(frequency_table[peer * local + f])
             lam_q = lam_q + (-0.5 * freq) * jnp.exp((-0.5 * freq) * q) * got[peer, 4 + f]
-    set_rates(local, table, q, lam_q * by_energy, lam_q * by_first, decays, rests)
+    by_energy, by_first = lam_q * by_energy, lam_q * by_first
+    lam_edges(
+        local, table, grown, edge_cols, masks, q, by_energy, by_first, decays, rests, near_rows, far_rows, cols
+    )
     wind = jnp.zeros_like(q)
     for f in range(local):
         wind = wind + 0.5 * decays[f] * wind_parts[f]
     wind_1[...] = wind
-    lam_rows(local, grown, masks, decays, rests, lam, near_rows, far_rows, cols, packed)
-
-
-def back_of(lam, near_rows, far_rows, columns, coef, masks, r, t, first, last):
-    value = lam[r, span(t), :]
-    flow = row_of(masks.at[0], r) * value
-    if first:
-        prev_x = row_halo(near_rows, far_rows, t, True)
-    else:
-        prev_x = row_of(masks.at[0], r - 1) * lam[r - 1, span(t), :]
-    if last:
-        next_x = row_halo(near_rows, far_rows, t, False)
-    else:
-        next_x = row_of(masks.at[0], r + 1) * lam[r + 1, span(t), :]
-    prev_y, next_y = along_lanes(flow, columns, r, t)
+
+
+def along_x_kernel(
+    local, coef, grown, sea, held, decays, rests, near_rows, far_rows, flow, base, masks
+):
+    rows, bins, _ = grown.shape
+    tiles = bins // TILE
+    set_masks(sea, held, masks)
+
+    def start(r):
+        s1, s2 = row_of(masks.at[0], r), row_of(masks.at[1], r)
+        decay = [row_of(decays.at[f], r) for f in range(local)]
+        rest = [row_of(rests.at[f], r) for f in range(local)]
+        for t in range(tiles):
+            lam = grown[r, span(t), :] * pick(decay, t) + pick(rest, t)
+            value = s1 * lam
+            flow[r, span(t), :] = value
+            base[r, span(t), :] = s2 * lam + coef[STAY, span(t), :] * value
+
+    def start_pair(i, carry):
+        start(2 * i)
+        start(2 * i + 1)
+        return carry
+
+    lax.fori_loop(0, rows // 2, start_pair, 0)
+
+    def body(r, first, last):
+        for t in range(tiles):
+            prev_x = row_halo(near_rows, far_rows, t, True) if first else flow[r - 1, span(t), :]
+            next_x = row_halo(near_rows, far_rows, t, False) if last else flow[r + 1, span(t), :]
+            base[r, span(t), :] = (
+                base[r, span(t), :]
+                + coef[FROM_NEXT_X, span(t), :] * prev_x
+                + coef[FROM_PREV_X, span(t), :] * next_x
+            )
+
+    inner_rows(rows, body)
+    outer_rows(rows, body)
+
+
+def along_y(flow, base, columns, coef, r, t):
+    prev_y, next_y = along_lanes(flow[r, span(t), :], columns, r, t)
     return (
-        row_of(masks.at[1], r) * value
-        + coef[STAY, span(t), :] * flow
-        + coef[FROM_NEXT_X, span(t), :] * prev_x
-        + coef[FROM_PREV_X, span(t), :] * next_x
+        base[r, span(t), :]
         + coef[FROM_NEXT_Y, span(t), :] * prev_y
         + coef[FROM_PREV_Y, span(t), :] * next_y
     )
@@ -371,39 +418,45 @@
         decays[local + f] = 0.5 * decay
 
 
-def back_row(local, coef, lam, moved_0, wind, masks, halos, columns, decays, sums, grown, r, first, last):
-    half_wind = 0.5 * row_of(wind, r)
-    for_q = [row_of(decays.at[f], r) for f in range(local)]
-    for_wind = [row_of(decays.at[local + f], r) for f in range(local)]
-    lam_q = lam_wind = jnp.zeros((TILE, 128), F32)
-    for t in range(lam.shape[1] // TILE):
-        density = back_of(lam, *halos, columns, coef, masks, r, t, first, last)
-        g = coef[GROWTH, span(t), :]
-        density = density * jnp.exp(half_wind * g)
-        grown[span(t), :] = density
-        term = density * moved_0[span(t), :]
-        lam_q = lam_q + pick(for_q, t) * term
-        lam_wind = lam_wind + pick(for_wind, t) * (g * term)
-    sums[0, tile_at(r), :] = lam_q
-    sums[1, tile_at(r), :] = lam_wind
-
-
 def back_1_kernel(
-    local, table, coef, lam, moved_0, wind, sea, held, cells, wind_1,
-    near_cols, far_cols, near_rows, far_rows,
-    grown, slots, joined, masks, decays, sums,
+    local, table, coef, flow, base, moved_0, wind, cells, wind_1, near_cols, far_cols,
+    grown, edge_cols, slots, joined, packed, decays, sums,
 ):
-    rows = lam.shape[0]
-    set_masks(sea, held, masks)
+    rows, bins, _ = flow.shape
     join_columns(near_cols, far_cols, joined)
     set_decays(local, table, cells[0], decays)
-
-    def body(r, first, last):
-        halos = near_rows, far_rows
-        back_row(local, coef, lam, moved_0.at[r], wind, masks, halos, joined, decays, sums, grown.at[r], r, first, last)
-
-    inner_rows(rows, body)
-    outer_rows(rows, body)
+    zero = jnp.zeros((TILE, 128), F32)
+    groups = packed.shape[0]
+    for g in range(groups):
+        packed[g] = zero
+
+    def row(r, columns):
+        half_wind = 0.5 * row_of(wind, r)
+        for_q = [row_of(decays.at[f], r) for f in range(local)]
+        for_wind = [row_of(decays.at[local + f], r) for f in range(local)]
+        lam_q = lam_wind = zero
+        for t in range(bins // TILE):
+            g = coef[GROWTH, span(t), :]
+            density = along_y(flow, base, joined, coef, r, t) * jnp.exp(half_wind * g)
+            grown[r, span(t), :] = density
+            pack_columns(columns, density, r, t)
+            term = density * moved_0[r, span(t), :]
+            lam_q = lam_q + pick(for_q, t) * term
+            lam_wind = lam_wind + pick(for_wind, t) * (g * term)
+        sums[0, tile_at(r), :] = lam_q
+        sums[1, tile_at(r), :] = lam_wind
+
+    def pair(i, carry):
+        columns = [packed[g] for g in range(groups)]
+        row(2 * i, columns)
+        row(2 * i + 1, columns)
+        for g in range(groups):
+            packed[g] = columns[g]
+        return carry
+
+    lax.fori_loop(0, rows // 2, pair, 0)
+    for g in range(groups):
+        edge_cols[g] = packed[g]
     lam_q, lam_wind = gathered(sums, 0), gathered(sums, 1) + wind_1[...]
     for peer in range(slots.shape[0]):
         slots[peer, 0] = lam_q
@@ -411,27 +464,27 @@
 
 
 def lam_0_kernel(
-    local, table, grown, sea, held, cells, got,
-    lam, near_rows, far_rows, cols, masks, decays, rests, packed,
+    local, table, grown, edge_cols, sea, held, cells, got, decays, rests, near_rows, far_rows, cols, masks
 ):
     set_masks(sea, held, masks)
     lam_q = total_of(got, 0)
-    set_rates(local, table, cells[0], lam_q * cells[1], lam_q * cells[2], decays, rests)
-    lam_rows(local, grown, masks, decays, rests, lam, near_rows, far_rows, cols, packed)
-
-
-def back_0_kernel(
-    coef, lam, sea, held, got, near_cols, far_cols, near_rows, far_rows, out, wind_total, joined, laid, masks, sent
-):
-    rows = lam.shape[0]
-    set_masks(sea, held, masks)
+    by_energy, by_first = lam_q * cells[1], lam_q * cells[2]
+    lam_edges(
+        local, table, grown, edge_cols, masks, cells[0], by_energy, by_first, decays, rests, near_rows, far_rows, cols
+    )
+
+
+def wind_kernel(got, wind_total):
+    wind_total[...] = total_of(got, 1)
+
+
+def back_0_kernel(coef, flow, base, near_cols, far_cols, out, joined, laid, sent):
+    rows, bins, _ = flow.shape
     join_columns(near_cols, far_cols, joined)
-    wind_total[...] = total_of(got, 1)
     copies = [pltpu.make_async_copy(laid.at[r], out.at[:, r, :], sent.at[r]) for r in range(rows)]
-    halos = near_rows, far_rows
     for r in range(rows):
-        for t in range(lam.shape[1] // TILE):
-            laid[r, span(t), :] = back_of(lam, *halos, joined, coef, masks, r, t, r == 0, r == rows - 1)
+        for t in range(bins // TILE):
+            laid[r, span(t), :] = along_y(flow, base, joined, coef, r, t)
         copies[r].start()
     for copy in copies:
         copy.wait()
@@ -477,7 +530,6 @@
     rows, cols, whole, cell = (bins, ny), (groups, TILE, ny), (nx, bins, ny), (nx, ny)
     edges = [rows, rows, cols]
     masks = scratch(2, *cell)
-    decays, rests, packed = scratch(local, *cell), scratch(local, *cell), scratch(*cols)
 
     sems, tiles = pltpu.SemaphoreType.DMA((nx,)), nx * TILE
 
@@ -488,9 +540,9 @@
         pltpu.with_memory_space_constraint(trajectory.reshape(steps, bins, nx, ny), pltpu.HBM),
         scratch=[pltpu.SemaphoreType.DMA((steps, nx))],
     )
-    coef, grown = call(
+    coef, grown, edge_cols = call(
         functools.partial(prepare_kernel, local),
-        [(6,) + rows, whole],
+        [(6,) + rows, whole, cols],
         [SMEM] * 3 + [HBM, VMEM],
         growth, speed, code, adjoint_seed.reshape(bins, nx, ny), wind,
         scratch=[scratch(*whole), sems],
@@ -505,38 +557,55 @@
         us=4,
     )
     got = lax.all_to_all(slots, "sa", 0, 0)
-    lam, wind_1, cells, *edge = call(
+    by_freq = (local,) + cell
+    decays, rests, wind_1, cells, *edge = call(
         functools.partial(lam_1_kernel, local),
-        [whole, cell, (3,) + cell] + edges,
-        [SMEM] + [VMEM] * 5,
-        table, grown, sea, held, got, wind_parts,
-        scratch=[masks, decays, rests, packed],
+        [by_freq, by_freq, cell, (3,) + cell] + edges,
+        [SMEM] + [VMEM] * 6,
+        table, grown, edge_cols, sea, held, got, wind_parts,
+        scratch=[masks],
+        us=1,
     )
     from_columns, from_rows = exchange(*edge)
-    grown, slots = call(
+    flow, base = call(
+        functools.partial(along_x_kernel, local),
+        [whole, whole],
+        [VMEM] * 8,
+        coef, grown, sea, held, decays, rests, *from_rows,
+        scratch=[masks],
+    )
+    grown, edge_cols, slots = call(
         functools.partial(back_1_kernel, local),
-        [whole, (peers, 2) + cell],
-        [SMEM] + [VMEM] * 12,
-        table, coef, lam, moved_0, wind, sea, held, cells, wind_1, *from_columns, *from_rows,
-        scratch=[scratch(*cols), masks, scratch(2 * local, *cell), scratch(2, tiles, ny)],
-        us=3,
+        [whole, cols, (peers, 2) + cell],
+        [SMEM] + [VMEM] * 9,
+        table, coef, flow, base, moved_0, wind, cells, wind_1, *from_columns,
+        scratch=[scratch(*cols), scratch(*cols), scratch(2 * local, *cell), scratch(2, tiles, ny)],
     )
     got = lax.all_to_all(slots, "sa", 0, 0)
-    lam, *edge = call(
+    decays, rests, *edge = call(
         functools.partial(lam_0_kernel, local),
-        [whole] + edges,
-        [SMEM] + [VMEM] * 5,
-        table, grown, sea, held, cells, got,
-        scratch=[masks, decays, rests, packed],
+        [by_freq, by_freq] + edges,
+        [SMEM] + [VMEM] * 6,
+        table, grown, edge_cols, sea, held, cells, got,
+        scratch=[masks],
+        us=1,
     )
     from_columns, from_rows = exchange(*edge)
-    out, wind_total = call(
+    flow, base = call(
+        functools.partial(along_x_kernel, local),
+        [whole, whole],
+        [VMEM] * 8,
+        coef, grown, sea, held, decays, rests, *from_rows,
+        scratch=[masks],
+    )
+    (wind_total,) = call(wind_kernel, [cell], [VMEM], got, us=1)
+    (out,) = call(
         back_0_kernel,
-        [(bins, nx, ny), cell],
-        [VMEM] * 9,
-        coef, lam, sea, held, got, *from_columns, *from_rows,
-        out_specs=[HBM, VMEM],
-        scratch=[scratch(*cols), scratch(*whole), masks, sems],
+        [(bins, nx, ny)],
+        [VMEM] * 5,
+        coef, flow, base, *from_columns,
+        out_specs=[HBM],
+        scratch=[scratch(*cols), scratch(*whole), sems],
     )
     return out.reshape(local, dirs, nx, ny), wind_total
 

time: 96.9 us -> 96.5 us (level)
  waiting for transfers between devices: 2.32 us -> 0.58 us
  Pallas kernels: 16.4 us -> 17.7 us
    ppermute x6, waiting for transfers between devices: 2.27 us -> 0.56 us  [swap(): lax.ppermute(near, axis, pairs(0))]
    pallas_call x7 -> x10, Pallas kernels: 16.4 us -> 17.7 us  [call(): pl.pallas_call(body, out_shape=[jax.ShapeDtypeStruct(shape, F32) for shap...]
  transfers between devices with their start and end apart: 12 -> 12, of which waited for: 2 -> 1; matrix products, arithmetic and copies ran while one was open for 0% -> 0% of each run, Pallas kernels for 3% -> 5%
where the time goes in v4:
time: 96.5 us; the launch traced here: 95.9 us
  starting transfers between devices  40.1 us (42%)
  blocking collectives  36.5 us (38%)
  Pallas kernels  17.7 us (18%)
  between operations  0.97 us (1%)
    all_to_all x2, blocking collectives, shards(): got = lax.all_to_all(slots, 'sa', 0, 0)  36.5 us
    ppermute x6, starting transfers between devices, swap(): lax.ppermute(far, axis, pairs(1))  25.6 us
    pallas_call x10, Pallas kernels, call(): pl.pallas_call(body, out_shape=[jax.ShapeDtypeStruct(shape, F32) for shap...  17.7 us
    ppermute x6, starting transfers between devices, swap(): lax.ppermute(near, axis, pairs(0))  14.5 us
  transfers between devices with their start and end apart: 12, of which 1 were waited for; matrix products, arithmetic and copies ran while one was open for 0% of the time, Pallas kernels for 5%

profile of v4, /device:TPU:57, one launch (start us, length us, event | category | flops | bytes accessed | tf_op | source)
XLA Modules:
  0.0 95.9 jit_solution(10786354949627578606)
XLA Ops:
  0.6 0.0 copy-start
  0.6 0.0 copy-start.3
  0.7 0.0 copy-start.5
  0.7 0.0 copy-start.6
  0.7 0.0 copy-start.7
  0.7 2.6 %shard_map.105 = (f32[2,16,144,128]{3,2,1,0:T(8,128)S(1)}, f32[2,144,128]{2,1,0:T(8,128)S(1)}, f32[2,144,128]{2,1,0:T(8,128)S(1)}, f32[2,5,8,128]{3,2,1,0:T(8,128)S(1)}) custom-call(f32[2,144,16,128]{3,2,1,0:T(8,128)} %bitcast.4), custom_call_target="tpu_custom_call" | custom-call | flops 2000000 | bytes 2000000 | tf_op jit(solution)/shard_map/pallas_call | solution.py:508
  3.3 0.0 copy-start.1
  3.3 0.0 copy-start.2
  3.3 0.0 copy-start.4
  3.3 3.1 %collective-permute-start.2 = (f32[2,144,128]{2,1,0:T(8,128)S(1)}, f32[2,144,128]{2,1,0:T(8,128)S(1)}, u32[]{:S(2)}, u32[]{:S(2)}) collective-permute-start(f32[2,144,128]{2,1,0:T(8,128)S(1)} %get-tuple-element.36), channel_id=1, source_target_pairs={{0,32},{32,0},{64,96},{96,64},{128,160},{160,128},{192,224},{224,1... | collective-permute-start | bytes 442376 | tf_op jit(solution)/shard_map/ppermute | solution.py:499
  6.4 2.6 %collective-permute-start.3 = (f32[2,144,128]{2,1,0:T(8,128)S(1)}, f32[2,144,128]{2,1,0:T(8,128)S(1)}, u32[]{:S(2)}, u32[]{:S(2)}) collective-permute-start(f32[2,144,128]{2,1,0:T(8,128)S(1)} %get-tuple-element.37), channel_id=1, source_target_pairs={{32,64},{64,32},{96,128},{128,96},{160,192},{192,160},{224,256},{2... | collective-permute-start | bytes 442376 | tf_op jit(solution)/shard_map/ppermute | solution.py:499
  9.0 5.5 %collective-permute-start.1 = (f32[2,5,8,128]{3,2,1,0:T(8,128)S(1)}, f32[2,5,8,128]{3,2,1,0:T(8,128)S(1)}, u32[]{:S(2)}, u32[]{:S(2)}) collective-permute-start(f32[2,5,8,128]{3,2,1,0:T(8,128)S(1)} %get-tuple-element.35), channel_id=1, source_target_pairs={{8,16},{16,8},{9,17},{17,9},{10,18},{18,10},{11,19},{19,11},{12,20... | collective-permute-start | bytes 122888 | tf_op jit(solution)/shard_map/ppermute | solution.py:499
  14.5 1.9 %collective-permute-start = (f32[2,5,8,128]{3,2,1,0:T(8,128)S(1)}, f32[2,5,8,128]{3,2,1,0:T(8,128)S(1)}, u32[]{:S(2)}, u32[]{:S(2)}) collective-permute-start(f32[2,5,8,128]{3,2,1,0:T(8,128)S(1)} %get-tuple-element.35), channel_id=1, source_target_pairs={{0,8},{8,0},{16,24},{24,16},{1,9},{9,1},{17,25},{25,17},{2,10},{10... | collective-permute-start | bytes 122888 | tf_op jit(solution)/shard_map/ppermute | solution.py:499
  16.4 0.0 copy-done
  16.4 0.0 copy-done.3
  16.4 0.0 copy-done.5
  16.4 0.0 copy-done.6
  16.4 0.0 copy-done.7
  16.4 3.3 %shard_map.104 = (f32[6,144,128]{2,1,0:T(8,128)S(1)}, f32[16,144,128]{2,1,0:T(8,128)S(1)}, f32[5,8,128]{2,1,0:T(8,128)S(1)}) custom-call(f32[4,36]{1,0:T(4,128)S(1)} %copy-done.6, f32[2,4,36]{2,1,0:T(4,128)S(1)} %copy-done.5, s32[4,36]{1,0:T(4,128)S(1)} %copy-done.7, f32[144,16,128]{2,1,0:T(8,128)S(1)} %bitcast.3, f32[16,128]{1,0:T(8,128)S(1)} %copy-done.3), custom_call_target="tpu_custom_call" | custom-call | flops 2000000 | bytes 2000000 | tf_op jit(solution)/shard_map/pallas_call | solution.py:508
  19.8 0.0 collective-permute-done.1.far_cols
  19.8 0.0 collective-permute-done.near_cols
  19.8 0.0 collective-permute-done.2.near_rows
  19.8 0.0 collective-permute-done.3.far_rows
  19.8 0.0 copy-done.1
  19.8 0.0 copy-done.2
  19.8 0.0 copy-done.4
  19.9 3.3 %shard_map.106 = (f32[8,8,16,128]{3,2,1,0:T(8,128)S(1)}, f32[4,16,128]{2,1,0:T(8,128)S(1)}, f32[16,144,128]{2,1,0:T(8,128)S(1)}) custom-call(f32[2,32]{1,0:T(2,128)S(1)} %copy-done.4, f32[6,144,128]{2,1,0:T(8,128)S(1)} %get-tuple-element.31.coef, f32[2,16,144,128]{3,2,1,0:T(8,128)S(1)} %get-tuple-element.34.laid, ...), custom_call_target="tpu_custom_call" | custom-call | flops 4000000 | bytes 4000000 | tf_op jit(solution)/shard_map/pallas_call | solution.py:508
  23.1 26.2 %all_to_all.10.got = f32[8,8,16,128]{3,2,1,0:T(8,128)S(1)} all-to-all(f32[8,8,16,128]{3,2,1,0:T(8,128)S(1)} %get-tuple-element.38), channel_id=1, replica_groups=mesh['gx'=16,'gy'=4,'sa'=8] {'sa'}, dimensions={0} | all-to-all | bytes 1048576 | tf_op jit(solution)/shard_map/all_to_all | solution.py:559
  49.3 0.8 shard_map.107
  50.1 3.7 %collective-permute-start.4 = (f32[144,128]{1,0:T(8,128)S(1)}, f32[144,128]{1,0:T(8,128)S(1)}, u32[]{:S(2)}, u32[]{:S(2)}) collective-permute-start(f32[144,128]{1,0:T(8,128)S(1)} %get-tuple-element.42), channel_id=1, source_target_pairs={{0,32},{32,0},{64,96},{96,64},{128,160},{160,128},{192,224},{224,1... | collective-permute-start | bytes 221192 | tf_op jit(solution)/shard_map/ppermute | solution.py:499
  53.8 2.8 %collective-permute-start.5 = (f32[144,128]{1,0:T(8,128)S(1)}, f32[144,128]{1,0:T(8,128)S(1)}, u32[]{:S(2)}, u32[]{:S(2)}) collective-permute-start(f32[144,128]{1,0:T(8,128)S(1)} %get-tuple-element.43), channel_id=1, source_target_pairs={{32,64},{64,32},{96,128},{128,96},{160,192},{192,160},{224,256},{2... | collective-permute-start | bytes 221192 | tf_op jit(solution)/shard_map/ppermute | solution.py:499
  56.6 4.9 %collective-permute-start.7 = (f32[5,8,128]{2,1,0:T(8,128)S(1)}, f32[5,8,128]{2,1,0:T(8,128)S(1)}, u32[]{:S(2)}, u32[]{:S(2)}) collective-permute-start(f32[5,8,128]{2,1,0:T(8,128)S(1)} %get-tuple-element.49), channel_id=1, source_target_pairs={{8,16},{16,8},{9,17},{17,9},{10,18},{18,10},{11,19},{19,11},{12,20... | collective-permute-start | bytes 61448 | tf_op jit(solution)/shard_map/ppermute | solution.py:499
  61.5 1.9 %collective-permute-start.6 = (f32[5,8,128]{2,1,0:T(8,128)S(1)}, f32[5,8,128]{2,1,0:T(8,128)S(1)}, u32[]{:S(2)}, u32[]{:S(2)}) collective-permute-start(f32[5,8,128]{2,1,0:T(8,128)S(1)} %get-tuple-element.49), channel_id=1, source_target_pairs={{0,8},{8,0},{16,24},{24,16},{1,9},{9,1},{17,25},{25,17},{2,10},{10... | collective-permute-start | bytes 61448 | tf_op jit(solution)/shard_map/ppermute | solution.py:499
  63.4 0.0 collective-permute-done.4.near_rows
  63.4 0.0 collective-permute-done.5.far_rows
  63.5 0.6 shard_map.108
  64.0 0.0 collective-permute-done.7.far_cols
  64.0 0.6 collective-permute-done.6.near_cols
  64.6 3.4 %shard_map.109 = (f32[16,144,128]{2,1,0:T(8,128)S(1)}, f32[5,8,128]{2,1,0:T(8,128)S(1)}, f32[8,2,16,128]{3,2,1,0:T(8,128)S(1)}) custom-call(f32[2,32]{1,0:T(2,128)S(1)} %copy-done.4, f32[6,144,128]{2,1,0:T(8,128)S(1)} %get-tuple-element.31.coef, f32[16,144,128]{2,1,0:T(8,128)S(1)} %get-tuple-element.44.flow, f32[16,144,128]{2,1,0:T(8,128)S(1)} %get-tuple-element.45.base, ...), custom_call_target="tpu_custom_call" | custom-call | flops 2000000 | bytes 2000000 | tf_op jit(solution)/shard_map/pallas_call | solution.py:508
  68.0 10.4 %all_to_all.11.got = f32[8,2,16,128]{3,2,1,0:T(8,128)S(1)} all-to-all(f32[8,2,16,128]{3,2,1,0:T(8,128)S(1)} %get-tuple-element.52), channel_id=1, replica_groups=mesh['gx'=16,'gy'=4,'sa'=8] {'sa'}, dimensions={0} | all-to-all | bytes 262144 | tf_op jit(solution)/shard_map/all_to_all | solution.py:584
  78.4 0.8 shard_map.110
  79.1 1.9 %collective-permute-start.8 = (f32[144,128]{1,0:T(8,128)S(1)}, f32[144,128]{1,0:T(8,128)S(1)}, u32[]{:S(2)}, u32[]{:S(2)}) collective-permute-start(f32[144,128]{1,0:T(8,128)S(1)} %get-tuple-element.55), channel_id=1, source_target_pairs={{0,32},{32,0},{64,96},{96,64},{128,160},{160,128},{192,224},{224,1... | collective-permute-start | bytes 221192 | tf_op jit(solution)/shard_map/ppermute | solution.py:499
  81.1 4.7 %collective-permute-start.9 = (f32[144,128]{1,0:T(8,128)S(1)}, f32[144,128]{1,0:T(8,128)S(1)}, u32[]{:S(2)}, u32[]{:S(2)}) collective-permute-start(f32[144,128]{1,0:T(8,128)S(1)} %get-tuple-element.56), channel_id=1, source_target_pairs={{32,64},{64,32},{96,128},{128,96},{160,192},{192,160},{224,256},{2... | collective-permute-start | bytes 221192 | tf_op jit(solution)/shard_map/ppermute | solution.py:499
  85.8 5.1 %collective-permute-start.11 = (f32[5,8,128]{2,1,0:T(8,128)S(1)}, f32[5,8,128]{2,1,0:T(8,128)S(1)}, u32[]{:S(2)}, u32[]{:S(2)}) collective-permute-start(f32[5,8,128]{2,1,0:T(8,128)S(1)} %get-tuple-element.59), channel_id=1, source_target_pairs={{8,16},{16,8},{9,17},{17,9},{10,18},{18,10},{11,19},{19,11},{12,20... | collective-permute-start | bytes 61448 | tf_op jit(solution)/shard_map/ppermute | solution.py:499
  90.9 1.9 %collective-permute-start.10 = (f32[5,8,128]{2,1,0:T(8,128)S(1)}, f32[5,8,128]{2,1,0:T(8,128)S(1)}, u32[]{:S(2)}, u32[]{:S(2)}) collective-permute-start(f32[5,8,128]{2,1,0:T(8,128)S(1)} %get-tuple-element.59), channel_id=1, source_target_pairs={{0,8},{8,0},{16,24},{24,16},{1,9},{9,1},{17,25},{25,17},{2,10},{10... | collective-permute-start | bytes 61448 | tf_op jit(solution)/shard_map/ppermute | solution.py:499
  92.9 0.6 shard_map.113
  93.5 0.0 collective-permute-done.8.near_rows
  93.5 0.0 collective-permute-done.9.far_rows
  93.5 0.6 shard_map.111
  94.1 0.0 collective-permute-done.11.far_cols
  94.1 0.0 collective-permute-done.10.near_cols
  94.1 1.8 %shard_map.112 = f32[144,16,128]{2,1,0:T(8,128)} custom-call(f32[6,144,128]{2,1,0:T(8,128)S(1)} %get-tuple-element.31.coef, f32[16,144,128]{2,1,0:T(8,128)S(1)} %get-tuple-element.57.flow, f32[16,144,128]{2,1,0:T(8,128)S(1)} %get-tuple-element.58.base, f32[5,8,128]{2,1,0:T(8,128)S(1)} %collective-permute-done.10.near_cols, ...), custom_call_target="tpu_custom_call" | custom-call | flops 2000000 | bytes 2000000 | tf_op jit(solution)/shard_map/pallas_call | solution.py:508
Async XLA Ops:
  0.6 15.8 %copy-start = (f32[4,36,16,128]{3,2,1,0:T(8,128)S(1)}, f32[4,36,16,128]{3,2,1,0:T(8,128)}, u32[]{:S(2)}) copy-start(f32[4,36,16,128]{3,2,1,0:T(8,128)} %param.10) | copy-start | bytes 3538948
  0.6 15.8 %copy-start.3 = (f32[16,128]{1,0:T(8,128)S(1)}, f32[16,128]{1,0:T(8,128)}, u32[]{:S(2)}) copy-start(f32[16,128]{1,0:T(8,128)} %wind.3) | copy-start | bytes 24580
  0.7 15.8 %copy-start.5 = (f32[2,4,36]{2,1,0:T(4,128)S(1)}, f32[2,4,36]{2,1,0:T(4,128)}, u32[]{:S(2)}) copy-start(f32[2,4,36]{2,1,0:T(4,128)} %speed.1) | copy-start | bytes 3460
  0.7 15.8 %copy-start.6 = (f32[4,36]{1,0:T(4,128)S(1)}, f32[4,36]{1,0:T(4,128)}, u32[]{:S(2)}) copy-start(f32[4,36]{1,0:T(4,128)} %growth.1) | copy-start | bytes 1732
  0.7 15.8 %copy-start.7 = (s32[4,36]{1,0:T(4,128)S(1)}, s32[4,36]{1,0:T(4,128)}, u32[]{:S(2)}) copy-start(s32[4,36]{1,0:T(4,128)} %code.1) | copy-start | bytes 1732
  3.3 16.6 %copy-start.1 = (s32[16,128]{1,0:T(8,128)S(1)}, s32[16,128]{1,0:T(8,128)}, u32[]{:S(2)}) copy-start(s32[16,128]{1,0:T(8,128)} %sea.9) | copy-start | bytes 24580
  3.3 16.6 %copy-start.2 = (s32[16,128]{1,0:T(8,128)S(1)}, s32[16,128]{1,0:T(8,128)}, u32[]{:S(2)}) copy-start(s32[16,128]{1,0:T(8,128)} %held.9) | copy-start | bytes 24580
  3.3 16.6 %copy-start.4 = (f32[2,32]{1,0:T(2,128)S(1)}, f32[2,32]{1,0:T(2,128)}, u32[]{:S(2)}) copy-start(f32[2,32]{1,0:T(2,128)} %constant.2.clone.table) | copy-start | bytes 772
  3.3 16.5 %collective-permute-start.2 = (f32[2,144,128]{2,1,0:T(8,128)S(1)}, f32[2,144,128]{2,1,0:T(8,128)S(1)}, u32[]{:S(2)}, u32[]{:S(2)}) collective-permute-start(f32[2,144,128]{2,1,0:T(8,128)S(1)} %get-tuple-element.36), channel_id=1, source_target_pairs={{0,32},{32,0},{64,96},{96,64},{128,160},{160,128},{192,224},{224,1... | collective-permute-start | bytes 442376 | tf_op jit(solution)/shard_map/ppermute | solution.py:499
  6.4 13.4 %collective-permute-start.3 = (f32[2,144,128]{2,1,0:T(8,128)S(1)}, f32[2,144,128]{2,1,0:T(8,128)S(1)}, u32[]{:S(2)}, u32[]{:S(2)}) collective-permute-start(f32[2,144,128]{2,1,0:T(8,128)S(1)} %get-tuple-element.37), channel_id=1, source_target_pairs={{32,64},{64,32},{96,128},{128,96},{160,192},{192,160},{224,256},{2... | collective-permute-start | bytes 442376 | tf_op jit(solution)/shard_map/ppermute | solution.py:499
  9.0 10.8 %collective-permute-start.1 = (f32[2,5,8,128]{3,2,1,0:T(8,128)S(1)}, f32[2,5,8,128]{3,2,1,0:T(8,128)S(1)}, u32[]{:S(2)}, u32[]{:S(2)}) collective-permute-start(f32[2,5,8,128]{3,2,1,0:T(8,128)S(1)} %get-tuple-element.35), channel_id=1, source_target_pairs={{8,16},{16,8},{9,17},{17,9},{10,18},{18,10},{11,19},{19,11},{12,20... | collective-permute-start | bytes 122888 | tf_op jit(solution)/shard_map/ppermute | solution.py:499
  14.5 5.3 %collective-permute-start = (f32[2,5,8,128]{3,2,1,0:T(8,128)S(1)}, f32[2,5,8,128]{3,2,1,0:T(8,128)S(1)}, u32[]{:S(2)}, u32[]{:S(2)}) collective-permute-start(f32[2,5,8,128]{3,2,1,0:T(8,128)S(1)} %get-tuple-element.35), channel_id=1, source_target_pairs={{0,8},{8,0},{16,24},{24,16},{1,9},{9,1},{17,25},{25,17},{2,10},{10... | collective-permute-start | bytes 122888 | tf_op jit(solution)/shard_map/ppermute | solution.py:499
  50.1 13.3 %collective-permute-start.4 = (f32[144,128]{1,0:T(8,128)S(1)}, f32[144,128]{1,0:T(8,128)S(1)}, u32[]{:S(2)}, u32[]{:S(2)}) collective-permute-start(f32[144,128]{1,0:T(8,128)S(1)} %get-tuple-element.42), channel_id=1, source_target_pairs={{0,32},{32,0},{64,96},{96,64},{128,160},{160,128},{192,224},{224,1... | collective-permute-start | bytes 221192 | tf_op jit(solution)/shard_map/ppermute | solution.py:499
  53.8 9.6 %collective-permute-start.5 = (f32[144,128]{1,0:T(8,128)S(1)}, f32[144,128]{1,0:T(8,128)S(1)}, u32[]{:S(2)}, u32[]{:S(2)}) collective-permute-start(f32[144,128]{1,0:T(8,128)S(1)} %get-tuple-element.43), channel_id=1, source_target_pairs={{32,64},{64,32},{96,128},{128,96},{160,192},{192,160},{224,256},{2... | collective-permute-start | bytes 221192 | tf_op jit(solution)/shard_map/ppermute | solution.py:499
  56.6 7.5 %collective-permute-start.7 = (f32[5,8,128]{2,1,0:T(8,128)S(1)}, f32[5,8,128]{2,1,0:T(8,128)S(1)}, u32[]{:S(2)}, u32[]{:S(2)}) collective-permute-start(f32[5,8,128]{2,1,0:T(8,128)S(1)} %get-tuple-element.49), channel_id=1, source_target_pairs={{8,16},{16,8},{9,17},{17,9},{10,18},{18,10},{11,19},{19,11},{12,20... | collective-permute-start | bytes 61448 | tf_op jit(solution)/shard_map/ppermute | solution.py:499
  61.5 3.1 %collective-permute-start.6 = (f32[5,8,128]{2,1,0:T(8,128)S(1)}, f32[5,8,128]{2,1,0:T(8,128)S(1)}, u32[]{:S(2)}, u32[]{:S(2)}) collective-permute-start(f32[5,8,128]{2,1,0:T(8,128)S(1)} %get-tuple-element.49), channel_id=1, source_target_pairs={{0,8},{8,0},{16,24},{24,16},{1,9},{9,1},{17,25},{25,17},{2,10},{10... | collective-permute-start | bytes 61448 | tf_op jit(solution)/shard_map/ppermute | solution.py:499
  79.1 14.4 %collective-permute-start.8 = (f32[144,128]{1,0:T(8,128)S(1)}, f32[144,128]{1,0:T(8,128)S(1)}, u32[]{:S(2)}, u32[]{:S(2)}) collective-permute-start(f32[144,128]{1,0:T(8,128)S(1)} %get-tuple-element.55), channel_id=1, source_target_pairs={{0,32},{32,0},{64,96},{96,64},{128,160},{160,128},{192,224},{224,1... | collective-permute-start | bytes 221192 | tf_op jit(solution)/shard_map/ppermute | solution.py:499
  81.1 12.4 %collective-permute-start.9 = (f32[144,128]{1,0:T(8,128)S(1)}, f32[144,128]{1,0:T(8,128)S(1)}, u32[]{:S(2)}, u32[]{:S(2)}) collective-permute-start(f32[144,128]{1,0:T(8,128)S(1)} %get-tuple-element.56), channel_id=1, source_target_pairs={{32,64},{64,32},{96,128},{128,96},{160,192},{192,160},{224,256},{2... | collective-permute-start | bytes 221192 | tf_op jit(solution)/shard_map/ppermute | solution.py:499
  85.8 8.3 %collective-permute-start.11 = (f32[5,8,128]{2,1,0:T(8,128)S(1)}, f32[5,8,128]{2,1,0:T(8,128)S(1)}, u32[]{:S(2)}, u32[]{:S(2)}) collective-permute-start(f32[5,8,128]{2,1,0:T(8,128)S(1)} %get-tuple-element.59), channel_id=1, source_target_pairs={{8,16},{16,8},{9,17},{17,9},{10,18},{18,10},{11,19},{19,11},{12,20... | collective-permute-start | bytes 61448 | tf_op jit(solution)/shard_map/ppermute | solution.py:499
  90.9 3.2 %collective-permute-start.10 = (f32[5,8,128]{2,1,0:T(8,128)S(1)}, f32[5,8,128]{2,1,0:T(8,128)S(1)}, u32[]{:S(2)}, u32[]{:S(2)}) collective-permute-start(f32[5,8,128]{2,1,0:T(8,128)S(1)} %get-tuple-element.59), channel_id=1, source_target_pairs={{0,8},{8,0},{16,24},{24,16},{1,9},{9,1},{17,25},{25,17},{2,10},{10... | collective-permute-start | bytes 61448 | tf_op jit(solution)/shard_map/ppermute | solution.py:499

commit v5 on v4

--- a/solution.py
+++ b/solution.py
@@ -26,7 +26,7 @@
 SMEM = pl.BlockSpec(memory_space=pltpu.SMEM)
 HBM = pl.BlockSpec(memory_space=pltpu.HBM)
 
-STAY, FROM_PREV_X, FROM_NEXT_X, FROM_PREV_Y, FROM_NEXT_Y, GROWTH = range(6)
+STAY, FROM_PREV_X, FROM_NEXT_X, FROM_PREV_Y, FROM_NEXT_Y, GROWTH, EDGE_Y, BACK_EDGE_Y = range(8)
 
 
 def bin_constants(table, f, local):
@@ -110,13 +110,15 @@
         out[g] = jnp.where(lane % 2 == 0, pltpu.roll(before, 1, 1), pltpu.roll(after, 127, 1))
 
 
-def along_lanes(value, columns, r, t):
+def along_lanes(value):
     lane = lanes_of(value.shape)
-    at = column_lane(r, t)
-    edge = pltpu.roll(columns[t // PACK], lax.rem(128 - at, 128), 1)
-    before = jnp.where(lane == 0, edge, pltpu.roll(value, 1, 1))
-    after = jnp.where(lane == 127, edge, pltpu.roll(value, 127, 1))
+    before = jnp.where(lane == 0, 0.0, pltpu.roll(value, 1, 1))
+    after = jnp.where(lane == 127, 0.0, pltpu.roll(value, 127, 1))
     return before, after
+
+
+def from_outside(columns, r, t):
+    return pltpu.roll(columns[t // PACK], (128 - column_lane(r, t)) % 128, 1)
 
 
 def put_rows(near_rows, far_rows, t, value, first, last):
@@ -225,6 +227,11 @@
         return carry
 
     lax.fori_loop(0, DIRS, fill, 0)
+    lane = lanes_of((TILE, lanes))
+    for t in range(bins // TILE):
+        before, after = coef[FROM_PREV_Y, span(t), :], coef[FROM_NEXT_Y, span(t), :]
+        coef[EDGE_Y, span(t), :] = jnp.where(lane == 0, before, jnp.where(lane == 127, after, 0.0))
+        coef[BACK_EDGE_Y, span(t), :] = jnp.where(lane == 0, after, jnp.where(lane == 127, before, 0.0))
     packed = [jnp.zeros((TILE, lanes), F32)] * edge_cols.shape[0]
     for r in range(rows):
         if r % WAITS == 0:
@@ -239,55 +246,55 @@
         edge_cols[g] = packed[g]
 
 
-def moved_of(laid, near_rows, far_rows, columns, coef, s1, s2, r, t, first, last):
-    value = laid[r, span(t), :]
-    prev_x = row_halo(near_rows, far_rows, t, True) if first else laid[r - 1, span(t), :]
-    next_x = row_halo(near_rows, far_rows, t, False) if last else laid[r + 1, span(t), :]
-    prev_y, next_y = along_lanes(value, columns, r, t)
-    flow = (
-        coef[STAY, span(t), :] * value
-        + coef[FROM_PREV_X, span(t), :] * prev_x
-        + coef[FROM_NEXT_X, span(t), :] * next_x
-        + coef[FROM_PREV_Y, span(t), :] * prev_y
-        + coef[FROM_NEXT_Y, span(t), :] * next_y
-    )
-    return s1 * flow + s2 * value
-
-
-def forward_row(local, coef, laid, grown, masks, halos, columns, sums, moved_0, r, first, last):
-    bins = laid.shape[2]
-    s1, s2 = row_of(masks.at[0], r), row_of(masks.at[1], r)
-    parts = [[jnp.zeros((TILE, 128), F32)] * local for _ in range(4)]
-    for t in range(bins // TILE):
-        early, later = (
-            moved_of(laid.at[s], *(h.at[s] for h in halos), columns.at[s], coef, s1, s2, r, t, first, last)
-            for s in range(2)
-        )
-        moved_0[span(t), :] = early
-        term = grown[r, span(t), :] * later
-        values = later, early, term, coef[GROWTH, span(t), :] * term
-        for part, value in zip(parts, values):
-            accumulate(part, t, value)
-    for i, part in enumerate(parts):
-        for f in range(local):
-            sums[i * local + f, tile_at(r), :] = part[f]
-
-
-def forward_kernel(
-    local, table, coef, laid, grown, sea, held, near_cols, far_cols, near_rows, far_rows,
-    slots, wind_parts, moved_0, joined, masks, sums,
-):
-    _, rows, _, _ = laid.shape
+def inner_forward_kernel(coef, laid, sea, held, near_rows, far_rows, base, masks):
+    steps, rows, bins, _ = laid.shape
     set_masks(sea, held, masks)
-    for s in range(2):
-        join_columns(near_cols.at[s], far_cols.at[s], joined.at[s])
 
     def body(r, first, last):
-        halos = near_rows, far_rows
-        forward_row(local, coef, laid, grown, masks, halos, joined, sums, moved_0.at[r], r, first, last)
+        s1, s2 = row_of(masks.at[0], r), row_of(masks.at[1], r)
+        for s in range(steps):
+            near, far = near_rows.at[s], far_rows.at[s]
+            for t in range(bins // TILE):
+                value = laid[s, r, span(t), :]
+                prev_x = row_halo(near, far, t, True) if first else laid[s, r - 1, span(t), :]
+                next_x = row_halo(near, far, t, False) if last else laid[s, r + 1, span(t), :]
+                prev_y, next_y = along_lanes(value)
+                flow = (
+                    coef[STAY, span(t), :] * value
+                    + coef[FROM_PREV_X, span(t), :] * prev_x
+                    + coef[FROM_NEXT_X, span(t), :] * next_x
+                    + coef[FROM_PREV_Y, span(t), :] * prev_y
+                    + coef[FROM_NEXT_Y, span(t), :] * next_y
+                )
+                base[s, r, span(t), :] = s1 * flow + s2 * value
 
     inner_rows(rows, body)
     outer_rows(rows, body)
+
+
+def forward_kernel(
+    local, table, coef, base, grown, sea, held, far_cols, near_cols, slots, wind_parts, moved_0, joined, masks, sums
+):
+    steps, rows, bins, _ = base.shape
+    set_masks(sea, held, masks)
+    for s in range(steps):
+        join_columns(near_cols.at[s], far_cols.at[s], joined.at[s])
+    for r in range(rows):
+        s1 = row_of(masks.at[0], r)
+        parts = [[jnp.zeros((TILE, 128), F32)] * local for _ in range(4)]
+        for t in range(bins // TILE):
+            edge = s1 * coef[EDGE_Y, span(t), :]
+            early, later = (
+                base[s, r, span(t), :] + edge * from_outside(joined.at[s], r, t) for s in range(steps)
+            )
+            moved_0[r, span(t), :] = early
+            term = grown[r, span(t), :] * later
+            values = later, early, term, coef[GROWTH, span(t), :] * term
+            for part, value in zip(parts, values):
+                accumulate(part, t, value)
+        for i, part in enumerate(parts):
+            for f in range(local):
+                sums[i * local + f, tile_at(r), :] = part[f]
     totals = [jnp.zeros((rows, 128), F32)] * 4
     for f in range(local):
         freq, weight = bin_constants(table, f, local)
@@ -363,8 +370,8 @@
     wind_1[...] = wind
 
 
-def along_x_kernel(
-    local, coef, grown, sea, held, decays, rests, near_rows, far_rows, flow, base, masks
+def inner_back_kernel(
+    local, coef, grown, sea, held, decays, rests, near_rows, far_rows, base, flow, masks
 ):
     rows, bins, _ = grown.shape
     tiles = bins // TILE
@@ -391,23 +398,21 @@
         for t in range(tiles):
             prev_x = row_halo(near_rows, far_rows, t, True) if first else flow[r - 1, span(t), :]
             next_x = row_halo(near_rows, far_rows, t, False) if last else flow[r + 1, span(t), :]
+            prev_y, next_y = along_lanes(flow[r, span(t), :])
             base[r, span(t), :] = (
                 base[r, span(t), :]
                 + coef[FROM_NEXT_X, span(t), :] * prev_x
                 + coef[FROM_PREV_X, span(t), :] * next_x
+                + coef[FROM_NEXT_Y, span(t), :] * prev_y
+                + coef[FROM_PREV_Y, span(t), :] * next_y
             )
 
     inner_rows(rows, body)
     outer_rows(rows, body)
 
 
-def along_y(flow, base, columns, coef, r, t):
-    prev_y, next_y = along_lanes(flow[r, span(t), :], columns, r, t)
-    return (
-        base[r, span(t), :]
-        + coef[FROM_NEXT_Y, span(t), :] * prev_y
-        + coef[FROM_PREV_Y, span(t), :] * next_y
-    )
+def complete(base, columns, coef, r, t):
+    return base[r, span(t), :] + coef[BACK_EDGE_Y, span(t), :] * from_outside(columns, r, t)
 
 
 def set_decays(local, table, q, decays):
@@ -419,43 +424,30 @@
 
 
 def back_1_kernel(
-    local, table, coef, flow, base, moved_0, wind, cells, wind_1, near_cols, far_cols,
-    grown, edge_cols, slots, joined, packed, decays, sums,
+    local, table, coef, base, moved_0, wind, cells, wind_1, far_cols, near_cols,
+    grown, edge_cols, slots, joined, decays, sums,
 ):
-    rows, bins, _ = flow.shape
+    rows, bins, _ = base.shape
     join_columns(near_cols, far_cols, joined)
     set_decays(local, table, cells[0], decays)
     zero = jnp.zeros((TILE, 128), F32)
-    groups = packed.shape[0]
-    for g in range(groups):
-        packed[g] = zero
-
-    def row(r, columns):
+    packed = [zero] * edge_cols.shape[0]
+    for r in range(rows):
         half_wind = 0.5 * row_of(wind, r)
         for_q = [row_of(decays.at[f], r) for f in range(local)]
         for_wind = [row_of(decays.at[local + f], r) for f in range(local)]
         lam_q = lam_wind = zero
         for t in range(bins // TILE):
             g = coef[GROWTH, span(t), :]
-            density = along_y(flow, base, joined, coef, r, t) * jnp.exp(half_wind * g)
+            density = complete(base, joined, coef, r, t) * jnp.exp(half_wind * g)
             grown[r, span(t), :] = density
-            pack_columns(columns, density, r, t)
+            pack_columns(packed, density, r, t)
             term = density * moved_0[r, span(t), :]
             lam_q = lam_q + pick(for_q, t) * term
             lam_wind = lam_wind + pick(for_wind, t) * (g * term)
         sums[0, tile_at(r), :] = lam_q
         sums[1, tile_at(r), :] = lam_wind
-
-    def pair(i, carry):
-        columns = [packed[g] for g in range(groups)]
-        row(2 * i, columns)
-        row(2 * i + 1, columns)
-        for g in range(groups):
-            packed[g] = columns[g]
-        return carry
-
-    lax.fori_loop(0, rows // 2, pair, 0)
-    for g in range(groups):
+    for g in range(edge_cols.shape[0]):
         edge_cols[g] = packed[g]
     lam_q, lam_wind = gathered(sums, 0), gathered(sums, 1) + wind_1[...]
     for peer in range(slots.shape[0]):
@@ -478,13 +470,13 @@
     wind_total[...] = total_of(got, 1)
 
 
-def back_0_kernel(coef, flow, base, near_cols, far_cols, out, joined, laid, sent):
-    rows, bins, _ = flow.shape
+def back_0_kernel(coef, base, far_cols, near_cols, out, joined, laid, sent):
+    rows, bins, _ = base.shape
     join_columns(near_cols, far_cols, joined)
     copies = [pltpu.make_async_copy(laid.at[r], out.at[:, r, :], sent.at[r]) for r in range(rows)]
     for r in range(rows):
         for t in range(bins // TILE):
-            laid[r, span(t), :] = along_y(flow, base, joined, coef, r, t)
+            laid[r, span(t), :] = complete(base, joined, coef, r, t)
         copies[r].start()
     for copy in copies:
         copy.wait()
@@ -496,12 +488,16 @@
     def pairs(first):
         return [(i + a, i + 1 - a) for i in range(first, count - 1, 2) for a in (0, 1)]
 
-    return lax.ppermute(near, axis, pairs(0)), lax.ppermute(far, axis, pairs(1))
+    if axis == "gy":
+        far, near = lax.ppermute(far, axis, pairs(1)), lax.ppermute(near, axis, pairs(0))
+    else:
+        near, far = lax.ppermute(near, axis, pairs(0)), lax.ppermute(far, axis, pairs(1))
+    return near, far
 
 
 def exchange(near_rows, far_rows, cols):
-    from_columns = swap(cols, cols, "gy")
-    return from_columns, swap(near_rows, far_rows, "gx")
+    near_cols, far_cols = swap(cols, cols, "gy")
+    return (far_cols, near_cols), swap(near_rows, far_rows, "gx")
 
 
 def call(body, outs, specs, *args, out_specs=None, scratch=(), us=2, mib=40):
@@ -542,19 +538,25 @@
     )
     coef, grown, edge_cols = call(
         functools.partial(prepare_kernel, local),
-        [(6,) + rows, whole, cols],
+        [(8,) + rows, whole, cols],
         [SMEM] * 3 + [HBM, VMEM],
         growth, speed, code, adjoint_seed.reshape(bins, nx, ny), wind,
         scratch=[scratch(*whole), sems],
     )
     from_columns, from_rows = exchange(*edge)
+    (base,) = call(
+        inner_forward_kernel,
+        [(steps,) + whole],
+        [VMEM] * 6,
+        coef, laid, sea, held, *from_rows,
+        scratch=[masks],
+    )
     slots, wind_parts, moved_0 = call(
         functools.partial(forward_kernel, local),
         [(peers, 4 + local) + cell, (local,) + cell, whole],
-        [SMEM] + [VMEM] * 9,
-        table, coef, laid, grown, sea, held, *from_columns, *from_rows,
+        [SMEM] + [VMEM] * 7,
+        table, coef, base, grown, sea, held, *from_columns,
         scratch=[scratch(steps, *cols), masks, scratch(4 * local, tiles, ny)],
-        us=4,
     )
     got = lax.all_to_all(slots, "sa", 0, 0)
     by_freq = (local,) + cell
@@ -567,19 +569,19 @@
         us=1,
     )
     from_columns, from_rows = exchange(*edge)
-    flow, base = call(
-        functools.partial(along_x_kernel, local),
-        [whole, whole],
+    (base,) = call(
+        functools.partial(inner_back_kernel, local),
+        [whole],
         [VMEM] * 8,
         coef, grown, sea, held, decays, rests, *from_rows,
-        scratch=[masks],
+        scratch=[scratch(*whole), masks],
     )
     grown, edge_cols, slots = call(
         functools.partial(back_1_kernel, local),
         [whole, cols, (peers, 2) + cell],
-        [SMEM] + [VMEM] * 9,
-        table, coef, flow, base, moved_0, wind, cells, wind_1, *from_columns,
-        scratch=[scratch(*cols), scratch(*cols), scratch(2 * local, *cell), scratch(2, tiles, ny)],
+        [SMEM] + [VMEM] * 8,
+        table, coef, base, moved_0, wind, cells, wind_1, *from_columns,
+        scratch=[scratch(*cols), scratch(2 * local, *cell), scratch(2, tiles, ny)],
     )
     got = lax.all_to_all(slots, "sa", 0, 0)
     decays, rests, *edge = call(
@@ -591,19 +593,19 @@
         us=1,
     )
     from_columns, from_rows = exchange(*edge)
-    flow, base = call(
-        functools.partial(along_x_kernel, local),
-        [whole, whole],
+    (base,) = call(
+        functools.partial(inner_back_kernel, local),
+        [whole],
         [VMEM] * 8,
         coef, grown, sea, held, decays, rests, *from_rows,
-        scratch=[masks],
+        scratch=[scratch(*whole), masks],
     )
     (wind_total,) = call(wind_kernel, [cell], [VMEM], got, us=1)
     (out,) = call(
         back_0_kernel,
         [(bins, nx, ny)],
-        [VMEM] * 5,
-        coef, flow, base, *from_columns,
+        [VMEM] * 4,
+        coef, base, *from_columns,
         out_specs=[HBM],
         scratch=[scratch(*cols), scratch(*whole), sems],
     )

time: 96.5 us -> 95.3 us (0.988)
    pallas_call x10 -> x11, Pallas kernels: 17.7 us -> 17.5 us  [call(): pl.pallas_call(body, out_shape=[jax.ShapeDtypeStruct(shape, F32) for shap...]
  transfers between devices with their start and end apart: 12 -> 12, of which waited for: 1 -> 0; matrix products, arithmetic and copies ran while one was open for 0% -> 0% of each run, Pallas kernels for 5% -> 10%
where the time goes in v5:
time: 95.3 us; the launch traced here: 94.8 us
  starting transfers between devices  40 us (42%)
  blocking collectives  36.3 us (38%)
  Pallas kernels  17.5 us (18%)
  between operations  1 us (1%)
    all_to_all x2, blocking collectives, shards(): got = lax.all_to_all(slots, 'sa', 0, 0)  36.3 us
    ppermute x6, starting transfers between devices, swap(): lax.ppermute(far, axis, pairs(1))  25.6 us
    pallas_call x11, Pallas kernels, call(): pl.pallas_call(body, out_shape=[jax.ShapeDtypeStruct(shape, F32) for shap...  17.5 us
    ppermute x6, starting transfers between devices, swap(): lax.ppermute(near, axis, pairs(0))  14.4 us
  transfers between devices with their start and end apart: 12, of which 0 were waited for; matrix products, arithmetic and copies ran while one was open for 0% of the time, Pallas kernels for 10%

profile of v5, /device:TPU:57, one launch (start us, length us, event | category | flops | bytes accessed | tf_op | source)
XLA Modules:
  0.0 94.8 jit_solution(8218773518332869646)
XLA Ops:
  0.6 0.0 copy-start
  0.6 0.0 copy-start.3
  0.7 0.0 copy-start.5
  0.7 0.0 copy-start.6
  0.7 0.0 copy-start.7
  0.7 2.6 %shard_map.105 = (f32[2,16,144,128]{3,2,1,0:T(8,128)S(1)}, f32[2,144,128]{2,1,0:T(8,128)S(1)}, f32[2,144,128]{2,1,0:T(8,128)S(1)}, f32[2,5,8,128]{3,2,1,0:T(8,128)S(1)}) custom-call(f32[2,144,16,128]{3,2,1,0:T(8,128)} %bitcast.4), custom_call_target="tpu_custom_call" | custom-call | flops 2000000 | bytes 2000000 | tf_op jit(solution)/shard_map/pallas_call | solution.py:504
  3.3 0.0 copy-start.1
  3.3 0.0 copy-start.2
  3.3 3.0 %collective-permute-start = (f32[2,144,128]{2,1,0:T(8,128)S(1)}, f32[2,144,128]{2,1,0:T(8,128)S(1)}, u32[]{:S(2)}, u32[]{:S(2)}) collective-permute-start(f32[2,144,128]{2,1,0:T(8,128)S(1)} %get-tuple-element.31), channel_id=1, source_target_pairs={{0,32},{32,0},{64,96},{96,64},{128,160},{160,128},{192,224},{224,1... | collective-permute-start | bytes 442376 | tf_op jit(solution)/shard_map/ppermute | solution.py:494
  6.3 2.6 %collective-permute-start.1 = (f32[2,144,128]{2,1,0:T(8,128)S(1)}, f32[2,144,128]{2,1,0:T(8,128)S(1)}, u32[]{:S(2)}, u32[]{:S(2)}) collective-permute-start(f32[2,144,128]{2,1,0:T(8,128)S(1)} %get-tuple-element.32), channel_id=1, source_target_pairs={{32,64},{64,32},{96,128},{128,96},{160,192},{192,160},{224,256},{2... | collective-permute-start | bytes 442376 | tf_op jit(solution)/shard_map/ppermute | solution.py:494
  8.8 5.5 %collective-permute-start.2 = (f32[2,5,8,128]{3,2,1,0:T(8,128)S(1)}, f32[2,5,8,128]{3,2,1,0:T(8,128)S(1)}, u32[]{:S(2)}, u32[]{:S(2)}) collective-permute-start(f32[2,5,8,128]{3,2,1,0:T(8,128)S(1)} %get-tuple-element.33), channel_id=1, source_target_pairs={{8,16},{16,8},{9,17},{17,9},{10,18},{18,10},{11,19},{19,11},{12,20... | collective-permute-start | bytes 122888 | tf_op jit(solution)/shard_map/ppermute | solution.py:492
  14.3 1.9 %collective-permute-start.3 = (f32[2,5,8,128]{3,2,1,0:T(8,128)S(1)}, f32[2,5,8,128]{3,2,1,0:T(8,128)S(1)}, u32[]{:S(2)}, u32[]{:S(2)}) collective-permute-start(f32[2,5,8,128]{3,2,1,0:T(8,128)S(1)} %get-tuple-element.33), channel_id=1, source_target_pairs={{0,8},{8,0},{16,24},{24,16},{1,9},{9,1},{17,25},{25,17},{2,10},{10... | collective-permute-start | bytes 122888 | tf_op jit(solution)/shard_map/ppermute | solution.py:492
  16.2 0.0 copy-done
  16.2 0.0 copy-done.3
  16.3 0.0 copy-done.5
  16.3 0.0 copy-done.6
  16.3 0.0 copy-done.7
  16.3 3.4 %shard_map.104 = (f32[8,144,128]{2,1,0:T(8,128)S(1)}, f32[16,144,128]{2,1,0:T(8,128)S(1)}, f32[5,8,128]{2,1,0:T(8,128)S(1)}) custom-call(f32[4,36]{1,0:T(4,128)S(1)} %copy-done.6, f32[2,4,36]{2,1,0:T(4,128)S(1)} %copy-done.5, s32[4,36]{1,0:T(4,128)S(1)} %copy-done.7, f32[144,16,128]{2,1,0:T(8,128)S(1)} %bitcast.3, f32[16,128]{1,0:T(8,128)S(1)} %copy-done.3), custom_call_target="tpu_custom_call" | custom-call | flops 2000000 | bytes 2000000 | tf_op jit(solution)/shard_map/pallas_call | solution.py:504
  19.6 0.0 collective-permute-done.near_rows
  19.7 0.0 collective-permute-done.1.far_rows
  19.7 0.0 copy-done.1
  19.7 0.0 copy-done.2
  19.7 0.0 copy-start.4
  19.7 2.0 %shard_map.106.base = f32[2,16,144,128]{3,2,1,0:T(8,128)S(1)} custom-call(f32[8,144,128]{2,1,0:T(8,128)S(1)} %get-tuple-element.27.coef, f32[2,16,144,128]{3,2,1,0:T(8,128)S(1)} %get-tuple-element.30.laid, s32[16,128]{1,0:T(8,128)S(1)} %copy-done.1, s32[16,128]{1,0:T(8,128)S(1)} %copy-done.2, f32[2,144,128]{2,1,0:T(8,128)S(1)} %collective-permute-done.near_rows, ...), custom_call_target="tpu_custom_call" | custom-call | flops 2000000 | bytes 2000000 | tf_op jit(solution)/shard_map/pallas_call | solution.py:504
  21.8 0.0 collective-permute-done.2.far_cols
  21.8 0.0 collective-permute-done.3.near_cols
  21.8 0.0 copy-done.4
  21.8 1.5 %shard_map.107 = (f32[8,8,16,128]{3,2,1,0:T(8,128)S(1)}, f32[4,16,128]{2,1,0:T(8,128)S(1)}, f32[16,144,128]{2,1,0:T(8,128)S(1)}) custom-call(f32[2,32]{1,0:T(2,128)S(1)} %copy-done.4, f32[8,144,128]{2,1,0:T(8,128)S(1)} %get-tuple-element.27.coef, f32[2,16,144,128]{3,2,1,0:T(8,128)S(1)} %shard_map.106.base, f32[16,144,128]{2,1,0:T(8,128)S(1)} %get-tuple-element.28.grown, ...), custom_call_target="tpu_custom_call" | custom-call | flops 2000000 | bytes 2000000 | tf_op jit(solution)/shard_map/pallas_call | solution.py:504
  23.3 26.2 %all_to_all.10.got = f32[8,8,16,128]{3,2,1,0:T(8,128)S(1)} all-to-all(f32[8,8,16,128]{3,2,1,0:T(8,128)S(1)} %get-tuple-element.34), channel_id=1, replica_groups=mesh['gx'=16,'gy'=4,'sa'=8] {'sa'}, dimensions={0} | all-to-all | bytes 1048576 | tf_op jit(solution)/shard_map/all_to_all | solution.py:561
  49.4 0.8 shard_map.108
  50.2 3.7 %collective-permute-start.4 = (f32[144,128]{1,0:T(8,128)S(1)}, f32[144,128]{1,0:T(8,128)S(1)}, u32[]{:S(2)}, u32[]{:S(2)}) collective-permute-start(f32[144,128]{1,0:T(8,128)S(1)} %get-tuple-element.38), channel_id=1, source_target_pairs={{0,32},{32,0},{64,96},{96,64},{128,160},{160,128},{192,224},{224,1... | collective-permute-start | bytes 221192 | tf_op jit(solution)/shard_map/ppermute | solution.py:494
  53.9 2.8 %collective-permute-start.5 = (f32[144,128]{1,0:T(8,128)S(1)}, f32[144,128]{1,0:T(8,128)S(1)}, u32[]{:S(2)}, u32[]{:S(2)}) collective-permute-start(f32[144,128]{1,0:T(8,128)S(1)} %get-tuple-element.39), channel_id=1, source_target_pairs={{32,64},{64,32},{96,128},{128,96},{160,192},{192,160},{224,256},{2... | collective-permute-start | bytes 221192 | tf_op jit(solution)/shard_map/ppermute | solution.py:494
  56.7 4.9 %collective-permute-start.6 = (f32[5,8,128]{2,1,0:T(8,128)S(1)}, f32[5,8,128]{2,1,0:T(8,128)S(1)}, u32[]{:S(2)}, u32[]{:S(2)}) collective-permute-start(f32[5,8,128]{2,1,0:T(8,128)S(1)} %get-tuple-element.43), channel_id=1, source_target_pairs={{8,16},{16,8},{9,17},{17,9},{10,18},{18,10},{11,19},{19,11},{12,20... | collective-permute-start | bytes 61448 | tf_op jit(solution)/shard_map/ppermute | solution.py:492
  61.6 1.9 %collective-permute-start.7 = (f32[5,8,128]{2,1,0:T(8,128)S(1)}, f32[5,8,128]{2,1,0:T(8,128)S(1)}, u32[]{:S(2)}, u32[]{:S(2)}) collective-permute-start(f32[5,8,128]{2,1,0:T(8,128)S(1)} %get-tuple-element.43), channel_id=1, source_target_pairs={{0,8},{8,0},{16,24},{24,16},{1,9},{9,1},{17,25},{25,17},{2,10},{10... | collective-permute-start | bytes 61448 | tf_op jit(solution)/shard_map/ppermute | solution.py:492
  63.6 0.0 collective-permute-done.4.near_rows
  63.6 0.0 collective-permute-done.5.far_rows
  63.6 1.6 %shard_map.109.base = f32[16,144,128]{2,1,0:T(8,128)S(1)} custom-call(f32[8,144,128]{2,1,0:T(8,128)S(1)} %get-tuple-element.27.coef, f32[16,144,128]{2,1,0:T(8,128)S(1)} %get-tuple-element.28.grown, s32[16,128]{1,0:T(8,128)S(1)} %copy-done.1, s32[16,128]{1,0:T(8,128)S(1)} %copy-done.2, f32[4,16,128]{2,1,0:T(8,128)S(1)} %get-tuple-element.36.decays, ...), custom_call_target="tpu_custom_call" | custom-call | flops 2000000 | bytes 2000000 | tf_op jit(solution)/shard_map/pallas_call | solution.py:504
  65.1 0.0 collective-permute-done.6.far_cols
  65.2 0.0 collective-permute-done.7.near_cols
  65.2 1.5 %shard_map.110 = (f32[16,144,128]{2,1,0:T(8,128)S(1)}, f32[5,8,128]{2,1,0:T(8,128)S(1)}, f32[8,2,16,128]{3,2,1,0:T(8,128)S(1)}) custom-call(f32[2,32]{1,0:T(2,128)S(1)} %copy-done.4, f32[8,144,128]{2,1,0:T(8,128)S(1)} %get-tuple-element.27.coef, f32[16,144,128]{2,1,0:T(8,128)S(1)} %shard_map.109.base, f32[16,144,128]{2,1,0:T(8,128)S(1)} %get-tuple-element.40.moved_0, ...), custom_call_target="tpu_custom_call" | custom-call | flops 2000000 | bytes 2000000 | tf_op jit(solution)/shard_map/pallas_call | solution.py:504
  66.6 10.1 %all_to_all.11.got = f32[8,2,16,128]{3,2,1,0:T(8,128)S(1)} all-to-all(f32[8,2,16,128]{3,2,1,0:T(8,128)S(1)} %get-tuple-element.46), channel_id=1, replica_groups=mesh['gx'=16,'gy'=4,'sa'=8] {'sa'}, dimensions={0} | all-to-all | bytes 262144 | tf_op jit(solution)/shard_map/all_to_all | solution.py:586
  76.8 0.8 shard_map.111
  77.5 1.9 %collective-permute-start.8 = (f32[144,128]{1,0:T(8,128)S(1)}, f32[144,128]{1,0:T(8,128)S(1)}, u32[]{:S(2)}, u32[]{:S(2)}) collective-permute-start(f32[144,128]{1,0:T(8,128)S(1)} %get-tuple-element.49), channel_id=1, source_target_pairs={{0,32},{32,0},{64,96},{96,64},{128,160},{160,128},{192,224},{224,1... | collective-permute-start | bytes 221192 | tf_op jit(solution)/shard_map/ppermute | solution.py:494
  79.5 4.5 %collective-permute-start.9 = (f32[144,128]{1,0:T(8,128)S(1)}, f32[144,128]{1,0:T(8,128)S(1)}, u32[]{:S(2)}, u32[]{:S(2)}) collective-permute-start(f32[144,128]{1,0:T(8,128)S(1)} %get-tuple-element.50), channel_id=1, source_target_pairs={{32,64},{64,32},{96,128},{128,96},{160,192},{192,160},{224,256},{2... | collective-permute-start | bytes 221192 | tf_op jit(solution)/shard_map/ppermute | solution.py:494
  84.0 5.4 %collective-permute-start.10 = (f32[5,8,128]{2,1,0:T(8,128)S(1)}, f32[5,8,128]{2,1,0:T(8,128)S(1)}, u32[]{:S(2)}, u32[]{:S(2)}) collective-permute-start(f32[5,8,128]{2,1,0:T(8,128)S(1)} %get-tuple-element.51), channel_id=1, source_target_pairs={{8,16},{16,8},{9,17},{17,9},{10,18},{18,10},{11,19},{19,11},{12,20... | collective-permute-start | bytes 61448 | tf_op jit(solution)/shard_map/ppermute | solution.py:492
  89.4 1.9 %collective-permute-start.11 = (f32[5,8,128]{2,1,0:T(8,128)S(1)}, f32[5,8,128]{2,1,0:T(8,128)S(1)}, u32[]{:S(2)}, u32[]{:S(2)}) collective-permute-start(f32[5,8,128]{2,1,0:T(8,128)S(1)} %get-tuple-element.51), channel_id=1, source_target_pairs={{0,8},{8,0},{16,24},{24,16},{1,9},{9,1},{17,25},{25,17},{2,10},{10... | collective-permute-start | bytes 61448 | tf_op jit(solution)/shard_map/ppermute | solution.py:492
  91.3 0.6 shard_map.114
  91.9 0.0 collective-permute-done.8.near_rows
  91.9 0.0 collective-permute-done.9.far_rows
  91.9 1.5 %shard_map.112.base = f32[16,144,128]{2,1,0:T(8,128)S(1)} custom-call(f32[8,144,128]{2,1,0:T(8,128)S(1)} %get-tuple-element.27.coef, f32[16,144,128]{2,1,0:T(8,128)S(1)} %get-tuple-element.44.grown, s32[16,128]{1,0:T(8,128)S(1)} %copy-done.1, s32[16,128]{1,0:T(8,128)S(1)} %copy-done.2, f32[4,16,128]{2,1,0:T(8,128)S(1)} %get-tuple-element.47.decays, ...), custom_call_target="tpu_custom_call" | custom-call | flops 2000000 | bytes 2000000 | tf_op jit(solution)/shard_map/pallas_call | solution.py:504
  93.5 0.0 collective-permute-done.10.far_cols
  93.5 0.0 collective-permute-done.11.near_cols
  93.5 1.3 %shard_map.113 = f32[144,16,128]{2,1,0:T(8,128)} custom-call(f32[8,144,128]{2,1,0:T(8,128)S(1)} %get-tuple-element.27.coef, f32[16,144,128]{2,1,0:T(8,128)S(1)} %shard_map.112.base, f32[5,8,128]{2,1,0:T(8,128)S(1)} %collective-permute-done.10.far_cols, f32[5,8,128]{2,1,0:T(8,128)S(1)} %collective-permute-done.11.near_cols), custom_call_target="tpu_custom_call" | custom-call | flops 2000000 | bytes 2000000 | tf_op jit(solution)/shard_map/pallas_call | solution.py:504
Async XLA Ops:
  0.6 15.6 %copy-start = (f32[4,36,16,128]{3,2,1,0:T(8,128)S(1)}, f32[4,36,16,128]{3,2,1,0:T(8,128)}, u32[]{:S(2)}) copy-start(f32[4,36,16,128]{3,2,1,0:T(8,128)} %param.10) | copy-start | bytes 3538948
  0.6 15.6 %copy-start.3 = (f32[16,128]{1,0:T(8,128)S(1)}, f32[16,128]{1,0:T(8,128)}, u32[]{:S(2)}) copy-start(f32[16,128]{1,0:T(8,128)} %wind.3) | copy-start | bytes 24580
  0.7 15.6 %copy-start.5 = (f32[2,4,36]{2,1,0:T(4,128)S(1)}, f32[2,4,36]{2,1,0:T(4,128)}, u32[]{:S(2)}) copy-start(f32[2,4,36]{2,1,0:T(4,128)} %speed.1) | copy-start | bytes 3460
  0.7 15.6 %copy-start.6 = (f32[4,36]{1,0:T(4,128)S(1)}, f32[4,36]{1,0:T(4,128)}, u32[]{:S(2)}) copy-start(f32[4,36]{1,0:T(4,128)} %growth.1) | copy-start | bytes 1732
  0.7 15.6 %copy-start.7 = (s32[4,36]{1,0:T(4,128)S(1)}, s32[4,36]{1,0:T(4,128)}, u32[]{:S(2)}) copy-start(s32[4,36]{1,0:T(4,128)} %code.1) | copy-start | bytes 1732
  3.3 16.4 %copy-start.1 = (s32[16,128]{1,0:T(8,128)S(1)}, s32[16,128]{1,0:T(8,128)}, u32[]{:S(2)}) copy-start(s32[16,128]{1,0:T(8,128)} %sea.11) | copy-start | bytes 24580
  3.3 16.4 %copy-start.2 = (s32[16,128]{1,0:T(8,128)S(1)}, s32[16,128]{1,0:T(8,128)}, u32[]{:S(2)}) copy-start(s32[16,128]{1,0:T(8,128)} %held.11) | copy-start | bytes 24580
  3.3 16.4 %collective-permute-start = (f32[2,144,128]{2,1,0:T(8,128)S(1)}, f32[2,144,128]{2,1,0:T(8,128)S(1)}, u32[]{:S(2)}, u32[]{:S(2)}) collective-permute-start(f32[2,144,128]{2,1,0:T(8,128)S(1)} %get-tuple-element.31), channel_id=1, source_target_pairs={{0,32},{32,0},{64,96},{96,64},{128,160},{160,128},{192,224},{224,1... | collective-permute-start | bytes 442376 | tf_op jit(solution)/shard_map/ppermute | solution.py:494
  6.3 13.4 %collective-permute-start.1 = (f32[2,144,128]{2,1,0:T(8,128)S(1)}, f32[2,144,128]{2,1,0:T(8,128)S(1)}, u32[]{:S(2)}, u32[]{:S(2)}) collective-permute-start(f32[2,144,128]{2,1,0:T(8,128)S(1)} %get-tuple-element.32), channel_id=1, source_target_pairs={{32,64},{64,32},{96,128},{128,96},{160,192},{192,160},{224,256},{2... | collective-permute-start | bytes 442376 | tf_op jit(solution)/shard_map/ppermute | solution.py:494
  8.8 12.9 %collective-permute-start.2 = (f32[2,5,8,128]{3,2,1,0:T(8,128)S(1)}, f32[2,5,8,128]{3,2,1,0:T(8,128)S(1)}, u32[]{:S(2)}, u32[]{:S(2)}) collective-permute-start(f32[2,5,8,128]{3,2,1,0:T(8,128)S(1)} %get-tuple-element.33), channel_id=1, source_target_pairs={{8,16},{16,8},{9,17},{17,9},{10,18},{18,10},{11,19},{19,11},{12,20... | collective-permute-start | bytes 122888 | tf_op jit(solution)/shard_map/ppermute | solution.py:492
  14.3 7.5 %collective-permute-start.3 = (f32[2,5,8,128]{3,2,1,0:T(8,128)S(1)}, f32[2,5,8,128]{3,2,1,0:T(8,128)S(1)}, u32[]{:S(2)}, u32[]{:S(2)}) collective-permute-start(f32[2,5,8,128]{3,2,1,0:T(8,128)S(1)} %get-tuple-element.33), channel_id=1, source_target_pairs={{0,8},{8,0},{16,24},{24,16},{1,9},{9,1},{17,25},{25,17},{2,10},{10... | collective-permute-start | bytes 122888 | tf_op jit(solution)/shard_map/ppermute | solution.py:492
  19.7 2.1 %copy-start.4 = (f32[2,32]{1,0:T(2,128)S(1)}, f32[2,32]{1,0:T(2,128)}, u32[]{:S(2)}) copy-start(f32[2,32]{1,0:T(2,128)} %constant.2.clone.table) | copy-start | bytes 772
  50.2 13.3 %collective-permute-start.4 = (f32[144,128]{1,0:T(8,128)S(1)}, f32[144,128]{1,0:T(8,128)S(1)}, u32[]{:S(2)}, u32[]{:S(2)}) collective-permute-start(f32[144,128]{1,0:T(8,128)S(1)} %get-tuple-element.38), channel_id=1, source_target_pairs={{0,32},{32,0},{64,96},{96,64},{128,160},{160,128},{192,224},{224,1... | collective-permute-start | bytes 221192 | tf_op jit(solution)/shard_map/ppermute | solution.py:494
  53.9 9.6 %collective-permute-start.5 = (f32[144,128]{1,0:T(8,128)S(1)}, f32[144,128]{1,0:T(8,128)S(1)}, u32[]{:S(2)}, u32[]{:S(2)}) collective-permute-start(f32[144,128]{1,0:T(8,128)S(1)} %get-tuple-element.39), channel_id=1, source_target_pairs={{32,64},{64,32},{96,128},{128,96},{160,192},{192,160},{224,256},{2... | collective-permute-start | bytes 221192 | tf_op jit(solution)/shard_map/ppermute | solution.py:494
  56.7 8.4 %collective-permute-start.6 = (f32[5,8,128]{2,1,0:T(8,128)S(1)}, f32[5,8,128]{2,1,0:T(8,128)S(1)}, u32[]{:S(2)}, u32[]{:S(2)}) collective-permute-start(f32[5,8,128]{2,1,0:T(8,128)S(1)} %get-tuple-element.43), channel_id=1, source_target_pairs={{8,16},{16,8},{9,17},{17,9},{10,18},{18,10},{11,19},{19,11},{12,20... | collective-permute-start | bytes 61448 | tf_op jit(solution)/shard_map/ppermute | solution.py:492
  61.6 3.5 %collective-permute-start.7 = (f32[5,8,128]{2,1,0:T(8,128)S(1)}, f32[5,8,128]{2,1,0:T(8,128)S(1)}, u32[]{:S(2)}, u32[]{:S(2)}) collective-permute-start(f32[5,8,128]{2,1,0:T(8,128)S(1)} %get-tuple-element.43), channel_id=1, source_target_pairs={{0,8},{8,0},{16,24},{24,16},{1,9},{9,1},{17,25},{25,17},{2,10},{10... | collective-permute-start | bytes 61448 | tf_op jit(solution)/shard_map/ppermute | solution.py:492
  77.5 14.4 %collective-permute-start.8 = (f32[144,128]{1,0:T(8,128)S(1)}, f32[144,128]{1,0:T(8,128)S(1)}, u32[]{:S(2)}, u32[]{:S(2)}) collective-permute-start(f32[144,128]{1,0:T(8,128)S(1)} %get-tuple-element.49), channel_id=1, source_target_pairs={{0,32},{32,0},{64,96},{96,64},{128,160},{160,128},{192,224},{224,1... | collective-permute-start | bytes 221192 | tf_op jit(solution)/shard_map/ppermute | solution.py:494
  79.5 12.5 %collective-permute-start.9 = (f32[144,128]{1,0:T(8,128)S(1)}, f32[144,128]{1,0:T(8,128)S(1)}, u32[]{:S(2)}, u32[]{:S(2)}) collective-permute-start(f32[144,128]{1,0:T(8,128)S(1)} %get-tuple-element.50), channel_id=1, source_target_pairs={{32,64},{64,32},{96,128},{128,96},{160,192},{192,160},{224,256},{2... | collective-permute-start | bytes 221192 | tf_op jit(solution)/shard_map/ppermute | solution.py:494
  84.0 9.5 %collective-permute-start.10 = (f32[5,8,128]{2,1,0:T(8,128)S(1)}, f32[5,8,128]{2,1,0:T(8,128)S(1)}, u32[]{:S(2)}, u32[]{:S(2)}) collective-permute-start(f32[5,8,128]{2,1,0:T(8,128)S(1)} %get-tuple-element.51), channel_id=1, source_target_pairs={{8,16},{16,8},{9,17},{17,9},{10,18},{18,10},{11,19},{19,11},{12,20... | collective-permute-start | bytes 61448 | tf_op jit(solution)/shard_map/ppermute | solution.py:492
  89.4 4.1 %collective-permute-start.11 = (f32[5,8,128]{2,1,0:T(8,128)S(1)}, f32[5,8,128]{2,1,0:T(8,128)S(1)}, u32[]{:S(2)}, u32[]{:S(2)}) collective-permute-start(f32[5,8,128]{2,1,0:T(8,128)S(1)} %get-tuple-element.51), channel_id=1, source_target_pairs={{0,8},{8,0},{16,24},{24,16},{1,9},{9,1},{17,25},{25,17},{2,10},{10... | collective-permute-start | bytes 61448 | tf_op jit(solution)/shard_map/ppermute | solution.py:492

commit v6 on v5

--- a/solution.py
+++ b/solution.py
@@ -13,6 +13,7 @@
 TILE = 8
 PACK = 4
 WAITS = 4
+FILL = 4
 F32 = jnp.float32
 
 steep_scale = 0.05
@@ -210,8 +211,8 @@
     for copy in copies:
         copy.start()
 
-    def fill(d, carry):
-        for f in range(local):
+    def fill(i, carry):
+        for d, f in [(i * FILL + k, f) for k in range(FILL) for f in range(local)]:
             x, y = speed[0, f, d], speed[1, f, d]
             next_x, next_y = lax.rem(code[f, d], 2) == 1, code[f, d] >= 2
             values = [
@@ -226,7 +227,7 @@
                 coef[k, pl.ds(f * DIRS + d, 1), :] = jnp.full((1, lanes), value, F32)
         return carry
 
-    lax.fori_loop(0, DIRS, fill, 0)
+    lax.fori_loop(0, DIRS // FILL, fill, 0)
     lane = lanes_of((TILE, lanes))
     for t in range(bins // TILE):
         before, after = coef[FROM_PREV_Y, span(t), :], coef[FROM_NEXT_Y, span(t), :]
@@ -466,10 +467,6 @@
     )
 
 
-def wind_kernel(got, wind_total):
-    wind_total[...] = total_of(got, 1)
-
-
 def back_0_kernel(coef, base, far_cols, near_cols, out, joined, laid, sent):
     rows, bins, _ = base.shape
     join_columns(near_cols, far_cols, joined)
@@ -600,7 +597,8 @@
         coef, grown, sea, held, decays, rests, *from_rows,
         scratch=[scratch(*whole), masks],
     )
-    (wind_total,) = call(wind_kernel, [cell], [VMEM], got, us=1)
+    got, base = lax.optimization_barrier((got, base))
+    wind_total = jnp.sum(got[:, 1], axis=0)
     (out,) = call(
         back_0_kernel,
         [(bins, nx, ny)],

time: 95.3 us -> 95.3 us (level)
    pallas_call x11 -> x10, Pallas kernels: 17.5 us -> 16.8 us  [call(): pl.pallas_call(body, out_shape=[jax.ShapeDtypeStruct(shape, F32) for shap...]
  transfers between devices with their start and end apart: 12 -> 12, of which waited for: 0 -> 0; matrix products, arithmetic and copies ran while one was open for 0% -> 1% of each run, Pallas kernels for 10% -> 9%
where the time goes in v6:
time: 95.3 us; the launch traced here: 94.7 us
  starting transfers between devices  40 us (42%)
  blocking collectives  36.3 us (38%)
  Pallas kernels  16.8 us (18%)
  between operations  1 us (1%)
    all_to_all x2, blocking collectives, shards(): got = lax.all_to_all(slots, 'sa', 0, 0)  36.3 us
    ppermute x6, starting transfers between devices, swap(): lax.ppermute(far, axis, pairs(1))  25.6 us
    pallas_call x10, Pallas kernels, call(): pl.pallas_call(body, out_shape=[jax.ShapeDtypeStruct(shape, F32) for shap...  16.8 us
    ppermute x6, starting transfers between devices, swap(): lax.ppermute(near, axis, pairs(0))  14.4 us
  transfers between devices with their start and end apart: 12, of which 0 were waited for; matrix products, arithmetic and copies ran while one was open for 1% of the time, Pallas kernels for 9%

profile of v6, /device:TPU:57, one launch (start us, length us, event | category | flops | bytes accessed | tf_op | source)
XLA Modules:
  0.0 94.7 jit_solution(7629142617369751160)
XLA Ops:
  0.6 0.0 copy-start
  0.6 0.0 copy-start.3
  0.7 0.0 copy-start.5
  0.7 0.0 copy-start.6
  0.7 0.0 copy-start.7
  0.7 2.6 %shard_map.105 = (f32[2,16,144,128]{3,2,1,0:T(8,128)S(1)}, f32[2,144,128]{2,1,0:T(8,128)S(1)}, f32[2,144,128]{2,1,0:T(8,128)S(1)}, f32[2,5,8,128]{3,2,1,0:T(8,128)S(1)}) custom-call(f32[2,144,16,128]{3,2,1,0:T(8,128)} %bitcast.4), custom_call_target="tpu_custom_call" | custom-call | flops 2000000 | bytes 2000000 | tf_op jit(solution)/shard_map/pallas_call | solution.py:501
  3.3 0.0 copy-start.1
  3.3 0.0 copy-start.2
  3.3 3.0 %collective-permute-start = (f32[2,144,128]{2,1,0:T(8,128)S(1)}, f32[2,144,128]{2,1,0:T(8,128)S(1)}, u32[]{:S(2)}, u32[]{:S(2)}) collective-permute-start(f32[2,144,128]{2,1,0:T(8,128)S(1)} %get-tuple-element.33), channel_id=1, source_target_pairs={{0,32},{32,0},{64,96},{96,64},{128,160},{160,128},{192,224},{224,1... | collective-permute-start | bytes 442376 | tf_op jit(solution)/shard_map/ppermute | solution.py:491
  6.3 2.6 %collective-permute-start.1 = (f32[2,144,128]{2,1,0:T(8,128)S(1)}, f32[2,144,128]{2,1,0:T(8,128)S(1)}, u32[]{:S(2)}, u32[]{:S(2)}) collective-permute-start(f32[2,144,128]{2,1,0:T(8,128)S(1)} %get-tuple-element.34), channel_id=1, source_target_pairs={{32,64},{64,32},{96,128},{128,96},{160,192},{192,160},{224,256},{2... | collective-permute-start | bytes 442376 | tf_op jit(solution)/shard_map/ppermute | solution.py:491
  8.8 5.5 %collective-permute-start.2 = (f32[2,5,8,128]{3,2,1,0:T(8,128)S(1)}, f32[2,5,8,128]{3,2,1,0:T(8,128)S(1)}, u32[]{:S(2)}, u32[]{:S(2)}) collective-permute-start(f32[2,5,8,128]{3,2,1,0:T(8,128)S(1)} %get-tuple-element.35), channel_id=1, source_target_pairs={{8,16},{16,8},{9,17},{17,9},{10,18},{18,10},{11,19},{19,11},{12,20... | collective-permute-start | bytes 122888 | tf_op jit(solution)/shard_map/ppermute | solution.py:489
  14.3 1.9 %collective-permute-start.3 = (f32[2,5,8,128]{3,2,1,0:T(8,128)S(1)}, f32[2,5,8,128]{3,2,1,0:T(8,128)S(1)}, u32[]{:S(2)}, u32[]{:S(2)}) collective-permute-start(f32[2,5,8,128]{3,2,1,0:T(8,128)S(1)} %get-tuple-element.35), channel_id=1, source_target_pairs={{0,8},{8,0},{16,24},{24,16},{1,9},{9,1},{17,25},{25,17},{2,10},{10... | collective-permute-start | bytes 122888 | tf_op jit(solution)/shard_map/ppermute | solution.py:489
  16.2 0.0 copy-done
  16.2 0.0 copy-done.3
  16.3 0.0 copy-done.5
  16.3 0.0 copy-done.6
  16.3 0.0 copy-done.7
  16.3 3.2 %shard_map.104 = (f32[8,144,128]{2,1,0:T(8,128)S(1)}, f32[16,144,128]{2,1,0:T(8,128)S(1)}, f32[5,8,128]{2,1,0:T(8,128)S(1)}) custom-call(f32[4,36]{1,0:T(4,128)S(1)} %copy-done.6, f32[2,4,36]{2,1,0:T(4,128)S(1)} %copy-done.5, s32[4,36]{1,0:T(4,128)S(1)} %copy-done.7, f32[144,16,128]{2,1,0:T(8,128)S(1)} %bitcast.3, f32[16,128]{1,0:T(8,128)S(1)} %copy-done.3), custom_call_target="tpu_custom_call" | custom-call | flops 2000000 | bytes 2000000 | tf_op jit(solution)/shard_map/pallas_call | solution.py:501
  19.5 0.0 collective-permute-done.near_rows
  19.6 0.0 collective-permute-done.1.far_rows
  19.6 0.0 copy-done.1
  19.6 0.0 copy-done.2
  19.6 0.0 copy-start.4
  19.6 2.0 %shard_map.106.base = f32[2,16,144,128]{3,2,1,0:T(8,128)S(1)} custom-call(f32[8,144,128]{2,1,0:T(8,128)S(1)} %get-tuple-element.29.coef, f32[2,16,144,128]{3,2,1,0:T(8,128)S(1)} %get-tuple-element.32.laid, s32[16,128]{1,0:T(8,128)S(1)} %copy-done.1, s32[16,128]{1,0:T(8,128)S(1)} %copy-done.2, f32[2,144,128]{2,1,0:T(8,128)S(1)} %collective-permute-done.near_rows, ...), custom_call_target="tpu_custom_call" | custom-call | flops 2000000 | bytes 2000000 | tf_op jit(solution)/shard_map/pallas_call | solution.py:501
  21.6 0.0 collective-permute-done.2.far_cols
  21.7 0.0 collective-permute-done.3.near_cols
  21.7 0.0 copy-done.4
  21.7 1.5 %shard_map.107 = (f32[8,8,16,128]{3,2,1,0:T(8,128)S(1)}, f32[4,16,128]{2,1,0:T(8,128)S(1)}, f32[16,144,128]{2,1,0:T(8,128)S(1)}) custom-call(f32[2,32]{1,0:T(2,128)S(1)} %copy-done.4, f32[8,144,128]{2,1,0:T(8,128)S(1)} %get-tuple-element.29.coef, f32[2,16,144,128]{3,2,1,0:T(8,128)S(1)} %shard_map.106.base, f32[16,144,128]{2,1,0:T(8,128)S(1)} %get-tuple-element.30.grown, ...), custom_call_target="tpu_custom_call" | custom-call | flops 2000000 | bytes 2000000 | tf_op jit(solution)/shard_map/pallas_call | solution.py:501
  23.1 26.2 %all_to_all.10.got = f32[8,8,16,128]{3,2,1,0:T(8,128)S(1)} all-to-all(f32[8,8,16,128]{3,2,1,0:T(8,128)S(1)} %get-tuple-element.36), channel_id=1, replica_groups=mesh['gx'=16,'gy'=4,'sa'=8] {'sa'}, dimensions={0} | all-to-all | bytes 1048576 | tf_op jit(solution)/shard_map/all_to_all | solution.py:558
  49.3 0.8 shard_map.108
  50.1 3.7 %collective-permute-start.4 = (f32[144,128]{1,0:T(8,128)S(1)}, f32[144,128]{1,0:T(8,128)S(1)}, u32[]{:S(2)}, u32[]{:S(2)}) collective-permute-start(f32[144,128]{1,0:T(8,128)S(1)} %get-tuple-element.40), channel_id=1, source_target_pairs={{0,32},{32,0},{64,96},{96,64},{128,160},{160,128},{192,224},{224,1... | collective-permute-start | bytes 221192 | tf_op jit(solution)/shard_map/ppermute | solution.py:491
  53.8 2.8 %collective-permute-start.5 = (f32[144,128]{1,0:T(8,128)S(1)}, f32[144,128]{1,0:T(8,128)S(1)}, u32[]{:S(2)}, u32[]{:S(2)}) collective-permute-start(f32[144,128]{1,0:T(8,128)S(1)} %get-tuple-element.41), channel_id=1, source_target_pairs={{32,64},{64,32},{96,128},{128,96},{160,192},{192,160},{224,256},{2... | collective-permute-start | bytes 221192 | tf_op jit(solution)/shard_map/ppermute | solution.py:491
  56.6 4.9 %collective-permute-start.6 = (f32[5,8,128]{2,1,0:T(8,128)S(1)}, f32[5,8,128]{2,1,0:T(8,128)S(1)}, u32[]{:S(2)}, u32[]{:S(2)}) collective-permute-start(f32[5,8,128]{2,1,0:T(8,128)S(1)} %get-tuple-element.45), channel_id=1, source_target_pairs={{8,16},{16,8},{9,17},{17,9},{10,18},{18,10},{11,19},{19,11},{12,20... | collective-permute-start | bytes 61448 | tf_op jit(solution)/shard_map/ppermute | solution.py:489
  61.5 1.9 %collective-permute-start.7 = (f32[5,8,128]{2,1,0:T(8,128)S(1)}, f32[5,8,128]{2,1,0:T(8,128)S(1)}, u32[]{:S(2)}, u32[]{:S(2)}) collective-permute-start(f32[5,8,128]{2,1,0:T(8,128)S(1)} %get-tuple-element.45), channel_id=1, source_target_pairs={{0,8},{8,0},{16,24},{24,16},{1,9},{9,1},{17,25},{25,17},{2,10},{10... | collective-permute-start | bytes 61448 | tf_op jit(solution)/shard_map/ppermute | solution.py:489
  63.5 0.0 collective-permute-done.4.near_rows
  63.5 0.0 collective-permute-done.5.far_rows
  63.5 1.6 %shard_map.109.base = f32[16,144,128]{2,1,0:T(8,128)S(1)} custom-call(f32[8,144,128]{2,1,0:T(8,128)S(1)} %get-tuple-element.29.coef, f32[16,144,128]{2,1,0:T(8,128)S(1)} %get-tuple-element.30.grown, s32[16,128]{1,0:T(8,128)S(1)} %copy-done.1, s32[16,128]{1,0:T(8,128)S(1)} %copy-done.2, f32[4,16,128]{2,1,0:T(8,128)S(1)} %get-tuple-element.38.decays, ...), custom_call_target="tpu_custom_call" | custom-call | flops 2000000 | bytes 2000000 | tf_op jit(solution)/shard_map/pallas_call | solution.py:501
  65.0 0.0 collective-permute-done.6.far_cols
  65.0 0.0 collective-permute-done.7.near_cols
  65.1 1.5 %shard_map.110 = (f32[16,144,128]{2,1,0:T(8,128)S(1)}, f32[5,8,128]{2,1,0:T(8,128)S(1)}, f32[8,2,16,128]{3,2,1,0:T(8,128)S(1)}) custom-call(f32[2,32]{1,0:T(2,128)S(1)} %copy-done.4, f32[8,144,128]{2,1,0:T(8,128)S(1)} %get-tuple-element.29.coef, f32[16,144,128]{2,1,0:T(8,128)S(1)} %shard_map.109.base, f32[16,144,128]{2,1,0:T(8,128)S(1)} %get-tuple-element.42.moved_0, ...), custom_call_target="tpu_custom_call" | custom-call | flops 2000000 | bytes 2000000 | tf_op jit(solution)/shard_map/pallas_call | solution.py:501
  66.5 10.1 %all_to_all.11.got = f32[8,2,16,128]{3,2,1,0:T(8,128)S(1)} all-to-all(f32[8,2,16,128]{3,2,1,0:T(8,128)S(1)} %get-tuple-element.46), channel_id=1, replica_groups=mesh['gx'=16,'gy'=4,'sa'=8] {'sa'}, dimensions={0} | all-to-all | bytes 262144 | tf_op jit(solution)/shard_map/all_to_all | solution.py:583
  76.7 0.8 shard_map.111
  77.4 1.9 %collective-permute-start.8 = (f32[144,128]{1,0:T(8,128)S(1)}, f32[144,128]{1,0:T(8,128)S(1)}, u32[]{:S(2)}, u32[]{:S(2)}) collective-permute-start(f32[144,128]{1,0:T(8,128)S(1)} %get-tuple-element.51), channel_id=1, source_target_pairs={{0,32},{32,0},{64,96},{96,64},{128,160},{160,128},{192,224},{224,1... | collective-permute-start | bytes 221192 | tf_op jit(solution)/shard_map/ppermute | solution.py:491
  79.4 4.5 %collective-permute-start.9 = (f32[144,128]{1,0:T(8,128)S(1)}, f32[144,128]{1,0:T(8,128)S(1)}, u32[]{:S(2)}, u32[]{:S(2)}) collective-permute-start(f32[144,128]{1,0:T(8,128)S(1)} %get-tuple-element.52), channel_id=1, source_target_pairs={{32,64},{64,32},{96,128},{128,96},{160,192},{192,160},{224,256},{2... | collective-permute-start | bytes 221192 | tf_op jit(solution)/shard_map/ppermute | solution.py:491
  83.9 5.4 %collective-permute-start.10 = (f32[5,8,128]{2,1,0:T(8,128)S(1)}, f32[5,8,128]{2,1,0:T(8,128)S(1)}, u32[]{:S(2)}, u32[]{:S(2)}) collective-permute-start(f32[5,8,128]{2,1,0:T(8,128)S(1)} %get-tuple-element.54), channel_id=1, source_target_pairs={{8,16},{16,8},{9,17},{17,9},{10,18},{18,10},{11,19},{19,11},{12,20... | collective-permute-start | bytes 61448 | tf_op jit(solution)/shard_map/ppermute | solution.py:489
  89.3 1.9 %collective-permute-start.11 = (f32[5,8,128]{2,1,0:T(8,128)S(1)}, f32[5,8,128]{2,1,0:T(8,128)S(1)}, u32[]{:S(2)}, u32[]{:S(2)}) collective-permute-start(f32[5,8,128]{2,1,0:T(8,128)S(1)} %get-tuple-element.54), channel_id=1, source_target_pairs={{0,8},{8,0},{16,24},{24,16},{1,9},{9,1},{17,25},{25,17},{2,10},{10... | collective-permute-start | bytes 61448 | tf_op jit(solution)/shard_map/ppermute | solution.py:489
  91.2 0.0 collective-permute-done.8.near_rows
  91.2 0.0 collective-permute-done.9.far_rows
  91.2 1.5 %shard_map.112.base = f32[16,144,128]{2,1,0:T(8,128)S(1)} custom-call(f32[8,144,128]{2,1,0:T(8,128)S(1)} %get-tuple-element.29.coef, f32[16,144,128]{2,1,0:T(8,128)S(1)} %get-tuple-element.47.grown, s32[16,128]{1,0:T(8,128)S(1)} %copy-done.1, s32[16,128]{1,0:T(8,128)S(1)} %copy-done.2, f32[4,16,128]{2,1,0:T(8,128)S(1)} %get-tuple-element.49.decays, ...), custom_call_target="tpu_custom_call" | custom-call | flops 2000000 | bytes 2000000 | tf_op jit(solution)/shard_map/pallas_call | solution.py:501
  92.8 0.6 slice_reduce_fusion
  93.4 0.0 collective-permute-done.10.far_cols
  93.4 0.0 collective-permute-done.11.near_cols
  93.4 1.3 %shard_map.113 = f32[144,16,128]{2,1,0:T(8,128)} custom-call(f32[8,144,128]{2,1,0:T(8,128)S(1)} %get-tuple-element.29.coef, f32[16,144,128]{2,1,0:T(8,128)S(1)} %shard_map.112.base, f32[5,8,128]{2,1,0:T(8,128)S(1)} %collective-permute-done.10.far_cols, f32[5,8,128]{2,1,0:T(8,128)S(1)} %collective-permute-done.11.near_cols), custom_call_target="tpu_custom_call" | custom-call | flops 2000000 | bytes 2000000 | tf_op jit(solution)/shard_map/pallas_call | solution.py:501
Async XLA Ops:
  0.6 15.6 %copy-start = (f32[4,36,16,128]{3,2,1,0:T(8,128)S(1)}, f32[4,36,16,128]{3,2,1,0:T(8,128)}, u32[]{:S(2)}) copy-start(f32[4,36,16,128]{3,2,1,0:T(8,128)} %param.10) | copy-start | bytes 3538948
  0.6 15.6 %copy-start.3 = (f32[16,128]{1,0:T(8,128)S(1)}, f32[16,128]{1,0:T(8,128)}, u32[]{:S(2)}) copy-start(f32[16,128]{1,0:T(8,128)} %wind.3) | copy-start | bytes 24580
  0.7 15.6 %copy-start.5 = (f32[2,4,36]{2,1,0:T(4,128)S(1)}, f32[2,4,36]{2,1,0:T(4,128)}, u32[]{:S(2)}) copy-start(f32[2,4,36]{2,1,0:T(4,128)} %speed.1) | copy-start | bytes 3460
  0.7 15.6 %copy-start.6 = (f32[4,36]{1,0:T(4,128)S(1)}, f32[4,36]{1,0:T(4,128)}, u32[]{:S(2)}) copy-start(f32[4,36]{1,0:T(4,128)} %growth.1) | copy-start | bytes 1732
  0.7 15.6 %copy-start.7 = (s32[4,36]{1,0:T(4,128)S(1)}, s32[4,36]{1,0:T(4,128)}, u32[]{:S(2)}) copy-start(s32[4,36]{1,0:T(4,128)} %code.1) | copy-start | bytes 1732
  3.3 16.3 %copy-start.1 = (s32[16,128]{1,0:T(8,128)S(1)}, s32[16,128]{1,0:T(8,128)}, u32[]{:S(2)}) copy-start(s32[16,128]{1,0:T(8,128)} %sea.11) | copy-start | bytes 24580
  3.3 16.3 %copy-start.2 = (s32[16,128]{1,0:T(8,128)S(1)}, s32[16,128]{1,0:T(8,128)}, u32[]{:S(2)}) copy-start(s32[16,128]{1,0:T(8,128)} %held.11) | copy-start | bytes 24580
  3.3 16.3 %collective-permute-start = (f32[2,144,128]{2,1,0:T(8,128)S(1)}, f32[2,144,128]{2,1,0:T(8,128)S(1)}, u32[]{:S(2)}, u32[]{:S(2)}) collective-permute-start(f32[2,144,128]{2,1,0:T(8,128)S(1)} %get-tuple-element.33), channel_id=1, source_target_pairs={{0,32},{32,0},{64,96},{96,64},{128,160},{160,128},{192,224},{224,1... | collective-permute-start | bytes 442376 | tf_op jit(solution)/shard_map/ppermute | solution.py:491
  6.3 13.3 %collective-permute-start.1 = (f32[2,144,128]{2,1,0:T(8,128)S(1)}, f32[2,144,128]{2,1,0:T(8,128)S(1)}, u32[]{:S(2)}, u32[]{:S(2)}) collective-permute-start(f32[2,144,128]{2,1,0:T(8,128)S(1)} %get-tuple-element.34), channel_id=1, source_target_pairs={{32,64},{64,32},{96,128},{128,96},{160,192},{192,160},{224,256},{2... | collective-permute-start | bytes 442376 | tf_op jit(solution)/shard_map/ppermute | solution.py:491
  8.8 12.8 %collective-permute-start.2 = (f32[2,5,8,128]{3,2,1,0:T(8,128)S(1)}, f32[2,5,8,128]{3,2,1,0:T(8,128)S(1)}, u32[]{:S(2)}, u32[]{:S(2)}) collective-permute-start(f32[2,5,8,128]{3,2,1,0:T(8,128)S(1)} %get-tuple-element.35), channel_id=1, source_target_pairs={{8,16},{16,8},{9,17},{17,9},{10,18},{18,10},{11,19},{19,11},{12,20... | collective-permute-start | bytes 122888 | tf_op jit(solution)/shard_map/ppermute | solution.py:489
  14.3 7.4 %collective-permute-start.3 = (f32[2,5,8,128]{3,2,1,0:T(8,128)S(1)}, f32[2,5,8,128]{3,2,1,0:T(8,128)S(1)}, u32[]{:S(2)}, u32[]{:S(2)}) collective-permute-start(f32[2,5,8,128]{3,2,1,0:T(8,128)S(1)} %get-tuple-element.35), channel_id=1, source_target_pairs={{0,8},{8,0},{16,24},{24,16},{1,9},{9,1},{17,25},{25,17},{2,10},{10... | collective-permute-start | bytes 122888 | tf_op jit(solution)/shard_map/ppermute | solution.py:489
  19.6 2.1 %copy-start.4 = (f32[2,32]{1,0:T(2,128)S(1)}, f32[2,32]{1,0:T(2,128)}, u32[]{:S(2)}) copy-start(f32[2,32]{1,0:T(2,128)} %constant.4.clone.table) | copy-start | bytes 772
  50.1 13.3 %collective-permute-start.4 = (f32[144,128]{1,0:T(8,128)S(1)}, f32[144,128]{1,0:T(8,128)S(1)}, u32[]{:S(2)}, u32[]{:S(2)}) collective-permute-start(f32[144,128]{1,0:T(8,128)S(1)} %get-tuple-element.40), channel_id=1, source_target_pairs={{0,32},{32,0},{64,96},{96,64},{128,160},{160,128},{192,224},{224,1... | collective-permute-start | bytes 221192 | tf_op jit(solution)/shard_map/ppermute | solution.py:491
  53.8 9.6 %collective-permute-start.5 = (f32[144,128]{1,0:T(8,128)S(1)}, f32[144,128]{1,0:T(8,128)S(1)}, u32[]{:S(2)}, u32[]{:S(2)}) collective-permute-start(f32[144,128]{1,0:T(8,128)S(1)} %get-tuple-element.41), channel_id=1, source_target_pairs={{32,64},{64,32},{96,128},{128,96},{160,192},{192,160},{224,256},{2... | collective-permute-start | bytes 221192 | tf_op jit(solution)/shard_map/ppermute | solution.py:491
  56.6 8.4 %collective-permute-start.6 = (f32[5,8,128]{2,1,0:T(8,128)S(1)}, f32[5,8,128]{2,1,0:T(8,128)S(1)}, u32[]{:S(2)}, u32[]{:S(2)}) collective-permute-start(f32[5,8,128]{2,1,0:T(8,128)S(1)} %get-tuple-element.45), channel_id=1, source_target_pairs={{8,16},{16,8},{9,17},{17,9},{10,18},{18,10},{11,19},{19,11},{12,20... | collective-permute-start | bytes 61448 | tf_op jit(solution)/shard_map/ppermute | solution.py:489
  61.5 3.5 %collective-permute-start.7 = (f32[5,8,128]{2,1,0:T(8,128)S(1)}, f32[5,8,128]{2,1,0:T(8,128)S(1)}, u32[]{:S(2)}, u32[]{:S(2)}) collective-permute-start(f32[5,8,128]{2,1,0:T(8,128)S(1)} %get-tuple-element.45), channel_id=1, source_target_pairs={{0,8},{8,0},{16,24},{24,16},{1,9},{9,1},{17,25},{25,17},{2,10},{10... | collective-permute-start | bytes 61448 | tf_op jit(solution)/shard_map/ppermute | solution.py:489
  77.4 13.8 %collective-permute-start.8 = (f32[144,128]{1,0:T(8,128)S(1)}, f32[144,128]{1,0:T(8,128)S(1)}, u32[]{:S(2)}, u32[]{:S(2)}) collective-permute-start(f32[144,128]{1,0:T(8,128)S(1)} %get-tuple-element.51), channel_id=1, source_target_pairs={{0,32},{32,0},{64,96},{96,64},{128,160},{160,128},{192,224},{224,1... | collective-permute-start | bytes 221192 | tf_op jit(solution)/shard_map/ppermute | solution.py:491
  79.4 11.9 %collective-permute-start.9 = (f32[144,128]{1,0:T(8,128)S(1)}, f32[144,128]{1,0:T(8,128)S(1)}, u32[]{:S(2)}, u32[]{:S(2)}) collective-permute-start(f32[144,128]{1,0:T(8,128)S(1)} %get-tuple-element.52), channel_id=1, source_target_pairs={{32,64},{64,32},{96,128},{128,96},{160,192},{192,160},{224,256},{2... | collective-permute-start | bytes 221192 | tf_op jit(solution)/shard_map/ppermute | solution.py:491
  83.9 9.5 %collective-permute-start.10 = (f32[5,8,128]{2,1,0:T(8,128)S(1)}, f32[5,8,128]{2,1,0:T(8,128)S(1)}, u32[]{:S(2)}, u32[]{:S(2)}) collective-permute-start(f32[5,8,128]{2,1,0:T(8,128)S(1)} %get-tuple-element.54), channel_id=1, source_target_pairs={{8,16},{16,8},{9,17},{17,9},{10,18},{18,10},{11,19},{19,11},{12,20... | collective-permute-start | bytes 61448 | tf_op jit(solution)/shard_map/ppermute | solution.py:489
  89.3 4.1 %collective-permute-start.11 = (f32[5,8,128]{2,1,0:T(8,128)S(1)}, f32[5,8,128]{2,1,0:T(8,128)S(1)}, u32[]{:S(2)}, u32[]{:S(2)}) collective-permute-start(f32[5,8,128]{2,1,0:T(8,128)S(1)} %get-tuple-element.54), channel_id=1, source_target_pairs={{0,8},{8,0},{16,24},{24,16},{1,9},{9,1},{17,25},{25,17},{2,10},{10... | collective-permute-start | bytes 61448 | tf_op jit(solution)/shard_map/ppermute | solution.py:489
